TPU v7x, 32 devices: a whole 2x2x4 slice. The times are simulated.
32 devices in a mesh: branch: 2 (over core), tm: 8 (over z, y), tok: 2 (over x).
Axes of the slice: x: 2, y: 2, z: 4, core: 2. Of those that a mesh axis runs over, the one named last changes fastest.
Arguments:
- states: float32 [8, 128, 3072], P('tm', 'tok'), may hold values from -6 to 6
- start_state: float32 [128, 3072], P('tok', 'branch'), may hold values from -12 to 12
- timesteps: int32 [8], P('tm'), may hold values from 0 to 49
- guidance_index: int32 [1], replicated, may hold values from 0 to 7
- modulation: float32 [2, 3, 3072], P('branch'), may hold values from -2.5 to 2.5
- w_query: bfloat16 [3072, 2048], P('branch', 'tok'), may hold values from -6 to 6, as said below
- w_key: bfloat16 [3072, 2048], P('branch', 'tok'), may hold values from -6 to 6, as said below
- w_value: bfloat16 [3072, 2048], P('branch', 'tok'), may hold values from -0.109375 to 0.109375
- w_out: bfloat16 [2048, 3072], P('tok', 'branch'), may hold values from -0.5 to 0.5
Outputs:
- updated_states: float32 [8, 128, 3072], P('tm', 'tok', 'branch')
Inputs may be any that keep to these rules, and one draw needn't show every extreme that they name: `w_query`: independent entries of mean zero. `w_key`: independent entries of mean zero.
All inputs are finite; a program needn't handle non-finite values.
Results may differ from a plain program's by a relative error of at most 0.0085.
The roundings to bfloat16 on the way count: a program that leaves them out, or rounds other values in their place, can miss the bound.
Values may be sent and summed in bfloat16 or wider, within the bound.
No kernel may reach another device: no remote copies, remote signals or barrier semaphores. Data moves between devices by JAX's collectives and lax.ppermute only.
A program may use at most 64 MiB of HBM per device.

v0:
```python
import math

import jax
import jax.numpy as jnp
from jax import lax
from jax.sharding import PartitionSpec as P

HD = 128
NSTEPS = 50


def swapped(x, axis, bit):
    return lax.ppermute(x, axis, [(i, i ^ 1 << bit) for i in range(lax.axis_size(axis))])


def carried_in(value, axis, join, neutral):
    count, mine = (lax.axis_size(axis), lax.axis_index(axis))
    pieces = lax.all_gather(value, axis)
    running = jnp.full_like(value, 0) + jnp.asarray(neutral, value.dtype)

    def hop(position, running):
        longer = join(running, pieces[position])
        return jnp.where(position < mine, longer, running)

    return lax.fori_loop(0, count - 1, hop, running)


def embed(step_ids, model_width):
    half_width = model_width // 2
    frequency = jnp.exp(-math.log(10000.0) * jnp.arange(half_width, dtype=jnp.float32) / half_width)
    phases = step_ids.astype(jnp.float32)[:, None] * frequency[None, :]
    return jnp.concatenate([jnp.sin(phases), jnp.cos(phases)], axis=1)


def add_sum(earlier, later):
    return earlier + later


def body(
    states, start_state, timesteps, guidance_index, modulation, w_query, w_key, w_value, w_out
):
    tm_count, tok_count, model_width = states.shape
    half_width = model_width // 2
    branch_index = lax.axis_index("branch")
    modulation_row = modulation[0]
    embedding = embed(timesteps, model_width)
    mean_value = jnp.mean(states, axis=2, keepdims=True)
    centered = states - mean_value
    variance = jnp.mean(centered * centered, axis=2, keepdims=True)
    normed = centered / jnp.sqrt(variance + 1e-06)
    modulated = (
        normed * (1.0 + modulation_row[1]) + modulation_row[0] + embedding[:, None, :]
    ).astype(jnp.bfloat16)
    gathered = lax.all_gather(modulated, "tok", axis=1, tiled=True)
    lat_count = gathered.shape[1]
    flat_rows = gathered.reshape(tm_count * lat_count, model_width)
    col_count = w_query.shape[1]
    own_columns = lax.dynamic_slice_in_dim(flat_rows, branch_index * half_width, half_width, 1)
    partner_cols = lax.dynamic_slice_in_dim(
        flat_rows, (1 - branch_index) * half_width, half_width, 1
    )
    received = swapped(partner_cols, "branch", 0)
    for_partner = jnp.concatenate(
        [
            jnp.dot(received, w_query, preferred_element_type=jnp.float32),
            jnp.dot(received, w_key, preferred_element_type=jnp.float32),
            jnp.dot(received, w_value, preferred_element_type=jnp.float32),
        ],
        axis=1,
    )
    returned = swapped(for_partner, "branch", 0)
    query_full = (
        jnp.dot(own_columns, w_query, preferred_element_type=jnp.float32) + returned[:, :col_count]
    )
    key_full = (
        jnp.dot(own_columns, w_key, preferred_element_type=jnp.float32)
        + returned[:, col_count : 2 * col_count]
    )
    value_full = (
        jnp.dot(own_columns, w_value, preferred_element_type=jnp.float32)
        + returned[:, 2 * col_count :]
    )
    head_count = col_count // HD
    query_heads = query_full.astype(jnp.bfloat16).reshape(tm_count, lat_count, head_count, HD)
    key_heads = key_full.astype(jnp.bfloat16).reshape(tm_count, lat_count, head_count, HD)
    value_heads = value_full.astype(jnp.bfloat16).reshape(tm_count, lat_count, head_count, HD)
    scores = jnp.einsum(
        "tqhc,tkhc->thqk", query_heads, key_heads, preferred_element_type=jnp.float32
    ) * (1.0 / math.sqrt(HD))
    softmax_w = jax.nn.softmax(scores, axis=-1).astype(jnp.bfloat16)
    attended = jnp.einsum(
        "thqk,tkhc->qthc", softmax_w, value_heads, preferred_element_type=jnp.float32
    ).astype(jnp.bfloat16)
    attended = attended.reshape(lat_count, tm_count, col_count)
    out_full = lax.all_gather(w_out, "branch", axis=1, tiled=True)
    summed = lax.psum_scatter(
        jnp.einsum("qtc,cd->qtd", attended, out_full, preferred_element_type=jnp.float32).astype(
            jnp.bfloat16
        ),
        "tok",
        scatter_dimension=0,
        tiled=True,
    ).astype(jnp.float32)
    drift = (1.0 + modulation_row[2]) * jnp.transpose(summed, (1, 0, 2))
    guide_scale = 1.5 + 0.5 * guidance_index[0].astype(jnp.float32)
    partner = swapped(drift, "branch", 0)
    conditional = jnp.where(branch_index == 0, drift, partner)
    unconditional = jnp.where(branch_index == 0, partner, drift)
    guided_full = unconditional + guide_scale * (conditional - unconditional)
    guided = lax.dynamic_slice_in_dim(guided_full, branch_index * half_width, half_width, 2)
    step_size = 2.0 * (1.0 + timesteps.astype(jnp.float32)) / NSTEPS
    increment = step_size[:, None, None] * guided
    local_prefix = jnp.cumsum(increment, axis=0)
    device_total = local_prefix[-1]
    earlier_sum = carried_in(device_total, "tm", add_sum, jnp.zeros_like(device_total))
    return start_state[None, :, :] + earlier_sum[None, :, :] + local_prefix


def solution(mesh):
    in_specs = (
        P("tm", "tok", None),
        P("tok", "branch"),
        P("tm"),
        P(),
        P("branch", None, None),
        P("branch", "tok"),
        P("branch", "tok"),
        P("branch", "tok"),
        P("tok", "branch"),
    )
    out_specs = P("tm", "tok", "branch")
    return jax.shard_map(body, mesh=mesh, in_specs=in_specs, out_specs=out_specs, check_vma=False)
```

profile of v0, /device:TPU:0, one launch (start us, length us, event | category | flops | bytes accessed | tf_op | source)
XLA Modules:
  0.0 156.1 jit_solution(3141103331908427693)
XLA Ops:
  6.5 0.7 all-gather.3.cloned.1.call-update
  8.4 1.3 reduce_sum.27
  9.6 1.4 multiply_reduce_fusion
  11.1 1.5 add_convert_fusion
  12.6 12.9 %all_gather.9 = bf16[1,128,3072]{2,1,0:T(8,128)(2,1)S(1)} all-gather(bf16[1,64,3072]{2,1,0:T(8,128)(2,1)S(1)} %add_convert_fusion), channel_id=1, replica_groups=mesh['branch'=2,'tm'=8,'tok'=2] {'tok'}, dimensions={1}, use_global_device_ids=true | all-gather | bytes 1179648 | tf_op jit(solution)/shard_map/all_gather | solution.py:54
  25.5 0.9 copy-done.4
  26.4 2.3 %collective-permute-done = bf16[128,1536]{1,0:T(8,128)(2,1)S(1)} collective-permute-done((bf16[128,1536]{1,0:T(8,128)(2,1)S(1)}, bf16[128,1536]{1,0:T(8,128)(2,1)S(1)}, u32[]{:S(2)}, u32[]{:S(2)}) %collective-permute-start) | collective-permute-done | bytes 393248 | tf_op jit(solution)/shard_map/ppermute | solution.py:13
  28.7 0.6 fusion.49
  30.5 1.3 pad_maximum_fusion
  32.0 3.6 %collective-permute-done.1 = f32[128,3072]{1,0:T(8,128)} collective-permute-done((f32[128,3072]{1,0:T(8,128)}, f32[128,3072]{1,0:T(8,128)}, u32[]{:S(2)}, u32[]{:S(2)}) %collective-permute-start.1) | collective-permute-done | bytes 1572896 | tf_op jit(solution)/shard_map/ppermute | solution.py:13
  35.6 1.7 %fusion.6 = bf16[128,1024]{1,0:T(8,128)(2,1)S(1)} fusion(f32[128,3072]{1,0:T(8,128)} %collective-permute-done.1, bf16[1536,1024]{1,0:T(8,128)(2,1)S(1)} %copy-done, bf16[1,128,3072]{2,1,0:T(8,128)(2,1)} %copy-done.4, s32[]{:T(128)S(6)} %select_n.41), kind=kOutput, calls=%fused_computation.17 | convolution fusion | flops 402915328 | bytes 4325380 | tf_op jit(solution)/shard_map/dot_general | solution.py:80
  37.3 0.8 copy.19
  38.2 2.8 %fusion.19 = bf16[16,8,8,128]{3,2,1,0:T(8,128)(2,1)S(1)} fusion(f32[128,3072]{1,0:T(8,128)} %collective-permute-done.1, bf16[1536,1024]{1,0:T(8,128)(2,1)} %param.16, bf16[1,128,3072]{2,1,0:T(8,128)(2,1)} %copy-done.4, s32[]{:T(128)S(6)} %select_n.41), kind=kOutput, calls=%fused_computation.26 | convolution fusion | flops 402915328 | bytes 4325380 | tf_op jit(solution)/shard_map/dot_general | solution.py:73
  41.5 2.3 %fusion.22 = bf16[16,8,8,128]{3,2,1,0:T(8,128)(2,1)} fusion(f32[128,3072]{1,0:T(8,128)} %collective-permute-done.1, bf16[1536,1024]{1,0:T(8,128)(2,1)S(1)} %copy-done.3, bf16[1,128,3072]{2,1,0:T(8,128)(2,1)S(1)} %copy-done.5, s32[]{:T(128)S(6)} %select_n.41), kind=kOutput, calls=%fused_computation.27 | convolution fusion | flops 402915328 | bytes 4325380 | tf_op jit(solution)/shard_map/dot_general | solution.py:76
  43.8 1.3 fusion.44
  45.1 2.1 %convolution_multiply_fusion = f32[8,128,128]{1,2,0:T(8,128)} fusion(bf16[16,8,8,128]{3,2,1,0:T(8,128)(2,1)} %fusion.22, bf16[16,8,8,128]{3,2,1,0:T(8,128)(2,1)S(1)} %fusion.19), kind=kOutput, calls=%fused_computation.7 | convolution fusion | flops 33685504 | bytes 1048576 | tf_op jit(solution)/shard_map/tqhc,tkhc->thqk/dot_general | solution.py:87
  47.2 1.6 %convolution_convert_fusion.1 = bf16[8,128,128]{2,1,0:T(8,128)(2,1)S(1)} fusion(bf16[128,8,128]{0,2,1:T(8,128)(2,1)} %bitcast.75, f32[8,128]{1,0:T(8,128)S(1)} %fusion.44, f32[8,128,128]{1,2,0:T(8,128)} %convolution_multiply_fusion), kind=kOutput, calls=%fused_computation.8 | convolution fusion | flops 34079872 | bytes 1052672 | tf_op jit(solution)/shard_map/thqk,tkhc->qthc/dot_general | solution.py:91
  48.8 4.7 %fusion.1 = bf16[128,1,3072]{2,0,1:T(8,128)(2,1)} fusion(bf16[128,1024]{0,1:T(8,128)(2,1)S(1)} %bitcast.74, bf16[1024,3072]{1,0:T(8,128)(2,1)} %all-gather.3.cloned.1.call-done), kind=kOutput, calls=%fused_computation.3 | convolution fusion | flops 805699584 | bytes 7340032 | tf_op jit(solution)/shard_map/qtc,cd->qtd/dot_general | solution.py:97
  53.5 18.8 %reduce-scatter.2.cloned.1.call-done = bf16[64,1,3072]{2,0,1:T(8,128)(2,1)} async-done(((bf16[128,1,3072]{2,0,1:T(8,128)(2,1)}), bf16[64,1,3072]{2,0,1:T(8,128)(2,1)}) %reduce-scatter.2.cloned.1.call-update) | async-done | bytes 393232 | tf_op jit(solution)/shard_map/reduce_scatter | solution.py:96
  72.3 1.9 %convert_multiply_fusion = f32[1,64,3072]{2,1,0:T(8,128)} fusion(bf16[64,1,3072]{2,0,1:T(8,128)(2,1)} %reduce-scatter.2.cloned.1.call-done, f32[3072]{0:T(1024)S(1)} %bitcast.76), kind=kLoop, calls=%fused_computation.9 | loop fusion | flops 393216 | bytes 1191936 | tf_op jit(solution)/shard_map/mul | solution.py:104
  74.9 2.0 %collective-permute-done.2 = f32[1,64,3072]{2,1,0:T(8,128)} collective-permute-done((f32[1,64,3072]{2,1,0:T(8,128)}, f32[1,64,3072]{2,1,0:T(8,128)}, u32[]{:S(2)}, u32[]{:S(2)}) %collective-permute-start.2) | collective-permute-done | bytes 786464 | tf_op jit(solution)/shard_map/ppermute | solution.py:13
  76.9 1.9 %add_multiply_fusion = f32[1,64,1536]{2,1,0:T(8,128)} fusion(f32[1,64,3072]{2,1,0:T(8,128)} %convert_multiply_fusion, s32[]{:T(128)S(6)} %select_n.41, f32[1,64,3072]{2,1,0:T(8,128)} %collective-permute-done.2, f32[]{:T(128)} %bitcast.14, f32[]{:T(128)} %bitcast, pred[]{:T(512)S(6)} %eq.4), kind=kLoop, calls=%fused_computation.28 | loop fusion | flops 589824 | bytes 1179661 | tf_op jit(solution)/shard_map/mul | solution.py:112
  78.9 60.6 %all-gather.5.cloned.1.call-done = f32[8,64,1536]{2,1,0:T(8,128)} async-done(((f32[1,64,1536]{2,1,0:T(8,128)}), f32[8,64,1536]{2,1,0:T(8,128)}) %all-gather.5.cloned.1.call-update) | async-done | bytes 3145744 | tf_op jit(solution)/shard_map/all_gather | solution.py:18
  139.5 8.1 %while.14 = (s32[]{:T(128)}, f32[64,1536]{1,0:T(8,128)S(1)}, s32[]{:T(128)}, f32[8,64,1536]{2,1,0:T(8,128)}, s32[]{:T(128)}, /*index=5*/s32[]{:T(128)}) while((s32[]{:T(128)}, f32[64,1536]{1,0:T(8,128)S(1)}, s32[]{:T(128)}, f32[8,64,1536]{2,1,0:T(8,128)}, s32[]{:T(128)}, /*index=5*/s32[]{:T(128)}) %tuple.35), condition=%wide.region_6.7_spmd.clone, body=%wide.region_5.6_spmd.clone.sunk | while | flops 294916 | bytes 1179741 | solution.py:25
  139.5 1.1 add_select_fusion.2
  140.6 1.1 add_select_fusion.2
  141.8 1.1 add_select_fusion.2
  143.0 1.1 add_select_fusion.2
  144.1 1.1 add_select_fusion.2
  145.3 1.1 add_select_fusion.2
  146.5 1.1 add_select_fusion.2
  147.6 1.9 %bitcast_add_fusion = f32[1,64,1536]{2,1,0:T(8,128)} fusion(f32[1,64,1536]{2,1,0:T(8,128)} %add_multiply_fusion, f32[64,1536]{1,0:T(8,128)} %param.12, f32[64,1536]{1,0:T(8,128)S(1)} %get-tuple-element.84), kind=kLoop, calls=%fused_computation.19 | loop fusion | flops 196608 | bytes 1572864 | tf_op jit(solution)/shard_map/add | solution.py:116
  (31 shorter events, 2.3 us)
Async XLA Ops:
  6.5 23.4 %copy-start = (bf16[1536,1024]{1,0:T(8,128)(2,1)S(1)}, bf16[1536,1024]{1,0:T(8,128)(2,1)}, u32[]{:S(2)}) copy-start(bf16[1536,1024]{1,0:T(8,128)(2,1)} %param.18) | copy-start | bytes 9437188
  6.5 1.8 %copy-start.6 = (f32[1,3,3072]{2,0,1:T(1,128)S(1)}, f32[1,3,3072]{2,0,1:T(1,128)}, u32[]{:S(2)}) copy-start(f32[1,3,3072]{2,0,1:T(1,128)} %param.15) | copy-start | bytes 110596
  6.5 42.3 %all-gather.3.cloned.1.call-start = ((), (), s32[]{:S(2)}) async-start(), calls=%async_computation.1 | async-start | bytes 9437184 | tf_op jit(solution)/shard_map/all_gather | solution.py:95
  7.3 65.1 %reduce-scatter.2.cloned.1.call-start = ((), (), s32[]{:S(2)}) async-start(), calls=%async_computation.2 | async-start | bytes 1179648 | tf_op jit(solution)/shard_map/reduce_scatter | solution.py:96
  11.0 17.7 %copy-start.1 = (bf16[1536,1024]{1,0:T(8,128)(2,1)S(1)}, bf16[1536,1024]{1,0:T(8,128)(2,1)}, u32[]{:S(2)}) copy-start(bf16[1536,1024]{1,0:T(8,128)(2,1)} %param.16) | copy-start | bytes 9437188
  12.6 16.7 %copy-start.2 = (bf16[1536,1024]{1,0:T(8,128)(2,1)S(1)}, bf16[1536,1024]{1,0:T(8,128)(2,1)}, u32[]{:S(2)}) copy-start(bf16[1536,1024]{1,0:T(8,128)(2,1)} %param.17) | copy-start | bytes 9437188
  25.5 0.9 copy-start.4
  26.4 2.4 %collective-permute-start = (bf16[128,1536]{1,0:T(8,128)(2,1)S(1)}, bf16[128,1536]{1,0:T(8,128)(2,1)S(1)}, u32[]{:S(2)}, u32[]{:S(2)}) collective-permute-start(bf16[128,1536]{1,0:T(8,128)(2,1)S(1)} %dynamic-slice_bitcast_fusion), channel_id=1, source_target_pairs={{0,16},{16,0},{1,17},{17,1},{2,18},{18,2},{3,19},{19,3},{4,20},{20... | collective-permute-start | bytes 1179656 | tf_op jit(solution)/shard_map/ppermute | solution.py:13
  31.8 3.8 %collective-permute-start.1 = (f32[128,3072]{1,0:T(8,128)}, f32[128,3072]{1,0:T(8,128)}, u32[]{:S(2)}, u32[]{:S(2)}) collective-permute-start(f32[128,3072]{1,0:T(8,128)} %pad_maximum_fusion), channel_id=1, source_target_pairs={{0,16},{16,0},{1,17},{17,1},{2,18},{18,2},{3,19},{19,3},{4,20},{20... | collective-permute-start | bytes 4718600 | tf_op jit(solution)/shard_map/ppermute | solution.py:13
  38.2 3.1 %copy-start.3 = (bf16[1536,1024]{1,0:T(8,128)(2,1)S(1)}, bf16[1536,1024]{1,0:T(8,128)(2,1)}, u32[]{:S(2)}) copy-start(bf16[1536,1024]{1,0:T(8,128)(2,1)} %param.17) | copy-start | bytes 9437188
  38.2 3.3 %copy-start.5 = (bf16[1,128,3072]{2,1,0:T(8,128)(2,1)S(1)}, bf16[1,128,3072]{2,1,0:T(8,128)(2,1)}, u32[]{:S(2)}) copy-start(bf16[1,128,3072]{2,1,0:T(8,128)(2,1)} %copy-done.4) | copy-start | bytes 2359300
  53.5 86.0 %all-gather.5.cloned.1.call-start = ((), (), s32[]{:S(2)}) async-start(), calls=%async_computation.3 | async-start | bytes 3538944 | tf_op jit(solution)/shard_map/all_gather | solution.py:18
  74.3 2.6 %collective-permute-start.2 = (f32[1,64,3072]{2,1,0:T(8,128)}, f32[1,64,3072]{2,1,0:T(8,128)}, u32[]{:S(2)}, u32[]{:S(2)}) collective-permute-start(f32[1,64,3072]{2,1,0:T(8,128)} %convert_multiply_fusion), channel_id=1, source_target_pairs={{0,16},{16,0},{1,17},{17,1},{2,18},{18,2},{3,19},{19,3},{4,20},{20... | collective-permute-start | bytes 2359304 | tf_op jit(solution)/shard_map/ppermute | solution.py:13
Sparse Core Ops, SparseCore 0:
  8.9 20.0 all-gather.2
  53.6 18.6 reduce-scatter.1
  79.0 60.4 all-gather.4
where the time goes:
time: 157 us; the launch traced here: 156 us
  waiting for transfers between devices  88 us (56%)
  other arithmetic  19.5 us (12%)
  matrix products  18.3 us (12%)
  between operations  14.7 us (9%)
  blocking collectives  12.9 us (8%)
  local copies, waits for them, and re-layouts  2.21 us (1%)
    all_gather x1, waiting for transfers between devices, carried_in(): pieces = lax.all_gather(value, axis)  60.6 us
    reduce_scatter x1, waiting for transfers between devices, body(): lax.psum_scatter(jnp.einsum('qtc,cd->qtd', attended, out_full, preferred_...  18.8 us
    all_gather x1, blocking collectives, body(): gathered = lax.all_gather(modulated, 'tok', axis=1, tiled=True)  12.9 us
    select_n x7, other arithmetic, hop(): return jnp.where(position < mine, longer, running)  7.95 us
    ppermute x3, waiting for transfers between devices, swapped(): lax.ppermute(x, axis, [(i, i ^ 1 << bit) for i in range(lax.axis_size(axi...  7.86 us
    dot_general x1, matrix products, body(): jnp.einsum('qtc,cd->qtd', attended, out_full, preferred_element_type=jnp....  4.67 us
  transfers between devices with their start and end apart: 6, of which 5 were waited for; matrix products, arithmetic and copies ran while one was open for 13% of the time, Pallas kernels for 0%

commit v1 on v0

v1 whole, which is shorter than its diff:
```python
import functools
import math

import jax
import jax.numpy as jnp
from jax import lax
from jax.experimental import pallas as pl
from jax.experimental.pallas import tpu as pltpu
from jax.sharding import PartitionSpec as P

HD = 128
NSTEPS = 50
F32 = jnp.float32
BF16 = jnp.bfloat16
VMEM = pl.BlockSpec(memory_space=pltpu.VMEM)
SMEM = pl.BlockSpec(memory_space=pltpu.SMEM)


def xor_permute(x, axes, mask):
    return lax.ppermute(x, axes, [(i, i ^ mask) for i in range(lax.axis_size(axes))])


def dot(a, b):
    return jnp.dot(a, b, preferred_element_type=F32)


def embed_half(step_id, half_width, branch_index):
    frequency = jnp.exp(-math.log(10000.0) * jnp.arange(half_width, dtype=F32) / half_width)
    phases = step_id.astype(F32) * frequency
    return jnp.where(branch_index == 0, jnp.sin(phases), jnp.cos(phases))[None, :]


def norm_kernel(branch_ref, states_ref, out_ref):
    half_width = out_ref.shape[1]
    tokens = states_ref[...]
    width = tokens.shape[1]
    mean = jnp.sum(tokens, axis=1, keepdims=True) * (1.0 / width)
    centered = tokens - mean
    variance = jnp.sum(centered * centered, axis=1, keepdims=True) * (1.0 / width)
    deviation = jnp.sqrt(variance + 1e-06)
    start = pl.multiple_of(branch_ref[0] * half_width, HD)
    out_ref[...] = (states_ref[:, pl.ds(start, half_width)] - mean) / deviation


def normed_half(states, branch_index):
    rows, width = states.shape
    return pl.pallas_call(
        norm_kernel,
        out_shape=jax.ShapeDtypeStruct((rows, width // 2), F32),
        in_specs=[SMEM, VMEM],
        out_specs=VMEM,
    )(branch_index[None], states)


def attention_kernel(blocks, *refs):
    out_ref = refs[-1]
    rows = refs[0].shape[0]
    columns = refs[0].shape[1]

    def part(which, head):
        sl = slice(head * HD, (head + 1) * HD)
        pieces = []
        for block in range(blocks):
            mine, other = refs[(block * 3 + which) * 2], refs[(block * 3 + which) * 2 + 1]
            pieces.append((mine[0:rows // 2, sl] + other[:, sl]).astype(BF16))
        return jnp.concatenate(pieces, axis=0)

    for head in range(columns // HD):
        query, key, value = part(0, head), part(1, head), part(2, head)
        scores = lax.dot_general(query, key, (((1,), (1,)), ((), ())), preferred_element_type=F32)
        scores = scores * (1.0 / math.sqrt(HD))
        scores = jnp.exp(scores - jnp.max(scores, axis=1, keepdims=True))
        probs = (scores / jnp.sum(scores, axis=1, keepdims=True)).astype(BF16)
        out_ref[:, head * HD:(head + 1) * HD] = dot(probs, value).astype(BF16)


def attention(blocks):
    flat = [array for block in blocks for pair in block for array in pair]
    rows, columns = blocks[0][0][1].shape
    return pl.pallas_call(
        functools.partial(attention_kernel, len(blocks)),
        out_shape=jax.ShapeDtypeStruct((rows * len(blocks), columns), BF16),
        in_specs=[VMEM] * len(flat),
        out_specs=VMEM,
        compiler_params=pltpu.CompilerParams(vmem_limit_bytes=32 << 20),
    )(*flat)


def project_kernel(chunk, ints_ref, floats_ref, mine_ref, other_ref, w_ref, gates_ref, out_ref):
    lat = mine_ref.shape[0]
    columns = w_ref.shape[1]
    both = jnp.concatenate([mine_ref[...], other_ref[...]], axis=0)
    first = ints_ref[0] == 0
    scale, step = floats_ref[0], floats_ref[1]
    for start in range(0, columns, chunk):
        sl = slice(start, start + chunk)
        partial = dot(both, w_ref[:, sl]).astype(BF16).astype(F32)
        mine = (1.0 + gates_ref[0:1, sl]) * partial[:lat]
        other = (1.0 + gates_ref[1:2, sl]) * partial[lat:]
        conditional = jnp.where(first, mine, other)
        unconditional = jnp.where(first, other, mine)
        out_ref[:, sl] = step * (unconditional + scale * (conditional - unconditional))


def project(branch_index, scale, step, mine, other, w_out, gates):
    lat = mine.shape[0]
    columns = w_out.shape[1]
    chunk = 512 if columns % 512 == 0 else HD
    return pl.pallas_call(
        functools.partial(project_kernel, chunk),
        out_shape=jax.ShapeDtypeStruct((lat, columns), F32),
        in_specs=[SMEM, SMEM, VMEM, VMEM, VMEM, VMEM],
        out_specs=VMEM,
        compiler_params=pltpu.CompilerParams(vmem_limit_bytes=32 << 20),
    )(branch_index[None], jnp.stack([scale, step]), mine, other, w_out, gates)


def scan_general(parts):
    total = parts[0]
    for mask in range(1, len(parts)):
        total = total + xor_permute(parts[mask].astype(BF16), "tok", mask).astype(F32)
    position = lax.axis_index("tm")
    result, group = total, total
    mask = 1
    while mask < lax.axis_size("tm"):
        received = xor_permute(group.astype(BF16), "tm", mask).astype(F32)
        result = result + jnp.where(position & mask != 0, received, 0.0)
        group = group + received
        mask *= 2
    return result


def scan_planes(parts):
    axes = ("tm", "tok")
    position = lax.axis_index("tm")
    odd = position & 1 == 1
    rows = parts[0].shape[0] // 2

    def near(x):
        return jnp.where(odd, x[rows:], x[:rows])

    def far(x):
        return jnp.where(odd, x[:rows], x[rows:])

    diagonal = xor_permute(far(parts[1]).astype(BF16), axes, 3)
    across = xor_permute(near(parts[1]).astype(BF16), axes, 1)
    beside = xor_permute(far(parts[0]).astype(BF16), axes, 2)
    own_time = near(parts[0]) + across.astype(F32)
    pair_time = beside.astype(F32) + diagonal.astype(F32)
    group = own_time + pair_time
    earlier = jnp.zeros_like(group)
    mask = 2
    while mask < lax.axis_size("tm"):
        received = xor_permute(group.astype(BF16), "tm", mask).astype(F32)
        earlier = earlier + jnp.where(position & mask != 0, received, 0.0)
        group = group + received
        mask *= 2
    own = earlier + own_time + jnp.where(odd, pair_time, 0.0)
    for_pair = earlier + pair_time + jnp.where(odd, 0.0, own_time)
    returned = xor_permute(for_pair.astype(BF16), "tm", 1).astype(F32)
    return jnp.concatenate([jnp.where(odd, returned, own), jnp.where(odd, own, returned)], axis=0)


def body(
    states, start_state, timesteps, guidance_index, modulation, w_query, w_key, w_value, w_out
):
    tok_count = lax.axis_size("tok")
    branch_index = lax.axis_index("branch")
    rows, model_width = states.shape[1:]
    half_width = model_width // 2
    own_modulation = modulation[0]
    half = functools.partial(
        lax.dynamic_slice_in_dim, start_index=branch_index * half_width, slice_size=half_width, axis=1
    )
    other_modulation = xor_permute(own_modulation, "branch", 1)
    mods = [half(own_modulation), half(other_modulation)]
    embedding = embed_half(timesteps[0], half_width, branch_index)

    normed = normed_half(states[0], branch_index)
    tokens = [normed] + [xor_permute(normed, "tok", mask) for mask in range(1, tok_count)]

    blocks = []
    for block in tokens:
        modulated = jnp.concatenate(
            [block * (1.0 + mod[1:2]) + mod[0:1] + embedding for mod in mods], axis=0
        ).astype(BF16)
        projected = [dot(modulated, w) for w in (w_query, w_key, w_value)]
        blocks.append([(p, xor_permute(p[rows:], "branch", 1)) for p in projected])
    attended = attention(blocks)
    attended_other = xor_permute(attended, "branch", 1)

    guide_scale = 1.5 + 0.5 * guidance_index[0].astype(F32)
    step_size = 2.0 * (1.0 + timesteps[0].astype(F32)) / NSTEPS
    gates = jnp.concatenate([mods[0][2:3], mods[1][2:3]], axis=0)
    increments = project(
        branch_index, guide_scale, step_size, attended, attended_other, w_out, gates
    )
    parts = [increments[m * rows:(m + 1) * rows] for m in range(tok_count)]
    pairs = tok_count == 2 and lax.axis_size("tm") % 2 == 0 and rows % 32 == 0
    scan = scan_planes if pairs else scan_general
    return (start_state + scan(parts))[None]


def solution(mesh):
    in_specs = (
        P("tm", "tok", None),
        P("tok", "branch"),
        P("tm"),
        P(),
        P("branch", None, None),
        P("branch", "tok"),
        P("branch", "tok"),
        P("branch", "tok"),
        P("tok", "branch"),
    )
    out_specs = P("tm", "tok", "branch")
    return jax.shard_map(body, mesh=mesh, in_specs=in_specs, out_specs=out_specs, check_vma=False)
```

time: 157 us -> 79 us (0.50)
  waiting for transfers between devices: 88 us -> 20.5 us
  local copies, waits for them, and re-layouts: 2.21 us -> 19.9 us
  starting transfers between devices: 0.29 us -> 14.1 us
  between operations: 14.7 us -> 1.57 us
  matrix products: 18.3 us -> 5.34 us
  blocking collectives: 12.9 us -> 0 us
  other arithmetic: 19.5 us -> 8.29 us
  Pallas kernels: 0 us -> 8.24 us
    all_gather x2 -> x0, waiting for transfers between devices: 60.6 us -> none  [the longest x1 60.6 us: carried_in(): pieces = lax.all_gather(value, axis)]
    reduce_scatter x1 -> x0, waiting for transfers between devices: 18.8 us -> none  [body(): lax.psum_scatter(jnp.einsum('qtc,cd->qtd', attended, out_full, preferred_...]
    unnamed x14 -> x45, local copies, waits for them, and re-layouts: 1.34 us -> 16.1 us
    ppermute x3 -> x15, starting transfers between devices: 0.21 us -> 14.1 us  [xor_permute(): lax.ppermute(x, axes, [(i, i ^ mask) for i in range(lax.axis_size(axes))])]
    all_gather x1 -> x0, blocking collectives: 12.9 us -> none  [body(): gathered = lax.all_gather(modulated, 'tok', axis=1, tiled=True)]
    ppermute x3 -> x15, waiting for transfers between devices: 7.86 us -> 20.5 us  [xor_permute(): lax.ppermute(x, axes, [(i, i ^ mask) for i in range(lax.axis_size(axes))])]
    dot_general x9 -> x6, matrix products: 17 us -> 5.34 us  [dot(): return jnp.dot(a, b, preferred_element_type=F32)]
    pallas_call x0 -> x3, Pallas kernels: none -> 8.24 us  [the longest x1 3.88 us: attention(): pl.pallas_call(functools.partial(attention_kernel, len(blocks)), out_shap...]
  transfers between devices with their start and end apart: 6 -> 15, of which waited for: 5 -> 9; matrix products, arithmetic and copies ran while one was open for 13% -> 11% of each run, Pallas kernels for 0% -> 0%
where the time goes in v1:
time: 79 us; the launch traced here: 77.9 us
  waiting for transfers between devices  20.5 us (26%)
  local copies, waits for them, and re-layouts  19.9 us (25%)
  starting transfers between devices  14.1 us (18%)
  other arithmetic  8.29 us (10%)
  Pallas kernels  8.24 us (10%)
  matrix products  5.34 us (7%)
  between operations  1.57 us (2%)
    ppermute x15, waiting for transfers between devices, xor_permute(): lax.ppermute(x, axes, [(i, i ^ mask) for i in range(lax.axis_size(axes))])  20.5 us
    unnamed x45, local copies, waits for them, and re-layouts  16.1 us
    ppermute x15, starting transfers between devices, xor_permute(): lax.ppermute(x, axes, [(i, i ^ mask) for i in range(lax.axis_size(axes))])  14.1 us
    dot_general x6, matrix products, dot(): return jnp.dot(a, b, preferred_element_type=F32)  5.34 us
    pallas_call x1, Pallas kernels, attention(): pl.pallas_call(functools.partial(attention_kernel, len(blocks)), out_shap...  3.88 us
    slice x6, local copies, waits for them, and re-layouts, body(): blocks.append([(p, xor_permute(p[rows:], 'branch', 1)) for p in projected])  3.75 us
    pallas_call x1, Pallas kernels, normed_half(): pl.pallas_call(norm_kernel, out_shape=jax.ShapeDtypeStruct((rows, width /...  2.33 us
    add x2, other arithmetic, body(): 1.0 + mod[1:2]  2.29 us
  transfers between devices with their start and end apart: 15, of which 9 were waited for; matrix products, arithmetic and copies ran while one was open for 11% of the time, Pallas kernels for 0%

profile of v1, /device:TPU:0, one launch (start us, length us, event | category | flops | bytes accessed | tf_op | source)
XLA Modules:
  0.0 77.9 jit_solution(14900032233988947622)
XLA Ops:
  0.0 2.3 %shard_map.91 = f32[64,1536]{1,0:T(8,128)} custom-call(s32[1]{0:T(128)} %bitcast.branch_ref.ints_ref, f32[64,3072]{1,0:T(8,128)} %bitcast.17), custom_call_target="tpu_custom_call" | custom-call | tf_op jit(solution)/shard_map/pallas_call | solution.py:47
  2.3 2.9 %collective-permute-start.4 = (f32[64,1536]{1,0:T(8,128)}, f32[64,1536]{1,0:T(8,128)S(1)}, u32[]{:S(2)}, u32[]{:S(2)}) collective-permute-start(f32[64,1536]{1,0:T(8,128)} %shard_map.91), channel_id=1, source_target_pairs={{0,1},{1,0},{2,3},{3,2},{4,5},{5,4},{6,7},{7,6},{8,9},{9,8},{10,11... | collective-permute-start | bytes 1179656 | tf_op jit(solution)/shard_map/ppermute | solution.py:20
  5.3 1.4 %copy.12 = f32[1,3,3072]{2,1,0:T(4,128)} copy(f32[1,3,3072]{2,0,1:T(1,128)} %param.13) | data formatting | bytes 73728
  8.2 1.5 %fusion.11 = (f32[1536]{0:T(1024)S(1)}, f32[1536]{0:T(1024)S(1)}, f32[1,1536]{1,0:T(1,128)}) fusion(f32[3,3072]{1,0:T(4,128)} %collective-permute-done, s32[]{:T(128)S(6)} %add.143, s32[]{:T(128)S(6)} %select_n.70, s32[]{:T(128)S(6)} %add.145), kind=kLoop, calls=%fused_computation.35 | loop fusion | flops 1536 | bytes 36876 | tf_op jit(solution)/shard_map/add | solution.py:185
  9.8 4.8 %collective-permute-done.4 = f32[64,1536]{1,0:T(8,128)S(1)} collective-permute-done((f32[64,1536]{1,0:T(8,128)}, f32[64,1536]{1,0:T(8,128)S(1)}, u32[]{:S(2)}, u32[]{:S(2)}) %collective-permute-start.4) | collective-permute-done | bytes 393248 | tf_op jit(solution)/shard_map/ppermute | solution.py:20
  14.6 1.2 %add_convert_fusion.3 = (bf16[64,1536]{1,0:T(8,128)(2,1)S(1)}, bf16[64,1536]{1,0:T(8,128)(2,1)S(1)}, bf16[64,1536]{1,0:T(8,128)(2,1)S(1)}, bf16[64,1536]{1,0:T(8,128)(2,1)S(1)}) fusion(f32[64,1536]{1,0:T(8,128)} %shard_map.91, f32[1536]{0:T(1024)S(1)} %cosine_select_fusion, f32[1536]{0:T(1024)S(1)} %get-tuple-element.8, f32[1536]{0:T(1024)S(1)} %get-tuple-element.7, ...), kind=kLoop, calls=%fused_computation.7 | loop fusion | flops 1572864 | bytes 1603584 | tf_op jit(solution)/shard_map/convert.2
  15.8 2.5 %fusion.5.refs_8_ = f32[128,1024]{1,0:T(8,128)S(1)} fusion(bf16[1536,1024]{1,0:T(8,128)(2,1)} %param.15, bf16[64,1536]{1,0:T(8,128)(2,1)S(1)} %get-tuple-element.21, bf16[64,1536]{1,0:T(8,128)(2,1)S(1)} %get-tuple-element.22), kind=kOutput, calls=%fused_computation.23 | convolution fusion | flops 403439616 | bytes 4063232 | tf_op jit(solution)/shard_map/dot_general | solution.py:24
  19.5 1.1 %copy-done.18 = bf16[1536,1024]{1,0:T(8,128)(2,1)S(1)} copy-done((bf16[1536,1024]{1,0:T(8,128)(2,1)S(1)}, bf16[1536,1024]{1,0:T(8,128)(2,1)}, u32[]{:S(2)}) %copy-start.18) | copy-done | bytes 3145752
  21.2 1.6 %copy-done.19 = bf16[1536,1024]{1,0:T(8,128)(2,1)S(1)} copy-done((bf16[1536,1024]{1,0:T(8,128)(2,1)S(1)}, bf16[1536,1024]{1,0:T(8,128)(2,1)}, u32[]{:S(2)}) %copy-start.19) | copy-done | bytes 3145752
  31.4 1.0 %copy-done.2 = f32[128,1024]{1,0:T(8,128)S(1)} copy-done((f32[128,1024]{1,0:T(8,128)S(1)}, f32[128,1024]{1,0:T(8,128)}, u32[]{:S(2)}) %copy-start.2) | copy-done | bytes 524312
  32.4 1.0 %copy-done.4 = f32[128,1024]{1,0:T(8,128)S(1)} copy-done((f32[128,1024]{1,0:T(8,128)S(1)}, f32[128,1024]{1,0:T(8,128)}, u32[]{:S(2)}) %copy-start.4) | copy-done | bytes 524312
  33.5 1.0 %copy-done.6 = f32[128,1024]{1,0:T(8,128)S(1)} copy-done((f32[128,1024]{1,0:T(8,128)S(1)}, f32[128,1024]{1,0:T(8,128)}, u32[]{:S(2)}) %copy-start.6) | copy-done | bytes 524312
  34.5 1.0 %copy-done.8 = f32[128,1024]{1,0:T(8,128)S(1)} copy-done((f32[128,1024]{1,0:T(8,128)S(1)}, f32[128,1024]{1,0:T(8,128)}, u32[]{:S(2)}) %copy-start.8) | copy-done | bytes 524312
  35.6 1.0 %copy-done.10 = f32[128,1024]{1,0:T(8,128)S(1)} copy-done((f32[128,1024]{1,0:T(8,128)S(1)}, f32[128,1024]{1,0:T(8,128)}, u32[]{:S(2)}) %copy-start.10) | copy-done | bytes 524312
  36.6 1.0 %copy-done.12 = f32[128,1024]{1,0:T(8,128)S(1)} copy-done((f32[128,1024]{1,0:T(8,128)S(1)}, f32[128,1024]{1,0:T(8,128)}, u32[]{:S(2)}) %copy-start.12) | copy-done | bytes 524312
  39.5 3.9 %shard_map.92.mine_ref = bf16[128,1024]{1,0:T(8,128)(2,1)S(1)} custom-call(f32[128,1024]{1,0:T(8,128)S(1)} %copy-done.12, f32[64,1024]{1,0:T(8,128)} %collective-permute-done.1.refs_1_, f32[128,1024]{1,0:T(8,128)S(1)} %copy-done.8, f32[64,1024]{1,0:T(8,128)} %collective-permute-done.2.refs_3_, f32[128,1024]{1,0:T(8,128)S(1)} %copy-done.6, ...), custom_call_target="tpu_custom_call" | custom-call | tf_op jit(solution)/shard_map/pallas_call | solution.py:80
  43.7 1.4 %collective-permute-done.8.other_ref = bf16[128,1024]{1,0:T(8,128)(2,1)} collective-permute-done((bf16[128,1024]{1,0:T(8,128)(2,1)S(1)}, bf16[128,1024]{1,0:T(8,128)(2,1)}, u32[]{:S(2)}, u32[]{:S(2)}) %collective-permute-start.8) | collective-permute-done | bytes 262176 | tf_op jit(solution)/shard_map/ppermute | solution.py:20
  45.2 1.9 %copy-done.13 = bf16[1024,1536]{1,0:T(8,128)(2,1)S(1)} copy-done((bf16[1024,1536]{1,0:T(8,128)(2,1)S(1)}, bf16[1024,1536]{1,0:T(8,128)(2,1)}, u32[]{:S(2)}) %copy-start.13) | copy-done | bytes 3145752
  47.0 2.0 %shard_map.93 = f32[128,1536]{1,0:T(8,128)S(1)} custom-call(s32[1]{0:T(128)} %bitcast.branch_ref.ints_ref, f32[2]{0:T(128)S(1)} %pad_maximum_fusion.9.floats_ref, bf16[128,1024]{1,0:T(8,128)(2,1)S(1)} %shard_map.92.mine_ref, bf16[128,1024]{1,0:T(8,128)(2,1)} %collective-permute-done.8.other_ref, bf16[1024,1536]{1,0:T(8,128)(2,1)S(1)} %copy-done.13, ...), custom_call_target="tpu_custom_call" | custom-call | tf_op jit(solution)/shard_map/pallas_call | solution.py:109
  49.1 1.8 %collective-permute-start.10 = (bf16[32,1536]{1,0:T(8,128)(2,1)S(1)}, bf16[32,1536]{1,0:T(8,128)(2,1)S(1)}, u32[]{:S(2)}, u32[]{:S(2)}) collective-permute-start(bf16[32,1536]{1,0:T(8,128)(2,1)S(1)} %get-tuple-element.15), channel_id=1, source_target_pairs={{0,2},{1,3},{2,0},{3,1},{4,6},{5,7},{6,4},{7,5},{8,10},{9,11},{10,... | collective-permute-start | bytes 294920 | tf_op jit(solution)/shard_map/ppermute | solution.py:20
  51.0 1.4 %collective-permute-start.11 = (bf16[32,1536]{1,0:T(8,128)(2,1)S(1)}, bf16[32,1536]{1,0:T(8,128)(2,1)S(1)}, u32[]{:S(2)}, u32[]{:S(2)}) collective-permute-start(bf16[32,1536]{1,0:T(8,128)(2,1)S(1)} %get-tuple-element.14), channel_id=1, source_target_pairs={{0,3},{1,2},{2,1},{3,0},{4,7},{5,6},{6,5},{7,4},{8,11},{9,10},{10,... | collective-permute-start | bytes 294920 | tf_op jit(solution)/shard_map/ppermute | solution.py:20
  52.7 2.8 %collective-permute-done.10 = bf16[32,1536]{1,0:T(8,128)(2,1)S(1)} collective-permute-done((bf16[32,1536]{1,0:T(8,128)(2,1)S(1)}, bf16[32,1536]{1,0:T(8,128)(2,1)S(1)}, u32[]{:S(2)}, u32[]{:S(2)}) %collective-permute-start.10) | collective-permute-done | bytes 98336 | tf_op jit(solution)/shard_map/ppermute | solution.py:20
  55.5 2.0 %collective-permute-done.11 = bf16[32,1536]{1,0:T(8,128)(2,1)S(1)} collective-permute-done((bf16[32,1536]{1,0:T(8,128)(2,1)S(1)}, bf16[32,1536]{1,0:T(8,128)(2,1)S(1)}, u32[]{:S(2)}, u32[]{:S(2)}) %collective-permute-start.11) | collective-permute-done | bytes 98336 | tf_op jit(solution)/shard_map/ppermute | solution.py:20
  57.5 1.8 %collective-permute-start.12 = (bf16[32,1536]{1,0:T(8,128)(2,1)S(1)}, bf16[32,1536]{1,0:T(8,128)(2,1)S(1)}, u32[]{:S(2)}, u32[]{:S(2)}) collective-permute-start(bf16[32,1536]{1,0:T(8,128)(2,1)S(1)} %get-tuple-element.11), channel_id=1, source_target_pairs={{0,4},{2,6},{4,0},{6,2},{8,12},{10,14},{12,8},{14,10},{1,5},{3,7},... | collective-permute-start | bytes 294920 | tf_op jit(solution)/shard_map/ppermute | solution.py:20
  59.4 2.9 %collective-permute-done.12 = bf16[32,1536]{1,0:T(8,128)(2,1)S(1)} collective-permute-done((bf16[32,1536]{1,0:T(8,128)(2,1)S(1)}, bf16[32,1536]{1,0:T(8,128)(2,1)S(1)}, u32[]{:S(2)}, u32[]{:S(2)}) %collective-permute-start.12) | collective-permute-done | bytes 98336 | tf_op jit(solution)/shard_map/ppermute | solution.py:20
  63.5 2.8 %collective-permute-start.13 = (bf16[32,1536]{1,0:T(8,128)(2,1)}, bf16[32,1536]{1,0:T(8,128)(2,1)}, u32[]{:S(2)}, u32[]{:S(2)}) collective-permute-start(bf16[32,1536]{1,0:T(8,128)(2,1)} %fusion.2), channel_id=1, source_target_pairs={{0,8},{2,10},{4,12},{6,14},{8,0},{10,2},{12,4},{14,6},{1,9},{3,11}... | collective-permute-start | bytes 294920 | tf_op jit(solution)/shard_map/ppermute | solution.py:20
  66.3 3.1 %collective-permute-done.13 = bf16[32,1536]{1,0:T(8,128)(2,1)} collective-permute-done((bf16[32,1536]{1,0:T(8,128)(2,1)}, bf16[32,1536]{1,0:T(8,128)(2,1)}, u32[]{:S(2)}, u32[]{:S(2)}) %collective-permute-start.13) | collective-permute-done | bytes 98336 | tf_op jit(solution)/shard_map/ppermute | solution.py:20
  69.4 1.0 %add_convert_fusion.4 = bf16[32,1536]{1,0:T(8,128)(2,1)S(1)} fusion(f32[32,1536]{1,0:T(8,128)S(1)} %get-tuple-element.12, bf16[32,1536]{1,0:T(8,128)(2,1)S(1)} %collective-permute-done.11, bf16[32,1536]{1,0:T(8,128)(2,1)S(1)} %collective-permute-done.10, bf16[32,1536]{1,0:T(8,128)(2,1)} %collective-permute-done.13, bf16[32,1536]{1,0:T(8,128)(2,1)} %copy-done.20, ...), kind=kLoop, calls=%fused_computation.15 | loop fusion | flops 589824 | bytes 688131 | tf_op jit(solution)/shard_map/convert_element_type | solution.py:160
  70.4 1.8 %collective-permute-start.14 = (bf16[32,1536]{1,0:T(8,128)(2,1)S(1)}, bf16[32,1536]{1,0:T(8,128)(2,1)S(1)}, u32[]{:S(2)}, u32[]{:S(2)}) collective-permute-start(bf16[32,1536]{1,0:T(8,128)(2,1)S(1)} %add_convert_fusion.4), channel_id=1, source_target_pairs={{0,2},{2,0},{4,6},{6,4},{8,10},{10,8},{12,14},{14,12},{1,3},{3,1},... | collective-permute-start | bytes 294920 | tf_op jit(solution)/shard_map/ppermute | solution.py:20
  72.2 2.9 %collective-permute-done.14 = bf16[32,1536]{1,0:T(8,128)(2,1)S(1)} collective-permute-done((bf16[32,1536]{1,0:T(8,128)(2,1)S(1)}, bf16[32,1536]{1,0:T(8,128)(2,1)S(1)}, u32[]{:S(2)}, u32[]{:S(2)}) %collective-permute-start.14) | collective-permute-done | bytes 98336 | tf_op jit(solution)/shard_map/ppermute | solution.py:20
  75.1 1.0 %convert_select_fusion.1 = (f32[32,1536]{1,0:T(8,128)S(1)}, f32[32,1536]{1,0:T(8,128)S(1)}) fusion(bf16[32,1536]{1,0:T(8,128)(2,1)S(1)} %collective-permute-done.14, pred[]{:T(512)S(6)} %eq.6, bf16[32,1536]{1,0:T(8,128)(2,1)S(1)} %collective-permute-done.11, bf16[32,1536]{1,0:T(8,128)(2,1)S(1)} %collective-permute-done.10, ...), kind=kLoop, calls=%fused_computation.9 | loop fusion | flops 638976 | bytes 1081347 | tf_op jit(solution)/shard_map/jit(_where)/select_n | solution.py:161
  76.1 1.8 %fusion = f32[1,64,1536]{2,1,0:T(8,128)} fusion(f32[64,1536]{1,0:T(8,128)} %param.10, f32[32,1536]{1,0:T(8,128)S(1)} %convert_select_fusion, f32[32,1536]{1,0:T(8,128)S(1)} %get-tuple-element.9), kind=kLoop, calls=%fused_computation.3 | loop fusion | flops 196608 | bytes 1179648 | tf_op jit(solution)/shard_map/broadcast_in_dim | solution.py:201
  (71 shorter events, 14.5 us)
Async XLA Ops:
  0.0 18.3 %copy-start = (bf16[1536,1024]{1,0:T(8,128)(2,1)S(1)}, bf16[1536,1024]{1,0:T(8,128)(2,1)}, u32[]{:S(2)}) copy-start(bf16[1536,1024]{1,0:T(8,128)(2,1)} %param.16) | copy-start | bytes 9437188
  2.3 12.3 %collective-permute-start.4 = (f32[64,1536]{1,0:T(8,128)}, f32[64,1536]{1,0:T(8,128)S(1)}, u32[]{:S(2)}, u32[]{:S(2)}) collective-permute-start(f32[64,1536]{1,0:T(8,128)} %shard_map.91), channel_id=1, source_target_pairs={{0,1},{1,0},{2,3},{3,2},{4,5},{5,4},{6,7},{7,6},{8,9},{9,8},{10,11... | collective-permute-start | bytes 1179656 | tf_op jit(solution)/shard_map/ppermute | solution.py:20
  6.7 1.6 %collective-permute-start = (f32[3,3072]{1,0:T(4,128)}, f32[3,3072]{1,0:T(4,128)}, u32[]{:S(2)}, u32[]{:S(2)}) collective-permute-start(f32[3,3072]{1,0:T(4,128)} %bitcast.16), channel_id=1, source_target_pairs={{0,16},{16,0},{1,17},{17,1},{2,18},{18,2},{3,19},{19,3},{4,20},{20... | collective-permute-start | bytes 110600 | tf_op jit(solution)/shard_map/ppermute | solution.py:20
  18.3 6.0 %copy-start.1 = (f32[128,1024]{1,0:T(8,128)}, f32[128,1024]{1,0:T(8,128)S(1)}, u32[]{:S(2)}) copy-start(f32[128,1024]{1,0:T(8,128)S(1)} %fusion.5.refs_8_) | copy-start | bytes 1572868
  18.3 2.3 %copy-start.18 = (bf16[1536,1024]{1,0:T(8,128)(2,1)S(1)}, bf16[1536,1024]{1,0:T(8,128)(2,1)}, u32[]{:S(2)}) copy-start(bf16[1536,1024]{1,0:T(8,128)(2,1)} %param.15) | copy-start | bytes 9437188
  18.9 6.6 %copy-start.3 = (f32[128,1024]{1,0:T(8,128)}, f32[128,1024]{1,0:T(8,128)S(1)}, u32[]{:S(2)}) copy-start(f32[128,1024]{1,0:T(8,128)S(1)} %fusion.4.refs_10_) | copy-start | bytes 1572868
  20.5 2.9 %copy-start.5 = (f32[128,1024]{1,0:T(8,128)}, f32[128,1024]{1,0:T(8,128)S(1)}, u32[]{:S(2)}) copy-start(f32[128,1024]{1,0:T(8,128)S(1)} %fusion.7.refs_4_) | copy-start | bytes 1572868
  20.6 2.3 %copy-start.19 = (bf16[1536,1024]{1,0:T(8,128)(2,1)S(1)}, bf16[1536,1024]{1,0:T(8,128)(2,1)}, u32[]{:S(2)}) copy-start(bf16[1536,1024]{1,0:T(8,128)(2,1)} %param.14) | copy-start | bytes 9437188
  21.1 5.7 %copy-start.7 = (f32[128,1024]{1,0:T(8,128)}, f32[128,1024]{1,0:T(8,128)S(1)}, u32[]{:S(2)}) copy-start(f32[128,1024]{1,0:T(8,128)S(1)} %fusion.8.refs_2_) | copy-start | bytes 1572868
  21.2 7.6 %collective-permute-start.3 = (f32[64,1024]{1,0:T(8,128)S(1)}, f32[64,1024]{1,0:T(8,128)S(1)}, u32[]{:S(2)}, u32[]{:S(2)}) collective-permute-start(f32[64,1024]{1,0:T(8,128)S(1)} %slice.86), channel_id=1, source_target_pairs={{0,16},{16,0},{1,17},{17,1},{2,18},{18,2},{3,19},{19,3},{4,20},{20... | collective-permute-start | bytes 786440 | tf_op jit(solution)/shard_map/ppermute | solution.py:20
  23.4 5.4 %copy-start.9 = (f32[128,1024]{1,0:T(8,128)}, f32[128,1024]{1,0:T(8,128)S(1)}, u32[]{:S(2)}) copy-start(f32[128,1024]{1,0:T(8,128)S(1)} %fusion.6.refs_6_) | copy-start | bytes 1572868
  24.2 5.9 %collective-permute-start.5 = (f32[64,1024]{1,0:T(8,128)}, f32[64,1024]{1,0:T(8,128)S(1)}, u32[]{:S(2)}, u32[]{:S(2)}) collective-permute-start(f32[64,1024]{1,0:T(8,128)} %slice.87), channel_id=1, source_target_pairs={{0,16},{16,0},{1,17},{17,1},{2,18},{18,2},{3,19},{19,3},{4,20},{20... | collective-permute-start | bytes 786440 | tf_op jit(solution)/shard_map/ppermute | solution.py:20
  25.0 5.9 %collective-permute-start.6 = (f32[64,1024]{1,0:T(8,128)}, f32[64,1024]{1,0:T(8,128)}, u32[]{:S(2)}, u32[]{:S(2)}) collective-permute-start(f32[64,1024]{1,0:T(8,128)} %slice.88), channel_id=1, source_target_pairs={{0,16},{16,0},{1,17},{17,1},{2,18},{18,2},{3,19},{19,3},{4,20},{20... | collective-permute-start | bytes 786440 | tf_op jit(solution)/shard_map/ppermute | solution.py:20
  26.2 4.7 %collective-permute-start.7 = (f32[64,1024]{1,0:T(8,128)}, f32[64,1024]{1,0:T(8,128)}, u32[]{:S(2)}, u32[]{:S(2)}) collective-permute-start(f32[64,1024]{1,0:T(8,128)} %slice.89), channel_id=1, source_target_pairs={{0,16},{16,0},{1,17},{17,1},{2,18},{18,2},{3,19},{19,3},{4,20},{20... | collective-permute-start | bytes 786440 | tf_op jit(solution)/shard_map/ppermute | solution.py:20
  26.8 2.0 %copy-start.11 = (f32[128,1024]{1,0:T(8,128)}, f32[128,1024]{1,0:T(8,128)S(1)}, u32[]{:S(2)}) copy-start(f32[128,1024]{1,0:T(8,128)S(1)} %fusion.9.refs_0_) | copy-start | bytes 1572868
  26.8 16.9 %copy-start.21 = (f32[1,1536]{1,0:T(1,128)S(1)}, f32[1,1536]{1,0:T(1,128)}, u32[]{:S(2)}) copy-start(f32[1,1536]{1,0:T(1,128)} %get-tuple-element.20) | copy-start | bytes 18436
  27.6 3.3 %collective-permute-start.2 = (f32[64,1024]{1,0:T(8,128)}, f32[64,1024]{1,0:T(8,128)}, u32[]{:S(2)}, u32[]{:S(2)}) collective-permute-start(f32[64,1024]{1,0:T(8,128)} %slice.85), channel_id=1, source_target_pairs={{0,16},{16,0},{1,17},{17,1},{2,18},{18,2},{3,19},{19,3},{4,20},{20... | collective-permute-start | bytes 786440 | tf_op jit(solution)/shard_map/ppermute | solution.py:20
  29.5 1.9 %collective-permute-start.1 = (f32[64,1024]{1,0:T(8,128)}, f32[64,1024]{1,0:T(8,128)}, u32[]{:S(2)}, u32[]{:S(2)}) collective-permute-start(f32[64,1024]{1,0:T(8,128)} %slice.84), channel_id=1, source_target_pairs={{0,16},{16,0},{1,17},{17,1},{2,18},{18,2},{3,19},{19,3},{4,20},{20... | collective-permute-start | bytes 786440 | tf_op jit(solution)/shard_map/ppermute | solution.py:20
  31.4 1.0 %copy-start.2 = (f32[128,1024]{1,0:T(8,128)S(1)}, f32[128,1024]{1,0:T(8,128)}, u32[]{:S(2)}) copy-start(f32[128,1024]{1,0:T(8,128)} %copy-done.1) | copy-start | bytes 1572868
  32.4 1.0 %copy-start.4 = (f32[128,1024]{1,0:T(8,128)S(1)}, f32[128,1024]{1,0:T(8,128)}, u32[]{:S(2)}) copy-start(f32[128,1024]{1,0:T(8,128)} %copy-done.3) | copy-start | bytes 1572868
  33.5 1.0 %copy-start.6 = (f32[128,1024]{1,0:T(8,128)S(1)}, f32[128,1024]{1,0:T(8,128)}, u32[]{:S(2)}) copy-start(f32[128,1024]{1,0:T(8,128)} %copy-done.5) | copy-start | bytes 1572868
  34.5 1.0 %copy-start.8 = (f32[128,1024]{1,0:T(8,128)S(1)}, f32[128,1024]{1,0:T(8,128)}, u32[]{:S(2)}) copy-start(f32[128,1024]{1,0:T(8,128)} %copy-done.7) | copy-start | bytes 1572868
  35.6 1.0 %copy-start.10 = (f32[128,1024]{1,0:T(8,128)S(1)}, f32[128,1024]{1,0:T(8,128)}, u32[]{:S(2)}) copy-start(f32[128,1024]{1,0:T(8,128)} %copy-done.9) | copy-start | bytes 1572868
  36.6 1.0 %copy-start.12 = (f32[128,1024]{1,0:T(8,128)S(1)}, f32[128,1024]{1,0:T(8,128)}, u32[]{:S(2)}) copy-start(f32[128,1024]{1,0:T(8,128)} %copy-done.11) | copy-start | bytes 1572868
  43.4 1.7 %collective-permute-start.8 = (bf16[128,1024]{1,0:T(8,128)(2,1)S(1)}, bf16[128,1024]{1,0:T(8,128)(2,1)}, u32[]{:S(2)}, u32[]{:S(2)}) collective-permute-start(bf16[128,1024]{1,0:T(8,128)(2,1)S(1)} %shard_map.92.mine_ref), channel_id=1, source_target_pairs={{0,16},{16,0},{1,17},{17,1},{2,18},{18,2},{3,19},{19,3},{4,20},{20... | collective-permute-start | bytes 786440 | tf_op jit(solution)/shard_map/ppermute | solution.py:20
  45.2 1.9 %copy-start.13 = (bf16[1024,1536]{1,0:T(8,128)(2,1)S(1)}, bf16[1024,1536]{1,0:T(8,128)(2,1)}, u32[]{:S(2)}) copy-start(bf16[1024,1536]{1,0:T(8,128)(2,1)} %w_ref.1) | copy-start | bytes 9437188
  49.1 6.3 %collective-permute-start.10 = (bf16[32,1536]{1,0:T(8,128)(2,1)S(1)}, bf16[32,1536]{1,0:T(8,128)(2,1)S(1)}, u32[]{:S(2)}, u32[]{:S(2)}) collective-permute-start(bf16[32,1536]{1,0:T(8,128)(2,1)S(1)} %get-tuple-element.15), channel_id=1, source_target_pairs={{0,2},{1,3},{2,0},{3,1},{4,6},{5,7},{6,4},{7,5},{8,10},{9,11},{10,... | collective-permute-start | bytes 294920 | tf_op jit(solution)/shard_map/ppermute | solution.py:20
  51.0 6.5 %collective-permute-start.11 = (bf16[32,1536]{1,0:T(8,128)(2,1)S(1)}, bf16[32,1536]{1,0:T(8,128)(2,1)S(1)}, u32[]{:S(2)}, u32[]{:S(2)}) collective-permute-start(bf16[32,1536]{1,0:T(8,128)(2,1)S(1)} %get-tuple-element.14), channel_id=1, source_target_pairs={{0,3},{1,2},{2,1},{3,0},{4,7},{5,6},{6,5},{7,4},{8,11},{9,10},{10,... | collective-permute-start | bytes 294920 | tf_op jit(solution)/shard_map/ppermute | solution.py:20
  52.4 5.1 %collective-permute-start.9 = (bf16[32,1536]{1,0:T(8,128)(2,1)S(1)}, bf16[32,1536]{1,0:T(8,128)(2,1)S(1)}, u32[]{:S(2)}, u32[]{:S(2)}) collective-permute-start(bf16[32,1536]{1,0:T(8,128)(2,1)S(1)} %get-tuple-element.13), channel_id=1, source_target_pairs={{0,1},{1,0},{2,3},{3,2},{4,5},{5,4},{6,7},{7,6},{8,9},{9,8},{10,11... | collective-permute-start | bytes 294920 | tf_op jit(solution)/shard_map/ppermute | solution.py:20
  57.5 4.7 %collective-permute-start.12 = (bf16[32,1536]{1,0:T(8,128)(2,1)S(1)}, bf16[32,1536]{1,0:T(8,128)(2,1)S(1)}, u32[]{:S(2)}, u32[]{:S(2)}) collective-permute-start(bf16[32,1536]{1,0:T(8,128)(2,1)S(1)} %get-tuple-element.11), channel_id=1, source_target_pairs={{0,4},{2,6},{4,0},{6,2},{8,12},{10,14},{12,8},{14,10},{1,5},{3,7},... | collective-permute-start | bytes 294920 | tf_op jit(solution)/shard_map/ppermute | solution.py:20
  63.5 5.8 %collective-permute-start.13 = (bf16[32,1536]{1,0:T(8,128)(2,1)}, bf16[32,1536]{1,0:T(8,128)(2,1)}, u32[]{:S(2)}, u32[]{:S(2)}) collective-permute-start(bf16[32,1536]{1,0:T(8,128)(2,1)} %fusion.2), channel_id=1, source_target_pairs={{0,8},{2,10},{4,12},{6,14},{8,0},{10,2},{12,4},{14,6},{1,9},{3,11}... | collective-permute-start | bytes 294920 | tf_op jit(solution)/shard_map/ppermute | solution.py:20
  70.4 4.7 %collective-permute-start.14 = (bf16[32,1536]{1,0:T(8,128)(2,1)S(1)}, bf16[32,1536]{1,0:T(8,128)(2,1)S(1)}, u32[]{:S(2)}, u32[]{:S(2)}) collective-permute-start(bf16[32,1536]{1,0:T(8,128)(2,1)S(1)} %add_convert_fusion.4), channel_id=1, source_target_pairs={{0,2},{2,0},{4,6},{6,4},{8,10},{10,8},{12,14},{14,12},{1,3},{3,1},... | collective-permute-start | bytes 294920 | tf_op jit(solution)/shard_map/ppermute | solution.py:20
  (5 other events, 3.9 us)

commit v2 on v1

v2 whole, which is shorter than its diff:
```python
import functools
import math

import jax
import jax.numpy as jnp
from jax import lax
from jax.experimental import pallas as pl
from jax.experimental.pallas import tpu as pltpu
from jax.sharding import PartitionSpec as P

HD = 128
NSTEPS = 50
F32 = jnp.float32
BF16 = jnp.bfloat16
VMEM = pl.BlockSpec(memory_space=pltpu.VMEM)
SMEM = pl.BlockSpec(memory_space=pltpu.SMEM)
HBM = pl.BlockSpec(memory_space=pltpu.HBM)


def xor_permute(x, axes, mask):
    return lax.ppermute(x, axes, [(i, i ^ mask) for i in range(lax.axis_size(axes))])


def dot(a, b):
    return jnp.dot(a, b, preferred_element_type=F32)


def embed_half(step_id, half_width, branch_index):
    frequency = jnp.exp(-math.log(10000.0) * jnp.arange(half_width, dtype=F32) / half_width)
    phases = step_id.astype(F32) * frequency
    return jnp.where(branch_index == 0, jnp.sin(phases), jnp.cos(phases))[None, :]


def in_vmem(*arrays):
    return [pltpu.with_memory_space_constraint(array, pltpu.VMEM) for array in arrays]


def in_hbm(*arrays):
    return [pltpu.with_memory_space_constraint(array, pltpu.HBM) for array in arrays]


def call(kernel, out_shape, in_specs, out_specs, scratch_shapes=()):
    return pl.pallas_call(
        kernel,
        out_shape=out_shape,
        in_specs=in_specs,
        out_specs=out_specs,
        scratch_shapes=scratch_shapes,
        compiler_params=pltpu.CompilerParams(vmem_limit_bytes=16 << 20),
    )


def norm_kernel(pieces, branch_ref, states_ref, out_ref, tokens_ref, sems):
    half_width = out_ref.shape[1]
    rows, width = tokens_ref.shape
    size = rows // pieces
    copies = []
    for piece in range(pieces):
        sl = slice(piece * size, (piece + 1) * size)
        copy = pltpu.make_async_copy(states_ref.at[sl], tokens_ref.at[sl], sems.at[piece])
        copy.start()
        copies.append(copy)
    start = pl.multiple_of(branch_ref[0] * half_width, HD)
    for piece in range(pieces):
        sl = slice(piece * size, (piece + 1) * size)
        copies[piece].wait()
        tokens = tokens_ref[sl, :]
        mean = jnp.sum(tokens, axis=1, keepdims=True) * (1.0 / width)
        centered = tokens - mean
        variance = jnp.sum(centered * centered, axis=1, keepdims=True) * (1.0 / width)
        inverse = 1.0 / jnp.sqrt(variance + 1e-06)
        out_ref[sl, :] = (tokens_ref[sl, pl.ds(start, half_width)] - mean) * inverse


def normed_half(states, branch_index):
    rows, width = states.shape
    pieces = 4
    return call(
        functools.partial(norm_kernel, pieces),
        pltpu.VMEM((rows, width // 2), F32),
        [SMEM, HBM],
        VMEM,
        [pltpu.VMEM((rows, width), F32), pltpu.SemaphoreType.DMA((pieces,))],
    )(branch_index[None], *in_hbm(states))


def halves_kernel(branch_ref, modulation_ref, mine_ref, send_ref):
    half_width = mine_ref.shape[2]
    branch = branch_ref[0]
    for row in range(mine_ref.shape[0]):
        mine_ref[row] = modulation_ref[row, :, pl.ds(pl.multiple_of(branch * half_width, HD), half_width)]
        send_ref[row] = modulation_ref[
            row, :, pl.ds(pl.multiple_of((1 - branch) * half_width, HD), half_width)
        ]


def modulation_halves(modulation, branch_index):
    rows, _, width = modulation.shape
    out = pltpu.VMEM((rows, 1, width // 2), F32)
    return call(halves_kernel, [out, out], [SMEM, VMEM], [VMEM, VMEM])(branch_index[None], modulation)


def modulate_and_project(tokens_ref, mine_ref, other_ref, embedding_ref, weights, keep_ref, send_ref):
    rows = tokens_ref.shape[0]
    tokens = tokens_ref[...]
    embedding = embedding_ref[...]
    modulated = jnp.concatenate(
        [
            (tokens * (1.0 + mod_ref[1]) + mod_ref[0] + embedding).astype(BF16)
            for mod_ref in (mine_ref, other_ref)
        ],
        axis=0,
    )
    column = 0
    for weight_ref, ready in weights:
        ready()
        columns = weight_ref.shape[1]
        chunk = min(columns, 512)
        for start in range(0, columns, chunk):
            projected = dot(modulated, weight_ref[:, start:start + chunk])
            sl = slice(column + start, column + start + chunk)
            keep_ref[:, sl] = projected[:rows]
            send_ref[:, sl] = projected[rows:]
        column += columns


def first_kernel(*refs):
    tokens_ref, mine_ref, other_ref, embedding_ref = refs[:4]
    sources, targets = refs[4:8], refs[8:12]
    keep_ref, send_ref, sems = refs[12:]
    copies = [
        pltpu.make_async_copy(source, target, sems.at[i])
        for i, (source, target) in enumerate(zip(sources, targets))
    ]
    for copy in copies:
        copy.start()
    weights = [(target, copy.wait) for target, copy in zip(targets[:3], copies[:3])]
    modulate_and_project(tokens_ref, mine_ref, other_ref, embedding_ref, weights, keep_ref, send_ref)
    copies[3].wait()


def project_first(tokens, mine, other, embedding, weights):
    out = pltpu.VMEM((tokens.shape[0], 3 * weights[0].shape[1]), F32)
    result = call(
        first_kernel,
        [pltpu.VMEM(w.shape, w.dtype) for w in weights] + [out, out],
        [VMEM] * 4 + [HBM] * 4,
        [VMEM] * 6,
        [pltpu.SemaphoreType.DMA((4,))],
    )(*in_vmem(tokens, mine, other, embedding), *in_hbm(*weights))
    return result[:4], result[4], result[5]


def later_kernel(tokens_ref, mine_ref, other_ref, embedding_ref, wq_ref, wk_ref, wv_ref, keep_ref, send_ref):
    weights = [(ref, lambda: None) for ref in (wq_ref, wk_ref, wv_ref)]
    modulate_and_project(tokens_ref, mine_ref, other_ref, embedding_ref, weights, keep_ref, send_ref)


def project_later(tokens, mine, other, embedding, weights):
    out = pltpu.VMEM((tokens.shape[0], 3 * weights[0].shape[1]), F32)
    return call(later_kernel, [out, out], [VMEM] * 7, [VMEM] * 2)(
        *in_vmem(tokens, mine, other, embedding, *weights)
    )


def attention_kernel(*refs):
    out_ref = refs[-1]
    blocks = [(refs[i], refs[i + 1]) for i in range(0, len(refs) - 1, 2)]
    columns = out_ref.shape[1]

    def part(which, head):
        sl = slice(which * columns + head * HD, which * columns + (head + 1) * HD)
        return jnp.concatenate(
            [(mine[:, sl] + other[:, sl]).astype(BF16) for mine, other in blocks], axis=0
        )

    heads = columns // HD
    all_scores = [
        lax.dot_general(
            part(0, head), part(1, head), (((1,), (1,)), ((), ())), preferred_element_type=F32
        )
        for head in range(heads)
    ]
    all_probs = []
    for scores in all_scores:
        scores = scores * (1.0 / math.sqrt(HD))
        scores = jnp.exp(scores - jnp.max(scores, axis=1, keepdims=True))
        all_probs.append((scores / jnp.sum(scores, axis=1, keepdims=True)).astype(BF16))
    for head, probs in enumerate(all_probs):
        out_ref[:, head * HD:(head + 1) * HD] = dot(probs, part(2, head)).astype(BF16)


def attention(blocks):
    flat = [array for block in blocks for array in block]
    rows, columns = flat[0].shape
    return call(
        attention_kernel,
        pltpu.VMEM((rows * len(blocks), columns // 3), BF16),
        [VMEM] * len(flat),
        VMEM,
    )(*in_vmem(*flat))


def project_kernel(floats_ref, mine_ref, other_ref, w_ref, mine_mod_ref, other_mod_ref, *out_refs):
    lat = mine_ref.shape[0]
    rows, columns = out_refs[0].shape
    both = jnp.concatenate([mine_ref[...], other_ref[...]], axis=0)
    mine_factor, other_factor = floats_ref[0], floats_ref[1]
    chunk = 512 if columns % 512 == 0 else HD
    for start in range(0, columns, chunk):
        sl = slice(start, start + chunk)
        partial = dot(both, w_ref[:, sl]).astype(BF16).astype(F32)
        mine = mine_factor * (1.0 + mine_mod_ref[2, :, sl])
        other = other_factor * (1.0 + other_mod_ref[2, :, sl])
        for block, out_ref in enumerate(out_refs):
            here = block * rows
            out_ref[:, sl] = (
                mine * partial[here:here + rows] + other * partial[lat + here:lat + here + rows]
            )


def project(factors, mine, other, w_out, mine_mod, other_mod, blocks):
    lat = mine.shape[0]
    columns = w_out.shape[1]
    return call(
        project_kernel,
        [pltpu.VMEM((lat // blocks, columns), F32)] * blocks,
        [SMEM] + [VMEM] * 5,
        [VMEM] * blocks,
    )(factors, *in_vmem(mine, other, w_out, mine_mod, other_mod))


def scan_general(parts):
    total = parts[0]
    for mask in range(1, len(parts)):
        total = total + xor_permute(parts[mask].astype(BF16), "tok", mask).astype(F32)
    position = lax.axis_index("tm")
    result, group = total, total
    mask = 1
    while mask < lax.axis_size("tm"):
        received = xor_permute(group.astype(BF16), "tm", mask).astype(F32)
        result = result + jnp.where(position & mask != 0, received, 0.0)
        group = group + received
        mask *= 2
    return result


def scan_planes(parts):
    axes = ("tm", "tok")
    position = lax.axis_index("tm")
    odd = position & 1 == 1
    rows = parts[0].shape[0] // 2

    def near(x):
        return jnp.where(odd, x[rows:], x[:rows])

    def far(x):
        return jnp.where(odd, x[:rows], x[rows:])

    diagonal = xor_permute(far(parts[1]).astype(BF16), axes, 3)
    across = xor_permute(near(parts[1]).astype(BF16), axes, 1)
    beside = xor_permute(far(parts[0]).astype(BF16), axes, 2)
    own_time = near(parts[0]) + across.astype(F32)
    pair_time = beside.astype(F32) + diagonal.astype(F32)
    group = own_time + pair_time
    earlier = jnp.zeros_like(group)
    mask = 2
    while mask < lax.axis_size("tm"):
        received = xor_permute(group.astype(BF16), "tm", mask).astype(F32)
        earlier = earlier + jnp.where(position & mask != 0, received, 0.0)
        group = group + received
        mask *= 2
    own = earlier + own_time + jnp.where(odd, pair_time, 0.0)
    for_pair = earlier + pair_time + jnp.where(odd, 0.0, own_time)
    returned = xor_permute(for_pair.astype(BF16), "tm", 1).astype(F32)
    return jnp.concatenate([jnp.where(odd, returned, own), jnp.where(odd, own, returned)], axis=0)


def body(
    states, start_state, timesteps, guidance_index, modulation, w_query, w_key, w_value, w_out
):
    tok_count = lax.axis_size("tok")
    branch_index = lax.axis_index("branch")
    rows, model_width = states.shape[1:]
    half_width = model_width // 2
    normed = normed_half(states[0], branch_index)
    tokens = [normed] + [xor_permute(normed, "tok", mask) for mask in range(1, tok_count)]

    mine_mod, send_mod = modulation_halves(jnp.transpose(modulation, (1, 0, 2)), branch_index)
    other_mod = xor_permute(send_mod, "branch", 1)
    embedding = embed_half(timesteps[0], half_width, branch_index)

    weights, keep, send = project_first(
        tokens[0], mine_mod, other_mod, embedding, (w_query, w_key, w_value, w_out)
    )
    blocks = [(keep, xor_permute(send, "branch", 1))]
    for block in tokens[1:]:
        keep, send = project_later(block, mine_mod, other_mod, embedding, weights[:3])
        blocks.append((keep, xor_permute(send, "branch", 1)))
    attended = attention(blocks)
    attended_other = xor_permute(attended, "branch", 1)

    guide_scale = 1.5 + 0.5 * guidance_index[0].astype(F32)
    step_size = 2.0 * (1.0 + timesteps[0].astype(F32)) / NSTEPS
    factors = step_size * jnp.stack([guide_scale, 1.0 - guide_scale])
    factors = jnp.where(branch_index == 0, factors, factors[::-1])
    parts = project(factors, attended, attended_other, weights[3], mine_mod, other_mod, tok_count)
    pairs = tok_count == 2 and lax.axis_size("tm") % 2 == 0 and rows % 32 == 0
    scan = scan_planes if pairs else scan_general
    return (start_state + scan(parts))[None]


def solution(mesh):
    in_specs = (
        P("tm", "tok", None),
        P("tok", "branch"),
        P("tm"),
        P(),
        P("branch", None, None),
        P("branch", "tok"),
        P("branch", "tok"),
        P("branch", "tok"),
        P("tok", "branch"),
    )
    out_specs = P("tm", "tok", "branch")
    return jax.shard_map(body, mesh=mesh, in_specs=in_specs, out_specs=out_specs, check_vma=False)
```

time: 79 us -> 49.6 us (0.63)
  local copies, waits for them, and re-layouts: 19.9 us -> 3.52 us
  other arithmetic: 8.29 us -> 1.5 us
  matrix products: 5.34 us -> 0 us
  Pallas kernels: 8.24 us -> 11.6 us
  waiting for transfers between devices: 20.5 us -> 17.6 us
    unnamed x45 -> x16, local copies, waits for them, and re-layouts: 16.1 us -> 3.43 us
    dot_general x6 -> x0, matrix products: 5.34 us -> none  [dot(): return jnp.dot(a, b, preferred_element_type=F32)]
    slice x6 -> x0, local copies, waits for them, and re-layouts: 3.75 us -> none  [body(): blocks.append([(p, xor_permute(p[rows:], 'branch', 1)) for p in projected])]
    pallas_call x3 -> x6, Pallas kernels: 8.24 us -> 11.6 us  [the longest x1 4.68 us: project_first(): call(first_kernel, [pltpu.VMEM(w.shape, w.dtype) for w in weights] + [out...]
    ppermute x15 -> x11, waiting for transfers between devices: 20.5 us -> 17.6 us  [xor_permute(): lax.ppermute(x, axes, [(i, i ^ mask) for i in range(lax.axis_size(axes))])]
    add x2 -> x0, other arithmetic: 2.29 us -> none  [body(): 1.0 + mod[1:2]]
    another operation x2 -> x1, other arithmetic: 1.26 us -> 0.07 us  [body(): factors = step_size * jnp.stack([guide_scale, 1.0 - guide_scale])]
    broadcast_in_dim x1, other arithmetic: 1.8 us -> 0.8 us  [body(): return (start_state + scan(parts))[None]]
  transfers between devices with their start and end apart: 15 -> 11, of which waited for: 9 -> 9; matrix products, arithmetic and copies ran while one was open for 11% -> 1% of each run, Pallas kernels for 0% -> 14%
where the time goes in v2:
time: 49.6 us; the launch traced here: 49.2 us
  waiting for transfers between devices  17.6 us (35%)
  starting transfers between devices  13.6 us (27%)
  Pallas kernels  11.6 us (23%)
  local copies, waits for them, and re-layouts  3.52 us (7%)
  other arithmetic  1.5 us (3%)
  between operations  1.44 us (3%)
    ppermute x11, waiting for transfers between devices, xor_permute(): lax.ppermute(x, axes, [(i, i ^ mask) for i in range(lax.axis_size(axes))])  17.6 us
    ppermute x11, starting transfers between devices, xor_permute(): lax.ppermute(x, axes, [(i, i ^ mask) for i in range(lax.axis_size(axes))])  13.6 us
    pallas_call x1, Pallas kernels, project_first(): call(first_kernel, [pltpu.VMEM(w.shape, w.dtype) for w in weights] + [out...  4.68 us
    unnamed x16, local copies, waits for them, and re-layouts  3.43 us
    pallas_call x1, Pallas kernels, project_later(): call(later_kernel, [out, out], [VMEM] * 7, [VMEM] * 2)  2.39 us
    pallas_call x1, Pallas kernels, project(): call(project_kernel, [pltpu.VMEM((lat // blocks, columns), F32)] * blocks...  1.95 us
    pallas_call x1, Pallas kernels, normed_half(): call(functools.partial(norm_kernel, pieces), pltpu.VMEM((rows, width // 2...  1.86 us
  transfers between devices with their start and end apart: 11, of which 9 were waited for; matrix products, arithmetic and copies ran while one was open for 1% of the time, Pallas kernels for 14%

profile of v2, /device:TPU:0, one launch (start us, length us, event | category | flops | bytes accessed | tf_op | source)
XLA Modules:
  0.0 49.2 jit_solution(13311855365889105421)
XLA Ops:
  0.0 1.9 %shard_map.91.refs_0_ = f32[64,1536]{1,0:T(8,128)S(1)} custom-call(s32[1]{0:T(128)} %bitcast.1.branch_ref, f32[64,3072]{1,0:T(8,128)} %bitcast.7), custom_call_target="tpu_custom_call" | custom-call | tf_op jit(solution)/shard_map/pallas_call | solution.py:78
  1.9 3.0 %collective-permute-start.2 = (f32[64,1536]{1,0:T(8,128)S(1)}, f32[64,1536]{1,0:T(8,128)}, u32[]{:S(2)}, u32[]{:S(2)}) collective-permute-start(f32[64,1536]{1,0:T(8,128)S(1)} %shard_map.91.refs_0_), channel_id=1, source_target_pairs={{0,1},{1,0},{2,3},{3,2},{4,5},{5,4},{6,7},{7,6},{8,9},{9,8},{10,11... | collective-permute-start | bytes 1179656 | tf_op jit(solution)/shard_map/ppermute | solution.py:21
  4.9 0.8 %copy-done.6 = f32[1,3,3072]{2,0,1:T(1,128)S(1)} copy-done((f32[1,3,3072]{2,0,1:T(1,128)S(1)}, f32[1,3,3072]{2,0,1:T(1,128)}, u32[]{:S(2)}) %copy-start.6) | copy-done | bytes 36888
  5.7 0.6 %copy-done = f32[3,1,1536]{2,1,0:T(1,128)} copy-done((f32[3,1,1536]{2,1,0:T(1,128)}, f32[3,1,1536]{2,1,0:T(1,128)S(1)}, u32[]{:S(2)}) %copy-start) | copy-done | bytes 18456
  6.9 0.2 broadcast_select_fusion.refs_3_.embedding_ref
  7.1 0.3 collective-permute-done.refs_2_.other_ref.other_mod_ref
  7.4 0.6 %copy-done.3 = f32[3,1,1536]{2,1,0:T(1,128)} copy-done((f32[3,1,1536]{2,1,0:T(1,128)}, f32[3,1,1536]{2,1,0:T(1,128)S(1)}, u32[]{:S(2)}) %copy-start.3) | copy-done | bytes 18456
  8.0 0.7 %copy-done.1 = f32[3,1,1536]{2,1,0:T(1,128)S(1)} copy-done((f32[3,1,1536]{2,1,0:T(1,128)S(1)}, f32[3,1,1536]{2,1,0:T(1,128)}, u32[]{:S(2)}) %copy-start.1) | copy-done | bytes 18456
  8.8 0.7 %copy-done.4 = f32[3,1,1536]{2,1,0:T(1,128)S(1)} copy-done((f32[3,1,1536]{2,1,0:T(1,128)S(1)}, f32[3,1,1536]{2,1,0:T(1,128)}, u32[]{:S(2)}) %copy-start.4) | copy-done | bytes 18456
  9.5 4.7 %shard_map.93 = (bf16[1536,1024]{1,0:T(8,128)(2,1)S(1)}, bf16[1536,1024]{1,0:T(8,128)(2,1)S(1)}, bf16[1536,1024]{1,0:T(8,128)(2,1)S(1)}, bf16[1024,1536]{1,0:T(8...) custom-call(f32[64,1536]{1,0:T(8,128)S(1)} %shard_map.91.refs_0_, f32[3,1,1536]{2,1,0:T(1,128)S(1)} %copy-done.1, ...), custom_call_target="tpu_custom_call" | custom-call | tf_op jit(solution)/shard_map/pallas_call | solution.py:144
  14.2 0.3 collective-permute-start.1
  14.4 2.4 %shard_map.94 = (f32[64,3072]{1,0:T(8,128)S(1)}, f32[64,3072]{1,0:T(8,128)S(1)}) custom-call(f32[64,1536]{1,0:T(8,128)} %collective-permute-done.2.tokens_ref, f32[3,1,1536]{2,1,0:T(1,128)S(1)} %copy-done.1, f32[3,1,1536]{2,1,0:T(1,128)S(1)} %copy-done.4, f32[1,1536]{1,0:T(1,128)S(1)} %broadcast_select_fusion.refs_3_.embedding_ref, ...), custom_call_target="tpu_custom_call" | custom-call | tf_op jit(solution)/shard_map/pallas_call | solution.py:161
  16.9 0.4 collective-permute-start.3
  17.9 1.3 %collective-permute-done.3.refs_3_ = f32[64,3072]{1,0:T(8,128)S(1)} collective-permute-done((f32[64,3072]{1,0:T(8,128)S(1)}, f32[64,3072]{1,0:T(8,128)S(1)}, u32[]{:S(2)}, u32[]{:S(2)}) %collective-permute-start.3) | collective-permute-done | bytes 786464 | tf_op jit(solution)/shard_map/ppermute | solution.py:21
  19.2 0.7 %shard_map.95.mine_ref = bf16[128,1024]{1,0:T(8,128)(2,1)S(1)} custom-call(f32[64,3072]{1,0:T(8,128)S(1)} %get-tuple-element.19.refs_0_, f32[64,3072]{1,0:T(8,128)S(1)} %collective-permute-done.1.refs_1_, f32[64,3072]{1,0:T(8,128)S(1)} %get-tuple-element.24.refs_2_, f32[64,3072]{1,0:T(8,128)S(1)} %collective-permute-done.3.refs_3_), custom_call_target="tpu_custom_call" | custom-call | tf_op jit(solution)/shard_map/pallas_call | solution.py:196
  19.9 0.4 collective-permute-start.4
  20.4 0.1 reverse.3
  20.5 1.1 %collective-permute-done.4.other_ref = bf16[128,1024]{1,0:T(8,128)(2,1)} collective-permute-done((bf16[128,1024]{1,0:T(8,128)(2,1)S(1)}, bf16[128,1024]{1,0:T(8,128)(2,1)}, u32[]{:S(2)}, u32[]{:S(2)}) %collective-permute-start.4) | collective-permute-done | bytes 262176 | tf_op jit(solution)/shard_map/ppermute | solution.py:21
  21.6 1.9 %shard_map.96 = (f32[64,1536]{1,0:T(8,128)S(1)}, f32[64,1536]{1,0:T(8,128)S(1)}) custom-call(f32[2]{0:T(128)S(1)} %broadcast_select_fusion.1.floats_ref, bf16[128,1024]{1,0:T(8,128)(2,1)S(1)} %shard_map.95.mine_ref, bf16[128,1024]{1,0:T(8,128)(2,1)} %collective-permute-done.4.other_ref, bf16[1024,1536]{1,0:T(8,128)(2,1)S(1)} %get-tuple-element.26.w_ref, ...), custom_call_target="tpu_custom_call" | custom-call | tf_op jit(solution)/shard_map/pallas_call | solution.py:225
  23.6 2.4 %collective-permute-start.7 = (bf16[32,1536]{1,0:T(8,128)(2,1)S(1)}, bf16[32,1536]{1,0:T(8,128)(2,1)S(1)}, u32[]{:S(2)}, u32[]{:S(2)}) collective-permute-start(bf16[32,1536]{1,0:T(8,128)(2,1)S(1)} %get-tuple-element.34), channel_id=1, source_target_pairs={{0,3},{1,2},{2,1},{3,0},{4,7},{5,6},{6,5},{7,4},{8,11},{9,10},{10,... | collective-permute-start | bytes 294920 | tf_op jit(solution)/shard_map/ppermute | solution.py:21
  26.1 0.6 %collective-permute-start.6 = (bf16[32,1536]{1,0:T(8,128)(2,1)S(1)}, bf16[32,1536]{1,0:T(8,128)(2,1)S(1)}, u32[]{:S(2)}, u32[]{:S(2)}) collective-permute-start(bf16[32,1536]{1,0:T(8,128)(2,1)S(1)} %select_convert_fusion.1), channel_id=1, source_target_pairs={{0,2},{1,3},{2,0},{3,1},{4,6},{5,7},{6,4},{7,5},{8,10},{9,11},{10,... | collective-permute-start | bytes 294920 | tf_op jit(solution)/shard_map/ppermute | solution.py:21
  26.6 0.6 %collective-permute-start.5 = (bf16[32,1536]{1,0:T(8,128)(2,1)S(1)}, bf16[32,1536]{1,0:T(8,128)(2,1)S(1)}, u32[]{:S(2)}, u32[]{:S(2)}) collective-permute-start(bf16[32,1536]{1,0:T(8,128)(2,1)S(1)} %get-tuple-element.33), channel_id=1, source_target_pairs={{0,1},{1,0},{2,3},{3,2},{4,5},{5,4},{6,7},{7,6},{8,9},{9,8},{10,11... | collective-permute-start | bytes 294920 | tf_op jit(solution)/shard_map/ppermute | solution.py:21
  27.3 2.4 %collective-permute-done.7 = bf16[32,1536]{1,0:T(8,128)(2,1)S(1)} collective-permute-done((bf16[32,1536]{1,0:T(8,128)(2,1)S(1)}, bf16[32,1536]{1,0:T(8,128)(2,1)S(1)}, u32[]{:S(2)}, u32[]{:S(2)}) %collective-permute-start.7) | collective-permute-done | bytes 98336 | tf_op jit(solution)/shard_map/ppermute | solution.py:21
  29.7 2.0 %collective-permute-done.6 = bf16[32,1536]{1,0:T(8,128)(2,1)S(1)} collective-permute-done((bf16[32,1536]{1,0:T(8,128)(2,1)S(1)}, bf16[32,1536]{1,0:T(8,128)(2,1)S(1)}, u32[]{:S(2)}, u32[]{:S(2)}) %collective-permute-start.6) | collective-permute-done | bytes 98336 | tf_op jit(solution)/shard_map/ppermute | solution.py:21
  31.8 1.6 %collective-permute-start.8 = (bf16[32,1536]{1,0:T(8,128)(2,1)S(1)}, bf16[32,1536]{1,0:T(8,128)(2,1)S(1)}, u32[]{:S(2)}, u32[]{:S(2)}) collective-permute-start(bf16[32,1536]{1,0:T(8,128)(2,1)S(1)} %get-tuple-element.31), channel_id=1, source_target_pairs={{0,4},{2,6},{4,0},{6,2},{8,12},{10,14},{12,8},{14,10},{1,5},{3,7},... | collective-permute-start | bytes 294920 | tf_op jit(solution)/shard_map/ppermute | solution.py:21
  33.5 3.1 %collective-permute-done.8 = bf16[32,1536]{1,0:T(8,128)(2,1)S(1)} collective-permute-done((bf16[32,1536]{1,0:T(8,128)(2,1)S(1)}, bf16[32,1536]{1,0:T(8,128)(2,1)S(1)}, u32[]{:S(2)}, u32[]{:S(2)}) %collective-permute-start.8) | collective-permute-done | bytes 98336 | tf_op jit(solution)/shard_map/ppermute | solution.py:21
  36.6 2.7 %collective-permute-start.9 = (bf16[32,1536]{1,0:T(8,128)(2,1)S(1)}, bf16[32,1536]{1,0:T(8,128)(2,1)S(1)}, u32[]{:S(2)}, u32[]{:S(2)}) collective-permute-start(bf16[32,1536]{1,0:T(8,128)(2,1)S(1)} %fusion.2), channel_id=1, source_target_pairs={{0,8},{2,10},{4,12},{6,14},{8,0},{10,2},{12,4},{14,6},{1,9},{3,11}... | collective-permute-start | bytes 294920 | tf_op jit(solution)/shard_map/ppermute | solution.py:21
  39.3 4.2 %collective-permute-done.9 = bf16[32,1536]{1,0:T(8,128)(2,1)S(1)} collective-permute-done((bf16[32,1536]{1,0:T(8,128)(2,1)S(1)}, bf16[32,1536]{1,0:T(8,128)(2,1)S(1)}, u32[]{:S(2)}, u32[]{:S(2)}) %collective-permute-start.9) | collective-permute-done | bytes 98336 | tf_op jit(solution)/shard_map/ppermute | solution.py:21
  43.6 1.7 %collective-permute-start.10 = (bf16[32,1536]{1,0:T(8,128)(2,1)S(1)}, bf16[32,1536]{1,0:T(8,128)(2,1)S(1)}, u32[]{:S(2)}, u32[]{:S(2)}) collective-permute-start(bf16[32,1536]{1,0:T(8,128)(2,1)S(1)} %add_convert_fusion), channel_id=1, source_target_pairs={{0,2},{2,0},{4,6},{6,4},{8,10},{10,8},{12,14},{14,12},{1,3},{3,1},... | collective-permute-start | bytes 294920 | tf_op jit(solution)/shard_map/ppermute | solution.py:21
  45.2 3.0 %collective-permute-done.10 = bf16[32,1536]{1,0:T(8,128)(2,1)S(1)} collective-permute-done((bf16[32,1536]{1,0:T(8,128)(2,1)S(1)}, bf16[32,1536]{1,0:T(8,128)(2,1)S(1)}, u32[]{:S(2)}, u32[]{:S(2)}) %collective-permute-start.10) | collective-permute-done | bytes 98336 | tf_op jit(solution)/shard_map/ppermute | solution.py:21
  48.3 0.1 convert_select_fusion.1
  48.4 0.8 %fusion = f32[1,64,1536]{2,1,0:T(8,128)} fusion(f32[64,1536]{1,0:T(8,128)S(1)} %copy-done.7, f32[32,1536]{1,0:T(8,128)S(1)} %convert_select_fusion, f32[32,1536]{1,0:T(8,128)S(1)} %get-tuple-element.29), kind=kLoop, calls=%fused_computation.1 | loop fusion | flops 196608 | bytes 1179648 | tf_op jit(solution)/shard_map/broadcast_in_dim | solution.py:310
  (24 shorter events, 0.5 us)
Async XLA Ops:
  1.9 12.6 %collective-permute-start.2 = (f32[64,1536]{1,0:T(8,128)S(1)}, f32[64,1536]{1,0:T(8,128)}, u32[]{:S(2)}, u32[]{:S(2)}) collective-permute-start(f32[64,1536]{1,0:T(8,128)S(1)} %shard_map.91.refs_0_), channel_id=1, source_target_pairs={{0,1},{1,0},{2,3},{3,2},{4,5},{5,4},{6,7},{7,6},{8,9},{9,8},{10,11... | collective-permute-start | bytes 1179656 | tf_op jit(solution)/shard_map/ppermute | solution.py:21
  4.9 0.8 %copy-start.6 = (f32[1,3,3072]{2,0,1:T(1,128)S(1)}, f32[1,3,3072]{2,0,1:T(1,128)}, u32[]{:S(2)}) copy-start(f32[1,3,3072]{2,0,1:T(1,128)} %param.13) | copy-start | bytes 110596
  5.7 0.6 %copy-start = (f32[3,1,1536]{2,1,0:T(1,128)}, f32[3,1,1536]{2,1,0:T(1,128)S(1)}, u32[]{:S(2)}) copy-start(f32[3,1,1536]{2,1,0:T(1,128)S(1)} %get-tuple-element.17.refs_1_.mine_ref.mine_mod_ref) | copy-start | bytes 55300
  6.3 1.2 %collective-permute-start = (f32[3,1,1536]{2,1,0:T(1,128)S(1)}, f32[3,1,1536]{2,1,0:T(1,128)S(1)}, u32[]{:S(2)}, u32[]{:S(2)}) collective-permute-start(f32[3,1,1536]{2,1,0:T(1,128)S(1)} %get-tuple-element.18), channel_id=1, source_target_pairs={{0,16},{16,0},{1,17},{17,1},{2,18},{18,2},{3,19},{19,3},{4,20},{20... | collective-permute-start | bytes 55304 | tf_op jit(solution)/shard_map/ppermute | solution.py:21
  7.4 0.6 %copy-start.3 = (f32[3,1,1536]{2,1,0:T(1,128)}, f32[3,1,1536]{2,1,0:T(1,128)S(1)}, u32[]{:S(2)}) copy-start(f32[3,1,1536]{2,1,0:T(1,128)S(1)} %collective-permute-done.refs_2_.other_ref.other_mod_ref) | copy-start | bytes 55300
  8.0 0.7 %copy-start.1 = (f32[3,1,1536]{2,1,0:T(1,128)S(1)}, f32[3,1,1536]{2,1,0:T(1,128)}, u32[]{:S(2)}) copy-start(f32[3,1,1536]{2,1,0:T(1,128)} %copy-done) | copy-start | bytes 55300
  8.8 0.7 %copy-start.4 = (f32[3,1,1536]{2,1,0:T(1,128)S(1)}, f32[3,1,1536]{2,1,0:T(1,128)}, u32[]{:S(2)}) copy-start(f32[3,1,1536]{2,1,0:T(1,128)} %copy-done.3) | copy-start | bytes 55300
  14.2 3.7 %collective-permute-start.1 = (f32[64,3072]{1,0:T(8,128)S(1)}, f32[64,3072]{1,0:T(8,128)S(1)}, u32[]{:S(2)}, u32[]{:S(2)}) collective-permute-start(f32[64,3072]{1,0:T(8,128)S(1)} %get-tuple-element.20), channel_id=1, source_target_pairs={{0,16},{16,0},{1,17},{17,1},{2,18},{18,2},{3,19},{19,3},{4,20},{20... | collective-permute-start | bytes 2359304 | tf_op jit(solution)/shard_map/ppermute | solution.py:21
  16.8 4.8 %copy-start.2 = (f32[3,1,1536]{2,1,0:T(1,128)S(1)}, f32[3,1,1536]{2,1,0:T(1,128)}, u32[]{:S(2)}) copy-start(f32[3,1,1536]{2,1,0:T(1,128)} %copy-done) | copy-start | bytes 55300
  16.9 4.8 %copy-start.5 = (f32[3,1,1536]{2,1,0:T(1,128)S(1)}, f32[3,1,1536]{2,1,0:T(1,128)}, u32[]{:S(2)}) copy-start(f32[3,1,1536]{2,1,0:T(1,128)} %copy-done.3) | copy-start | bytes 55300
  16.9 2.4 %collective-permute-start.3 = (f32[64,3072]{1,0:T(8,128)S(1)}, f32[64,3072]{1,0:T(8,128)S(1)}, u32[]{:S(2)}, u32[]{:S(2)}) collective-permute-start(f32[64,3072]{1,0:T(8,128)S(1)} %get-tuple-element.25), channel_id=1, source_target_pairs={{0,16},{16,0},{1,17},{17,1},{2,18},{18,2},{3,19},{19,3},{4,20},{20... | collective-permute-start | bytes 2359304 | tf_op jit(solution)/shard_map/ppermute | solution.py:21
  19.9 1.7 %collective-permute-start.4 = (bf16[128,1024]{1,0:T(8,128)(2,1)S(1)}, bf16[128,1024]{1,0:T(8,128)(2,1)}, u32[]{:S(2)}, u32[]{:S(2)}) collective-permute-start(bf16[128,1024]{1,0:T(8,128)(2,1)S(1)} %shard_map.95.mine_ref), channel_id=1, source_target_pairs={{0,16},{16,0},{1,17},{17,1},{2,18},{18,2},{3,19},{19,3},{4,20},{20... | collective-permute-start | bytes 786440 | tf_op jit(solution)/shard_map/ppermute | solution.py:21
  23.6 24.8 %copy-start.7 = (f32[64,1536]{1,0:T(8,128)S(1)}, f32[64,1536]{1,0:T(8,128)}, u32[]{:S(2)}) copy-start(f32[64,1536]{1,0:T(8,128)} %param.10) | copy-start | bytes 1179652
  23.6 6.1 %collective-permute-start.7 = (bf16[32,1536]{1,0:T(8,128)(2,1)S(1)}, bf16[32,1536]{1,0:T(8,128)(2,1)S(1)}, u32[]{:S(2)}, u32[]{:S(2)}) collective-permute-start(bf16[32,1536]{1,0:T(8,128)(2,1)S(1)} %get-tuple-element.34), channel_id=1, source_target_pairs={{0,3},{1,2},{2,1},{3,0},{4,7},{5,6},{6,5},{7,4},{8,11},{9,10},{10,... | collective-permute-start | bytes 294920 | tf_op jit(solution)/shard_map/ppermute | solution.py:21
  26.1 5.7 %collective-permute-start.6 = (bf16[32,1536]{1,0:T(8,128)(2,1)S(1)}, bf16[32,1536]{1,0:T(8,128)(2,1)S(1)}, u32[]{:S(2)}, u32[]{:S(2)}) collective-permute-start(bf16[32,1536]{1,0:T(8,128)(2,1)S(1)} %select_convert_fusion.1), channel_id=1, source_target_pairs={{0,2},{1,3},{2,0},{3,1},{4,6},{5,7},{6,4},{7,5},{8,10},{9,11},{10,... | collective-permute-start | bytes 294920 | tf_op jit(solution)/shard_map/ppermute | solution.py:21
  26.6 5.1 %collective-permute-start.5 = (bf16[32,1536]{1,0:T(8,128)(2,1)S(1)}, bf16[32,1536]{1,0:T(8,128)(2,1)S(1)}, u32[]{:S(2)}, u32[]{:S(2)}) collective-permute-start(bf16[32,1536]{1,0:T(8,128)(2,1)S(1)} %get-tuple-element.33), channel_id=1, source_target_pairs={{0,1},{1,0},{2,3},{3,2},{4,5},{5,4},{6,7},{7,6},{8,9},{9,8},{10,11... | collective-permute-start | bytes 294920 | tf_op jit(solution)/shard_map/ppermute | solution.py:21
  31.8 4.7 %collective-permute-start.8 = (bf16[32,1536]{1,0:T(8,128)(2,1)S(1)}, bf16[32,1536]{1,0:T(8,128)(2,1)S(1)}, u32[]{:S(2)}, u32[]{:S(2)}) collective-permute-start(bf16[32,1536]{1,0:T(8,128)(2,1)S(1)} %get-tuple-element.31), channel_id=1, source_target_pairs={{0,4},{2,6},{4,0},{6,2},{8,12},{10,14},{12,8},{14,10},{1,5},{3,7},... | collective-permute-start | bytes 294920 | tf_op jit(solution)/shard_map/ppermute | solution.py:21
  36.6 6.9 %collective-permute-start.9 = (bf16[32,1536]{1,0:T(8,128)(2,1)S(1)}, bf16[32,1536]{1,0:T(8,128)(2,1)S(1)}, u32[]{:S(2)}, u32[]{:S(2)}) collective-permute-start(bf16[32,1536]{1,0:T(8,128)(2,1)S(1)} %fusion.2), channel_id=1, source_target_pairs={{0,8},{2,10},{4,12},{6,14},{8,0},{10,2},{12,4},{14,6},{1,9},{3,11}... | collective-permute-start | bytes 294920 | tf_op jit(solution)/shard_map/ppermute | solution.py:21
  43.6 4.7 %collective-permute-start.10 = (bf16[32,1536]{1,0:T(8,128)(2,1)S(1)}, bf16[32,1536]{1,0:T(8,128)(2,1)S(1)}, u32[]{:S(2)}, u32[]{:S(2)}) collective-permute-start(bf16[32,1536]{1,0:T(8,128)(2,1)S(1)} %add_convert_fusion), channel_id=1, source_target_pairs={{0,2},{2,0},{4,6},{6,4},{8,10},{10,8},{12,14},{14,12},{1,3},{3,1},... | collective-permute-start | bytes 294920 | tf_op jit(solution)/shard_map/ppermute | solution.py:21

commit v3 on v2

v3 whole, which is shorter than its diff:
```python
import functools
import math

import jax
import jax.numpy as jnp
from jax import lax
from jax.experimental import pallas as pl
from jax.experimental.pallas import tpu as pltpu
from jax.sharding import PartitionSpec as P

HD = 128
NSTEPS = 50
F32 = jnp.float32
BF16 = jnp.bfloat16
VMEM = pl.BlockSpec(memory_space=pltpu.VMEM)
SMEM = pl.BlockSpec(memory_space=pltpu.SMEM)
ANY = pl.BlockSpec(memory_space=pl.ANY)
HBM = pl.BlockSpec(memory_space=pltpu.HBM)


def xor_permute(x, axes, mask):
    return lax.ppermute(x, axes, [(i, i ^ mask) for i in range(lax.axis_size(axes))])


def dot(a, b):
    return jnp.dot(a, b, preferred_element_type=F32)


def embed_half(step_ids, half_width, branch_index):
    frequency = jnp.exp(-math.log(10000.0) * jnp.arange(half_width, dtype=F32) / half_width)
    phases = step_ids.astype(F32)[:, None] * frequency[None, :]
    return jnp.where(branch_index == 0, jnp.sin(phases), jnp.cos(phases))


def in_vmem(*arrays):
    return [pltpu.with_memory_space_constraint(array, pltpu.VMEM) for array in arrays]


def in_hbm(*arrays):
    return [pltpu.with_memory_space_constraint(array, pltpu.HBM) for array in arrays]


def call(kernel, out_shape, in_specs, out_specs, scratch_shapes=()):
    return pl.pallas_call(
        kernel,
        out_shape=out_shape,
        in_specs=in_specs,
        out_specs=out_specs,
        scratch_shapes=scratch_shapes,
        compiler_params=pltpu.CompilerParams(vmem_limit_bytes=6 << 20),
    )


def norm_kernel(pieces, branch_ref, states_ref, *refs):
    out_refs, (tokens_ref, sems) = refs[:-2], refs[-2:]
    width = out_refs[0].shape[1]
    rows, model_width = tokens_ref.shape
    size = rows // pieces
    copies = []
    for piece in range(pieces):
        sl = slice(piece * size, (piece + 1) * size)
        copy = pltpu.make_async_copy(states_ref.at[sl], tokens_ref.at[sl], sems.at[piece])
        copy.start()
        copies.append(copy)
    for piece in range(pieces):
        sl = slice(piece * size, (piece + 1) * size)
        copies[piece].wait()
        tokens = tokens_ref[sl, :]
        mean = jnp.sum(tokens, axis=1, keepdims=True) * (1.0 / model_width)
        centered = tokens - mean
        variance = jnp.sum(centered * centered, axis=1, keepdims=True) * (1.0 / model_width)
        inverse = 1.0 / jnp.sqrt(variance + 1e-06)
        for index, out_ref in enumerate(out_refs):
            start = branch_ref[0] * (model_width // 2) + index * width
            columns = pl.ds(pl.multiple_of(start, HD), width)
            out_ref[sl, :] = (tokens_ref[sl, columns] - mean) * inverse


def normed_half(states, branch_index, cuts):
    rows, width = states.shape
    pieces = 1
    return call(
        functools.partial(norm_kernel, pieces),
        [pltpu.VMEM((rows, width // 2 // cuts), F32)] * cuts,
        [SMEM, HBM],
        [VMEM] * cuts,
        [pltpu.VMEM((rows, width), F32), pltpu.SemaphoreType.DMA((pieces,))],
    )(branch_index[None], *in_hbm(states))


def copy_kernel(source_ref, _, target_ref, sem):
    copy = pltpu.make_async_copy(source_ref, target_ref, sem)
    copy.start()
    copy.wait()


def into_vmem(array, after):
    return call(
        copy_kernel, pltpu.VMEM(array.shape, array.dtype), [HBM, ANY], VMEM, [pltpu.SemaphoreType.DMA]
    )(*in_hbm(array), after)


def modulate(tokens, factors):
    return jnp.concatenate(
        [
            (tokens * factors[i:i + 1] + factors[i + 1:i + 2]).astype(BF16)
            for i in (0, 2)
        ],
        axis=0,
    )


def first_kernel(cuts, branch_ref, step_ref, guidance_ref, *refs):
    tokens_refs, refs = refs[:cuts], refs[cuts:]
    mine_ref, other_ref, embedding_ref, *sources = refs[:6]
    factor_refs, refs = refs[6:6 + cuts], refs[6 + cuts:]
    mine_gate_ref, other_gate_ref, keep_ref, send_ref = refs[:4]
    targets, sems = refs[4:-1], refs[-1]
    width = tokens_refs[0].shape[1]
    copies = []
    for i, source in enumerate(sources):
        for cut in range(cuts):
            copies.append(
                pltpu.make_async_copy(
                    source.at[pl.ds(cut * width, width)], targets[i * cuts + cut], sems.at[i * cuts + cut]
                )
            )
    for copy in copies:
        copy.start()

    first = branch_ref[0] == 0
    step = 2.0 * (1.0 + step_ref[0].astype(F32)) / NSTEPS
    scale = 1.5 + 0.5 * guidance_ref[0].astype(F32)
    conditional, unconditional = step * scale, step * (1.0 - scale)
    base = branch_ref[0] * (width * cuts)
    half = pl.ds(pl.multiple_of(base, HD), width * cuts)
    mine_gate_ref[...] = jnp.where(first, conditional, unconditional) * (1.0 + mine_ref[2, :, half])
    other_gate_ref[...] = jnp.where(first, unconditional, conditional) * (1.0 + other_ref[2, :, half])
    modulated = []
    for cut in range(cuts):
        columns = pl.ds(pl.multiple_of(base + cut * width, HD), width)
        embedding = embedding_ref[:, cut * width:(cut + 1) * width]
        rows = []
        for mod_ref in (mine_ref, other_ref):
            rows += [1.0 + mod_ref[1, :, columns], mod_ref[0, :, columns] + embedding]
        for i, row in enumerate(rows):
            factor_refs[cut][i:i + 1, :] = row
        modulated.append(modulate(tokens_refs[cut][...], rows_of(rows)))
    kept = keep_ref.shape[0]
    for i in range(len(sources)):
        columns = sources[i].shape[1]
        chunk = min(columns, 512)
        for cut in range(cuts):
            copies[i * cuts + cut].wait()
        for start in range(0, columns, chunk):
            projected = sum(
                dot(modulated[cut], targets[i * cuts + cut][:, start:start + chunk]) for cut in range(cuts)
            )
            sl = slice(i * columns + start, i * columns + start + chunk)
            keep_ref[:, sl] = projected[:kept]
            send_ref[:, sl] = projected[kept:]


def rows_of(rows):
    return jnp.concatenate(rows, axis=0)


def project_first(scalars, tokens, mine, other, embedding, weights):
    cuts = len(tokens)
    rows, width = tokens[0].shape
    columns = weights[0].shape[1]
    out = pltpu.VMEM((rows, 3 * columns), F32)
    gate = pltpu.VMEM((1, width * cuts), F32)
    result = call(
        functools.partial(first_kernel, cuts),
        [pltpu.VMEM((4, width), F32)] * cuts
        + [gate, gate, out, out]
        + [pltpu.VMEM((width, columns), BF16)] * (3 * cuts),
        [SMEM] * 3 + [VMEM] * (cuts + 3) + [HBM] * 3,
        [VMEM] * (4 * cuts + 4),
        [pltpu.SemaphoreType.DMA((3 * cuts,))],
    )(*scalars, *tokens, mine, other, embedding, *in_hbm(*weights))
    factors, (mine_gate, other_gate, keep, send), held = result[:cuts], result[cuts:cuts + 4], result[cuts + 4:]
    return factors, mine_gate, other_gate, keep, send, [held[cut::cuts] for cut in range(cuts)]


def later_kernel(added, tokens_ref, factors_ref, wq_ref, wk_ref, wv_ref, *refs):
    refs = list(refs)
    before = [refs.pop(0) for _ in range(2 * added)]
    keep_ref, send_ref = refs
    kept = keep_ref.shape[0]
    modulated = modulate(tokens_ref[...], factors_ref[...])
    for i, weight_ref in enumerate((wq_ref, wk_ref, wv_ref)):
        columns = weight_ref.shape[1]
        chunk = min(columns, 512)
        for start in range(0, columns, chunk):
            projected = dot(modulated, weight_ref[:, start:start + chunk])
            sl = slice(i * columns + start, i * columns + start + chunk)
            keep, send = projected[:kept], projected[kept:]
            if added:
                keep, send = before[0][:, sl] + keep, before[1][:, sl] + send
            keep_ref[:, sl] = keep
            send_ref[:, sl] = send


def project_later(tokens, factors, weights, before=()):
    out = pltpu.VMEM((tokens.shape[0], 3 * weights[0].shape[1]), F32)
    return call(
        functools.partial(later_kernel, len(before) // 2),
        [out, out],
        [VMEM] * (5 + len(before)),
        [VMEM] * 2,
    )(tokens, *in_vmem(factors, *weights, *before))


def attention_kernel(outs, *refs):
    refs, out_refs = refs[:-outs], refs[-outs:]
    blocks = [(refs[i], refs[i + 1]) for i in range(0, len(refs), 2)]
    width = out_refs[0].shape[1]
    columns = width * outs

    def part(which, head):
        sl = slice(which * columns + head * HD, which * columns + (head + 1) * HD)
        return jnp.concatenate(
            [(mine[:, sl] + other[:, sl]).astype(BF16) for mine, other in blocks], axis=0
        )

    heads = columns // HD
    all_scores = [
        lax.dot_general(
            part(0, head), part(1, head), (((1,), (1,)), ((), ())), preferred_element_type=F32
        )
        for head in range(heads)
    ]
    all_probs = []
    for scores in all_scores:
        scores = scores * (1.0 / math.sqrt(HD))
        scores = jnp.exp(scores - jnp.max(scores, axis=1, keepdims=True))
        all_probs.append((scores / jnp.sum(scores, axis=1, keepdims=True)).astype(BF16))
    for head, probs in enumerate(all_probs):
        out, start = divmod(head * HD, width)
        out_refs[out][:, start:start + HD] = dot(probs, part(2, head)).astype(BF16)


def attention(blocks, outs):
    flat = [array for block in blocks for array in block]
    rows, columns = flat[0].shape
    return call(
        functools.partial(attention_kernel, outs),
        [pltpu.VMEM((rows * len(blocks), columns // 3 // outs), BF16)] * outs,
        [VMEM] * len(flat),
        [VMEM] * outs,
    )(*in_vmem(*flat))


def project_kernel(cuts, added, *refs):
    attended_refs, (w_ref, gate_ref, *refs) = refs[:cuts], refs[cuts:]
    out_refs = refs[added:]
    rows, columns = out_refs[0].shape
    chunk = 512 if columns % 512 == 0 else HD
    attended = jnp.concatenate([ref[...] for ref in attended_refs], axis=1)
    for start in range(0, columns, chunk):
        sl = slice(start, start + chunk)
        increment = gate_ref[:, sl] * dot(attended, w_ref[:, sl]).astype(BF16).astype(F32)
        if added:
            increment = refs[0][:, sl] + increment
        for block, out_ref in enumerate(out_refs):
            out_ref[:, sl] = increment[block * rows:(block + 1) * rows]


def project(attended, w_out, gate, before=(), blocks=1):
    return call(
        functools.partial(project_kernel, len(attended), len(before)),
        [pltpu.VMEM((attended[0].shape[0] // blocks, w_out.shape[1]), F32)] * blocks,
        [VMEM] * (2 + len(attended) + len(before)),
        [VMEM] * blocks,
    )(*attended, w_out, *in_vmem(gate, *before))


def scan_general(parts):
    total = parts[0]
    for mask in range(1, len(parts)):
        total = total + xor_permute(parts[mask].astype(BF16), "tok", mask).astype(F32)
    position = lax.axis_index("tm")
    result, group = total, total
    mask = 1
    while mask < lax.axis_size("tm"):
        received = xor_permute(group.astype(BF16), "tm", mask).astype(F32)
        result = result + jnp.where(position & mask != 0, received, 0.0)
        group = group + received
        mask *= 2
    return result


def scan_planes(parts):
    axes = ("tm", "tok")
    position = lax.axis_index("tm")
    odd = position & 1 == 1
    rows = parts[0].shape[0] // 2

    def near(x):
        return jnp.where(odd, x[rows:], x[:rows])

    def far(x):
        return jnp.where(odd, x[:rows], x[rows:])

    diagonal = xor_permute(far(parts[1]).astype(BF16), axes, 3)
    across = xor_permute(near(parts[1]).astype(BF16), axes, 1)
    beside = xor_permute(far(parts[0]).astype(BF16), axes, 2)
    own_time = near(parts[0]) + across.astype(F32)
    pair_time = beside.astype(F32) + diagonal.astype(F32)
    group = own_time + pair_time
    earlier = jnp.zeros_like(group)
    mask = 2
    while mask < lax.axis_size("tm"):
        received = xor_permute(group.astype(BF16), "tm", mask).astype(F32)
        earlier = earlier + jnp.where(position & mask != 0, received, 0.0)
        group = group + received
        mask *= 2
    own = earlier + own_time + jnp.where(odd, pair_time, 0.0)
    for_pair = earlier + pair_time + jnp.where(odd, 0.0, own_time)
    returned = xor_permute(for_pair.astype(BF16), "tm", 1).astype(F32)
    return jnp.concatenate([jnp.where(odd, returned, own), jnp.where(odd, own, returned)], axis=0)


def body(
    states, start_state, timesteps, guidance_index, modulation, w_query, w_key, w_value, w_out
):
    tok_count = lax.axis_size("tok")
    branch_index = lax.axis_index("branch")
    rows, model_width = states.shape[1:]
    half_width = model_width // 2
    cuts = 2
    normed = normed_half(states[0], branch_index, cuts)
    modulation = into_vmem(jnp.transpose(modulation, (1, 0, 2)), normed[0])
    tokens = [
        [xor_permute(piece, "tok", mask) for piece in normed] for mask in range(1, tok_count)
    ]
    other_modulation = xor_permute(modulation, "branch", 1)
    embedding = embed_half(timesteps, half_width, branch_index)

    factors, mine_gate, other_gate, keep, send, weights = project_first(
        (branch_index[None], timesteps, guidance_index),
        normed, modulation, other_modulation, embedding, (w_query, w_key, w_value)
    )
    blocks = [(keep, xor_permute(send, "branch", 1))]
    for block in tokens:
        before = ()
        for cut in range(cuts):
            before = project_later(block[cut], factors[cut], weights[cut], before)
        keep, send = before
        blocks.append((keep, xor_permute(send, "branch", 1)))
    attended = attention(blocks, min(2, w_query.shape[1] // HD))
    attended_other = [xor_permute(array, "branch", 1) for array in attended]
    increments = project(attended, w_out, mine_gate)
    parts = project(attended_other, w_out, other_gate, increments, tok_count)
    pairs = tok_count == 2 and lax.axis_size("tm") % 2 == 0 and rows % 32 == 0
    scan = scan_planes if pairs else scan_general
    return (start_state + scan(parts))[None]


def solution(mesh):
    in_specs = (
        P("tm", "tok", None),
        P("tok", "branch"),
        P("tm"),
        P(),
        P("branch", None, None),
        P("branch", "tok"),
        P("branch", "tok"),
        P("branch", "tok"),
        P("tok", "branch"),
    )
    out_specs = P("tm", "tok", "branch")
    return jax.shard_map(body, mesh=mesh, in_specs=in_specs, out_specs=out_specs, check_vma=False)
```

time: 49.6 us -> 47 us (0.948)
  local copies, waits for them, and re-layouts: 3.52 us -> 0.61 us
  waiting for transfers between devices: 17.6 us -> 19.7 us
  starting transfers between devices: 13.6 us -> 12.6 us
  Pallas kernels: 11.6 us -> 11 us
    unnamed x16 -> x4, local copies, waits for them, and re-layouts: 3.43 us -> 0.61 us
    ppermute x11 -> x13, waiting for transfers between devices: 17.6 us -> 19.7 us  [xor_permute(): lax.ppermute(x, axes, [(i, i ^ mask) for i in range(lax.axis_size(axes))])]
    ppermute x11 -> x13, starting transfers between devices: 13.6 us -> 12.6 us  [xor_permute(): lax.ppermute(x, axes, [(i, i ^ mask) for i in range(lax.axis_size(axes))])]
    pallas_call x6 -> x8, Pallas kernels: 11.6 us -> 11 us  [the longest x1 4.4 us: project_first(): call(functools.partial(first_kernel, cuts), [pltpu.VMEM((4, width), F32)]...]
  transfers between devices with their start and end apart: 11 -> 13, of which waited for: 9 -> 8; matrix products, arithmetic and copies ran while one was open for 1% -> 0% of each run, Pallas kernels for 14% -> 16%
where the time goes in v3:
time: 47 us; the launch traced here: 46.7 us
  waiting for transfers between devices  19.7 us (42%)
  starting transfers between devices  12.6 us (27%)
  Pallas kernels  11 us (23%)
  between operations  1.47 us (3%)
  other arithmetic  1.34 us (3%)
  local copies, waits for them, and re-layouts  0.61 us (1%)
    ppermute x13, waiting for transfers between devices, xor_permute(): lax.ppermute(x, axes, [(i, i ^ mask) for i in range(lax.axis_size(axes))])  19.7 us
    ppermute x13, starting transfers between devices, xor_permute(): lax.ppermute(x, axes, [(i, i ^ mask) for i in range(lax.axis_size(axes))])  12.6 us
    pallas_call x1, Pallas kernels, project_first(): call(functools.partial(first_kernel, cuts), [pltpu.VMEM((4, width), F32)]...  4.4 us
    pallas_call x2, Pallas kernels, project(): call(functools.partial(project_kernel, len(attended), len(before)), [pltp...  2.07 us
    pallas_call x2, Pallas kernels, project_later(): call(functools.partial(later_kernel, len(before) // 2), [out, out], [VMEM...  1.58 us
    pallas_call x1, Pallas kernels, normed_half(): call(functools.partial(norm_kernel, pieces), [pltpu.VMEM((rows, width //...  1.43 us
  transfers between devices with their start and end apart: 13, of which 8 were waited for; matrix products, arithmetic and copies ran while one was open for 0% of the time, Pallas kernels for 16%

profile of v3, /device:TPU:0, one launch (start us, length us, event | category | flops | bytes accessed | tf_op | source)
XLA Modules:
  0.0 46.7 jit_solution(14350550478501132328)
XLA Ops:
  0.0 1.4 %shard_map.91 = (f32[64,768]{1,0:T(8,128)S(1)}, f32[64,768]{1,0:T(8,128)S(1)}) custom-call(s32[1]{0:T(128)} %bitcast.branch_ref, f32[64,3072]{1,0:T(8,128)} %bitcast.6), custom_call_target="tpu_custom_call" | custom-call | tf_op jit(solution)/shard_map/pallas_call | solution.py:82
  1.4 3.0 %collective-permute-start.3 = (f32[64,768]{1,0:T(8,128)S(1)}, f32[64,768]{1,0:T(8,128)S(1)}, u32[]{:S(2)}, u32[]{:S(2)}) collective-permute-start(f32[64,768]{1,0:T(8,128)S(1)} %get-tuple-element.27._.refs_0_), channel_id=1, source_target_pairs={{0,1},{1,0},{2,3},{3,2},{4,5},{5,4},{6,7},{7,6},{8,9},{9,8},{10,11... | collective-permute-start | bytes 589832 | tf_op jit(solution)/shard_map/ppermute | solution.py:22
  4.4 0.8 %shard_map.92.refs_2_ = f32[3,1,3072]{2,1,0:T(1,128)S(1)} custom-call(f32[3,1,3072]{2,1,0:T(1,128)} %bitcast.7, f32[64,768]{1,0:T(8,128)S(1)} %get-tuple-element.27._.refs_0_), custom_call_target="tpu_custom_call" | custom-call | tf_op jit(solution)/shard_map/pallas_call | solution.py:98
  5.3 0.1 collective-permute-start.2
  6.0 0.2 broadcast_select_fusion.refs_4_
  6.9 4.4 %shard_map.93 = (f32[4,768]{1,0:T(4,128)S(1)}, f32[4,768]{1,0:T(4,128)S(1)}, f32[1,1536]{1,0:T(1,128)S(1)}, f32[1,1536]{1,0:T(1,128)S(1)}, f32[64,3072]{1,0:T(8,...) custom-call(s32[1]{0:T(128)} %bitcast.branch_ref, ...), custom_call_target="tpu_custom_call" | custom-call | tf_op jit(solution)/shard_map/pallas_call | solution.py:174
  11.3 0.5 %collective-permute-start.1 = (f32[64,3072]{1,0:T(8,128)S(1)}, f32[64,3072]{1,0:T(8,128)S(1)}, u32[]{:S(2)}, u32[]{:S(2)}) collective-permute-start(f32[64,3072]{1,0:T(8,128)S(1)} %get-tuple-element.30), channel_id=1, source_target_pairs={{0,16},{16,0},{1,17},{17,1},{2,18},{18,2},{3,19},{19,3},{4,20},{20... | collective-permute-start | bytes 2359304 | tf_op jit(solution)/shard_map/ppermute | solution.py:22
  11.8 0.8 %shard_map.94 = (f32[64,3072]{1,0:T(8,128)S(1)}, f32[64,3072]{1,0:T(8,128)S(1)}) custom-call(f32[64,768]{1,0:T(8,128)S(1)} %collective-permute-done.3.tokens_ref, f32[4,768]{1,0:T(4,128)S(1)} %get-tuple-element.35.factors_ref, bf16[768,1024]{1,0:T(8,128)(2,1)S(1)} %get-tuple-element.36.wq_ref, bf16[768,1024]{1,0:T(8,128)(2,1)S(1)} %get-tuple-element.37.wk_ref, ...), custom_call_target="tpu_custom_call" | custom-call | tf_op jit(solution)/shard_map/pallas_call | solution.py:208
  12.6 0.9 %collective-permute-done.2.tokens_ref = f32[64,768]{1,0:T(8,128)S(1)} collective-permute-done((f32[64,768]{1,0:T(8,128)S(1)}, f32[64,768]{1,0:T(8,128)S(1)}, u32[]{:S(2)}, u32[]{:S(2)}) %collective-permute-start.2) | collective-permute-done | bytes 196640 | tf_op jit(solution)/shard_map/ppermute | solution.py:22
  13.6 0.8 %shard_map.95 = (f32[64,3072]{1,0:T(8,128)S(1)}, f32[64,3072]{1,0:T(8,128)S(1)}) custom-call(f32[64,768]{1,0:T(8,128)S(1)} %collective-permute-done.2.tokens_ref, f32[4,768]{1,0:T(4,128)S(1)} %get-tuple-element.31.factors_ref, bf16[768,1024]{1,0:T(8,128)(2,1)S(1)} %get-tuple-element.32.wq_ref, bf16[768,1024]{1,0:T(8,128)(2,1)S(1)} %get-tuple-element.33.wk_ref, ...), custom_call_target="tpu_custom_call" | custom-call | tf_op jit(solution)/shard_map/pallas_call | solution.py:208
  14.4 2.3 %collective-permute-done.4.refs_3_ = f32[64,3072]{1,0:T(8,128)S(1)} collective-permute-done((f32[64,3072]{1,0:T(8,128)S(1)}, f32[64,3072]{1,0:T(8,128)S(1)}, u32[]{:S(2)}, u32[]{:S(2)}) %collective-permute-start.4) | collective-permute-done | bytes 786464 | tf_op jit(solution)/shard_map/ppermute | solution.py:22
  16.7 0.7 %shard_map.96 = (bf16[128,512]{1,0:T(8,128)(2,1)S(1)}, bf16[128,512]{1,0:T(8,128)(2,1)S(1)}) custom-call(f32[64,3072]{1,0:T(8,128)S(1)} %get-tuple-element.29.refs_0_, f32[64,3072]{1,0:T(8,128)S(1)} %collective-permute-done.1.refs_1_, f32[64,3072]{1,0:T(8,128)S(1)} %get-tuple-element.41.refs_2_, f32[64,3072]{1,0:T(8,128)S(1)} %collective-permute-done.4.refs_3_), custom_call_target="tpu_custom_call" | custom-call | tf_op jit(solution)/shard_map/pallas_call | solution.py:248
  17.4 0.2 collective-permute-start.5
  17.6 0.4 collective-permute-start.6
  18.0 0.6 %copy-done = bf16[1024,1536]{1,0:T(8,128)(2,1)S(1)} copy-done((bf16[1024,1536]{1,0:T(8,128)(2,1)S(1)}, bf16[1024,1536]{1,0:T(8,128)(2,1)}, u32[]{:S(2)}) %copy-start) | copy-done | bytes 3145752
  18.6 0.6 %shard_map.97.refs_4_ = f32[128,1536]{1,0:T(8,128)S(1)} custom-call(bf16[128,512]{1,0:T(8,128)(2,1)S(1)} %get-tuple-element.43.refs_0_, bf16[128,512]{1,0:T(8,128)(2,1)S(1)} %get-tuple-element.44.refs_1_, bf16[1024,1536]{1,0:T(8,128)(2,1)S(1)} %copy-done, f32[1,1536]{1,0:T(1,128)S(1)} %get-tuple-element.46.refs_3_), custom_call_target="tpu_custom_call" | custom-call | tf_op jit(solution)/shard_map/pallas_call | solution.py:272
  19.2 1.5 %shard_map.98 = (f32[64,1536]{1,0:T(8,128)S(1)}, f32[64,1536]{1,0:T(8,128)S(1)}) custom-call(bf16[128,512]{1,0:T(8,128)(2,1)S(1)} %collective-permute-done.5.refs_0_, bf16[128,512]{1,0:T(8,128)(2,1)} %collective-permute-done.6.refs_1_, bf16[1024,1536]{1,0:T(8,128)(2,1)S(1)} %copy-done, f32[1,1536]{1,0:T(1,128)S(1)} %get-tuple-element.45.refs_3_, ...), custom_call_target="tpu_custom_call" | custom-call | tf_op jit(solution)/shard_map/pallas_call | solution.py:272
  20.7 1.8 %collective-permute-start.7 = (bf16[32,1536]{1,0:T(8,128)(2,1)S(1)}, bf16[32,1536]{1,0:T(8,128)(2,1)S(1)}, u32[]{:S(2)}, u32[]{:S(2)}) collective-permute-start(bf16[32,1536]{1,0:T(8,128)(2,1)S(1)} %get-tuple-element.53), channel_id=1, source_target_pairs={{0,1},{1,0},{2,3},{3,2},{4,5},{5,4},{6,7},{7,6},{8,9},{9,8},{10,11... | collective-permute-start | bytes 294920 | tf_op jit(solution)/shard_map/ppermute | solution.py:22
  22.5 1.5 %collective-permute-start.9 = (bf16[32,1536]{1,0:T(8,128)(2,1)S(1)}, bf16[32,1536]{1,0:T(8,128)(2,1)S(1)}, u32[]{:S(2)}, u32[]{:S(2)}) collective-permute-start(bf16[32,1536]{1,0:T(8,128)(2,1)S(1)} %get-tuple-element.54), channel_id=1, source_target_pairs={{0,3},{1,2},{2,1},{3,0},{4,7},{5,6},{6,5},{7,4},{8,11},{9,10},{10,... | collective-permute-start | bytes 294920 | tf_op jit(solution)/shard_map/ppermute | solution.py:22
  24.1 0.3 collective-permute-start.8
  24.4 1.4 %collective-permute-done.7 = bf16[32,1536]{1,0:T(8,128)(2,1)S(1)} collective-permute-done((bf16[32,1536]{1,0:T(8,128)(2,1)S(1)}, bf16[32,1536]{1,0:T(8,128)(2,1)S(1)}, u32[]{:S(2)}, u32[]{:S(2)}) %collective-permute-start.7) | collective-permute-done | bytes 98336 | tf_op jit(solution)/shard_map/ppermute | solution.py:22
  25.8 3.4 %collective-permute-done.9 = bf16[32,1536]{1,0:T(8,128)(2,1)S(1)} collective-permute-done((bf16[32,1536]{1,0:T(8,128)(2,1)S(1)}, bf16[32,1536]{1,0:T(8,128)(2,1)S(1)}, u32[]{:S(2)}, u32[]{:S(2)}) %collective-permute-start.9) | collective-permute-done | bytes 98336 | tf_op jit(solution)/shard_map/ppermute | solution.py:22
  29.2 1.4 %collective-permute-done.8 = bf16[32,1536]{1,0:T(8,128)(2,1)S(1)} collective-permute-done((bf16[32,1536]{1,0:T(8,128)(2,1)S(1)}, bf16[32,1536]{1,0:T(8,128)(2,1)S(1)}, u32[]{:S(2)}, u32[]{:S(2)}) %collective-permute-start.8) | collective-permute-done | bytes 98336 | tf_op jit(solution)/shard_map/ppermute | solution.py:22
  30.7 1.6 %collective-permute-start.10 = (bf16[32,1536]{1,0:T(8,128)(2,1)S(1)}, bf16[32,1536]{1,0:T(8,128)(2,1)S(1)}, u32[]{:S(2)}, u32[]{:S(2)}) collective-permute-start(bf16[32,1536]{1,0:T(8,128)(2,1)S(1)} %get-tuple-element.51), channel_id=1, source_target_pairs={{0,4},{2,6},{4,0},{6,2},{8,12},{10,14},{12,8},{14,10},{1,5},{3,7},... | collective-permute-start | bytes 294920 | tf_op jit(solution)/shard_map/ppermute | solution.py:22
  32.3 3.1 %collective-permute-done.10 = bf16[32,1536]{1,0:T(8,128)(2,1)S(1)} collective-permute-done((bf16[32,1536]{1,0:T(8,128)(2,1)S(1)}, bf16[32,1536]{1,0:T(8,128)(2,1)S(1)}, u32[]{:S(2)}, u32[]{:S(2)}) %collective-permute-start.10) | collective-permute-done | bytes 98336 | tf_op jit(solution)/shard_map/ppermute | solution.py:22
  35.4 2.7 %collective-permute-start.11 = (bf16[32,1536]{1,0:T(8,128)(2,1)S(1)}, bf16[32,1536]{1,0:T(8,128)(2,1)S(1)}, u32[]{:S(2)}, u32[]{:S(2)}) collective-permute-start(bf16[32,1536]{1,0:T(8,128)(2,1)S(1)} %fusion.2), channel_id=1, source_target_pairs={{0,8},{2,10},{4,12},{6,14},{8,0},{10,2},{12,4},{14,6},{1,9},{3,11}... | collective-permute-start | bytes 294920 | tf_op jit(solution)/shard_map/ppermute | solution.py:22
  38.0 2.9 %collective-permute-done.11 = bf16[32,1536]{1,0:T(8,128)(2,1)S(1)} collective-permute-done((bf16[32,1536]{1,0:T(8,128)(2,1)S(1)}, bf16[32,1536]{1,0:T(8,128)(2,1)S(1)}, u32[]{:S(2)}, u32[]{:S(2)}) %collective-permute-start.11) | collective-permute-done | bytes 98336 | tf_op jit(solution)/shard_map/ppermute | solution.py:22
  41.0 0.1 add_convert_fusion
  41.1 0.4 collective-permute-start.12
  41.5 4.2 %collective-permute-done.12 = bf16[32,1536]{1,0:T(8,128)(2,1)S(1)} collective-permute-done((bf16[32,1536]{1,0:T(8,128)(2,1)S(1)}, bf16[32,1536]{1,0:T(8,128)(2,1)S(1)}, u32[]{:S(2)}, u32[]{:S(2)}) %collective-permute-start.12) | collective-permute-done | bytes 98336 | tf_op jit(solution)/shard_map/ppermute | solution.py:22
  45.7 0.1 convert_select_fusion.1
  45.9 0.8 %fusion = f32[1,64,1536]{2,1,0:T(8,128)} fusion(f32[64,1536]{1,0:T(8,128)S(1)} %copy-done.1, f32[32,1536]{1,0:T(8,128)S(1)} %convert_select_fusion, f32[32,1536]{1,0:T(8,128)S(1)} %get-tuple-element.49), kind=kLoop, calls=%fused_computation.1 | loop fusion | flops 196608 | bytes 1179648 | tf_op jit(solution)/shard_map/broadcast_in_dim | solution.py:359
  (15 shorter events, 0.3 us)
Async XLA Ops:
  1.4 10.4 %collective-permute-start.3 = (f32[64,768]{1,0:T(8,128)S(1)}, f32[64,768]{1,0:T(8,128)S(1)}, u32[]{:S(2)}, u32[]{:S(2)}) collective-permute-start(f32[64,768]{1,0:T(8,128)S(1)} %get-tuple-element.27._.refs_0_), channel_id=1, source_target_pairs={{0,1},{1,0},{2,3},{3,2},{4,5},{5,4},{6,7},{7,6},{8,9},{9,8},{10,11... | collective-permute-start | bytes 589832 | tf_op jit(solution)/shard_map/ppermute | solution.py:22
  5.2 1.7 %collective-permute-start = (f32[3,1,3072]{2,1,0:T(1,128)S(1)}, f32[3,1,3072]{2,1,0:T(1,128)S(1)}, u32[]{:S(2)}, u32[]{:S(2)}) collective-permute-start(f32[3,1,3072]{2,1,0:T(1,128)S(1)} %shard_map.92.refs_2_), channel_id=1, source_target_pairs={{0,16},{16,0},{1,17},{17,1},{2,18},{18,2},{3,19},{19,3},{4,20},{20... | collective-permute-start | bytes 110600 | tf_op jit(solution)/shard_map/ppermute | solution.py:22
  5.3 8.3 %collective-permute-start.2 = (f32[64,768]{1,0:T(8,128)S(1)}, f32[64,768]{1,0:T(8,128)S(1)}, u32[]{:S(2)}, u32[]{:S(2)}) collective-permute-start(f32[64,768]{1,0:T(8,128)S(1)} %get-tuple-element.28.refs_1_), channel_id=1, source_target_pairs={{0,1},{1,0},{2,3},{3,2},{4,5},{5,4},{6,7},{7,6},{8,9},{9,8},{10,11... | collective-permute-start | bytes 589832 | tf_op jit(solution)/shard_map/ppermute | solution.py:22
  11.3 3.1 %collective-permute-start.1 = (f32[64,3072]{1,0:T(8,128)S(1)}, f32[64,3072]{1,0:T(8,128)S(1)}, u32[]{:S(2)}, u32[]{:S(2)}) collective-permute-start(f32[64,3072]{1,0:T(8,128)S(1)} %get-tuple-element.30), channel_id=1, source_target_pairs={{0,16},{16,0},{1,17},{17,1},{2,18},{18,2},{3,19},{19,3},{4,20},{20... | collective-permute-start | bytes 2359304 | tf_op jit(solution)/shard_map/ppermute | solution.py:22
  14.3 2.4 %collective-permute-start.4 = (f32[64,3072]{1,0:T(8,128)S(1)}, f32[64,3072]{1,0:T(8,128)S(1)}, u32[]{:S(2)}, u32[]{:S(2)}) collective-permute-start(f32[64,3072]{1,0:T(8,128)S(1)} %get-tuple-element.42), channel_id=1, source_target_pairs={{0,16},{16,0},{1,17},{17,1},{2,18},{18,2},{3,19},{19,3},{4,20},{20... | collective-permute-start | bytes 2359304 | tf_op jit(solution)/shard_map/ppermute | solution.py:22
  16.7 1.9 %copy-start = (bf16[1024,1536]{1,0:T(8,128)(2,1)S(1)}, bf16[1024,1536]{1,0:T(8,128)(2,1)}, u32[]{:S(2)}) copy-start(bf16[1024,1536]{1,0:T(8,128)(2,1)} %refs_2_.3) | copy-start | bytes 9437188
  17.4 1.8 %collective-permute-start.5 = (bf16[128,512]{1,0:T(8,128)(2,1)S(1)}, bf16[128,512]{1,0:T(8,128)(2,1)S(1)}, u32[]{:S(2)}, u32[]{:S(2)}) collective-permute-start(bf16[128,512]{1,0:T(8,128)(2,1)S(1)} %get-tuple-element.43.refs_0_), channel_id=1, source_target_pairs={{0,16},{16,0},{1,17},{17,1},{2,18},{18,2},{3,19},{19,3},{4,20},{20... | collective-permute-start | bytes 393224 | tf_op jit(solution)/shard_map/ppermute | solution.py:22
  17.6 1.6 %collective-permute-start.6 = (bf16[128,512]{1,0:T(8,128)(2,1)S(1)}, bf16[128,512]{1,0:T(8,128)(2,1)}, u32[]{:S(2)}, u32[]{:S(2)}) collective-permute-start(bf16[128,512]{1,0:T(8,128)(2,1)S(1)} %get-tuple-element.44.refs_1_), channel_id=1, source_target_pairs={{0,16},{16,0},{1,17},{17,1},{2,18},{18,2},{3,19},{19,3},{4,20},{20... | collective-permute-start | bytes 393224 | tf_op jit(solution)/shard_map/ppermute | solution.py:22
  20.7 5.0 %collective-permute-start.7 = (bf16[32,1536]{1,0:T(8,128)(2,1)S(1)}, bf16[32,1536]{1,0:T(8,128)(2,1)S(1)}, u32[]{:S(2)}, u32[]{:S(2)}) collective-permute-start(bf16[32,1536]{1,0:T(8,128)(2,1)S(1)} %get-tuple-element.53), channel_id=1, source_target_pairs={{0,1},{1,0},{2,3},{3,2},{4,5},{5,4},{6,7},{7,6},{8,9},{9,8},{10,11... | collective-permute-start | bytes 294920 | tf_op jit(solution)/shard_map/ppermute | solution.py:22
  22.5 6.6 %collective-permute-start.9 = (bf16[32,1536]{1,0:T(8,128)(2,1)S(1)}, bf16[32,1536]{1,0:T(8,128)(2,1)S(1)}, u32[]{:S(2)}, u32[]{:S(2)}) collective-permute-start(bf16[32,1536]{1,0:T(8,128)(2,1)S(1)} %get-tuple-element.54), channel_id=1, source_target_pairs={{0,3},{1,2},{2,1},{3,0},{4,7},{5,6},{6,5},{7,4},{8,11},{9,10},{10,... | collective-permute-start | bytes 294920 | tf_op jit(solution)/shard_map/ppermute | solution.py:22
  24.1 6.5 %collective-permute-start.8 = (bf16[32,1536]{1,0:T(8,128)(2,1)S(1)}, bf16[32,1536]{1,0:T(8,128)(2,1)S(1)}, u32[]{:S(2)}, u32[]{:S(2)}) collective-permute-start(bf16[32,1536]{1,0:T(8,128)(2,1)S(1)} %select_convert_fusion.1), channel_id=1, source_target_pairs={{0,2},{1,3},{2,0},{3,1},{4,6},{5,7},{6,4},{7,5},{8,10},{9,11},{10,... | collective-permute-start | bytes 294920 | tf_op jit(solution)/shard_map/ppermute | solution.py:22
  30.6 15.2 %copy-start.1 = (f32[64,1536]{1,0:T(8,128)S(1)}, f32[64,1536]{1,0:T(8,128)}, u32[]{:S(2)}) copy-start(f32[64,1536]{1,0:T(8,128)} %param.10) | copy-start | bytes 1179652
  30.7 4.7 %collective-permute-start.10 = (bf16[32,1536]{1,0:T(8,128)(2,1)S(1)}, bf16[32,1536]{1,0:T(8,128)(2,1)S(1)}, u32[]{:S(2)}, u32[]{:S(2)}) collective-permute-start(bf16[32,1536]{1,0:T(8,128)(2,1)S(1)} %get-tuple-element.51), channel_id=1, source_target_pairs={{0,4},{2,6},{4,0},{6,2},{8,12},{10,14},{12,8},{14,10},{1,5},{3,7},... | collective-permute-start | bytes 294920 | tf_op jit(solution)/shard_map/ppermute | solution.py:22
  35.4 5.6 %collective-permute-start.11 = (bf16[32,1536]{1,0:T(8,128)(2,1)S(1)}, bf16[32,1536]{1,0:T(8,128)(2,1)S(1)}, u32[]{:S(2)}, u32[]{:S(2)}) collective-permute-start(bf16[32,1536]{1,0:T(8,128)(2,1)S(1)} %fusion.2), channel_id=1, source_target_pairs={{0,8},{2,10},{4,12},{6,14},{8,0},{10,2},{12,4},{14,6},{1,9},{3,11}... | collective-permute-start | bytes 294920 | tf_op jit(solution)/shard_map/ppermute | solution.py:22
  41.1 4.7 %collective-permute-start.12 = (bf16[32,1536]{1,0:T(8,128)(2,1)S(1)}, bf16[32,1536]{1,0:T(8,128)(2,1)S(1)}, u32[]{:S(2)}, u32[]{:S(2)}) collective-permute-start(bf16[32,1536]{1,0:T(8,128)(2,1)S(1)} %add_convert_fusion), channel_id=1, source_target_pairs={{0,2},{2,0},{4,6},{6,4},{8,10},{10,8},{12,14},{14,12},{1,3},{3,1},... | collective-permute-start | bytes 294920 | tf_op jit(solution)/shard_map/ppermute | solution.py:22

commit v4 on v3

--- a/solution.py
+++ b/solution.py
@@ -40,13 +40,14 @@
     return [pltpu.with_memory_space_constraint(array, pltpu.HBM) for array in arrays]
 
 
-def call(kernel, out_shape, in_specs, out_specs, scratch_shapes=()):
+def call(kernel, out_shape, in_specs, out_specs, scratch_shapes=(), flops=0, moved=0):
     return pl.pallas_call(
         kernel,
         out_shape=out_shape,
         in_specs=in_specs,
         out_specs=out_specs,
         scratch_shapes=scratch_shapes,
+        cost_estimate=pl.CostEstimate(flops=flops, bytes_accessed=moved, transcendentals=0),
         compiler_params=pltpu.CompilerParams(vmem_limit_bytes=6 << 20),
     )
 
@@ -85,6 +86,7 @@
         [SMEM, HBM],
         [VMEM] * cuts,
         [pltpu.VMEM((rows, width), F32), pltpu.SemaphoreType.DMA((pieces,))],
+        moved=4 * rows * width,
     )(branch_index[None], *in_hbm(states))
 
 
@@ -96,7 +98,8 @@
 
 def into_vmem(array, after):
     return call(
-        copy_kernel, pltpu.VMEM(array.shape, array.dtype), [HBM, ANY], VMEM, [pltpu.SemaphoreType.DMA]
+        copy_kernel, pltpu.VMEM(array.shape, array.dtype), [HBM, ANY], VMEM, [pltpu.SemaphoreType.DMA],
+        moved=4 * array.size,
     )(*in_hbm(array), after)
 
 
@@ -110,12 +113,12 @@
     )
 
 
-def first_kernel(cuts, branch_ref, step_ref, guidance_ref, *refs):
+def first_kernel(cuts, groups, branch_ref, step_ref, guidance_ref, *refs):
     tokens_refs, refs = refs[:cuts], refs[cuts:]
-    mine_ref, other_ref, embedding_ref, *sources = refs[:6]
-    factor_refs, refs = refs[6:6 + cuts], refs[6 + cuts:]
-    mine_gate_ref, other_gate_ref, keep_ref, send_ref = refs[:4]
-    targets, sems = refs[4:-1], refs[-1]
+    mine_ref, other_ref, embedding_ref, *sources, out_source = refs[:7]
+    factor_refs, refs = refs[7:7 + cuts], refs[7 + cuts:]
+    mine_gate_ref, other_gate_ref, keep_ref = refs[:3]
+    send_refs, targets, (out_target, sems) = refs[3:3 + groups], refs[3 + groups:-2], refs[-2:]
     width = tokens_refs[0].shape[1]
     copies = []
     for i, source in enumerate(sources):
@@ -125,6 +128,8 @@
                     source.at[pl.ds(cut * width, width)], targets[i * cuts + cut], sems.at[i * cuts + cut]
                 )
             )
+    held_rows = out_source.at[pl.ds(0, out_target.shape[0])]
+    copies.append(pltpu.make_async_copy(held_rows, out_target, sems.at[len(copies)]))
     for copy in copies:
         copy.start()
 
@@ -148,82 +153,91 @@
         modulated.append(modulate(tokens_refs[cut][...], rows_of(rows)))
     kept = keep_ref.shape[0]
     for i in range(len(sources)):
-        columns = sources[i].shape[1]
-        chunk = min(columns, 512)
+        chunk = sources[i].shape[1] // groups
         for cut in range(cuts):
             copies[i * cuts + cut].wait()
-        for start in range(0, columns, chunk):
+        for group in range(groups):
+            columns = slice(group * chunk, (group + 1) * chunk)
             projected = sum(
-                dot(modulated[cut], targets[i * cuts + cut][:, start:start + chunk]) for cut in range(cuts)
+                dot(modulated[cut], targets[i * cuts + cut][:, columns]) for cut in range(cuts)
             )
-            sl = slice(i * columns + start, i * columns + start + chunk)
-            keep_ref[:, sl] = projected[:kept]
-            send_ref[:, sl] = projected[kept:]
+            here = (group * 3 + i) * chunk
+            keep_ref[:, here:here + chunk] = projected[:kept]
+            send_refs[group][:, i * chunk:(i + 1) * chunk] = projected[kept:]
+    copies[-1].wait()
 
 
 def rows_of(rows):
     return jnp.concatenate(rows, axis=0)
 
 
-def project_first(scalars, tokens, mine, other, embedding, weights):
+def project_first(scalars, tokens, mine, other, embedding, weights, w_out, groups):
     cuts = len(tokens)
     rows, width = tokens[0].shape
     columns = weights[0].shape[1]
-    out = pltpu.VMEM((rows, 3 * columns), F32)
+    keep = pltpu.VMEM((rows, 3 * columns), F32)
+    send = pltpu.VMEM((rows, 3 * columns // groups), F32)
     gate = pltpu.VMEM((1, width * cuts), F32)
     result = call(
-        functools.partial(first_kernel, cuts),
+        functools.partial(first_kernel, cuts, groups),
         [pltpu.VMEM((4, width), F32)] * cuts
-        + [gate, gate, out, out]
-        + [pltpu.VMEM((width, columns), BF16)] * (3 * cuts),
-        [SMEM] * 3 + [VMEM] * (cuts + 3) + [HBM] * 3,
-        [VMEM] * (4 * cuts + 4),
-        [pltpu.SemaphoreType.DMA((3 * cuts,))],
-    )(*scalars, *tokens, mine, other, embedding, *in_hbm(*weights))
-    factors, (mine_gate, other_gate, keep, send), held = result[:cuts], result[cuts:cuts + 4], result[cuts + 4:]
-    return factors, mine_gate, other_gate, keep, send, [held[cut::cuts] for cut in range(cuts)]
-
-
-def later_kernel(added, tokens_ref, factors_ref, wq_ref, wk_ref, wv_ref, *refs):
-    refs = list(refs)
-    before = [refs.pop(0) for _ in range(2 * added)]
-    keep_ref, send_ref = refs
+        + [gate, gate, keep]
+        + [send] * groups
+        + [pltpu.VMEM((width, columns), BF16)] * (3 * cuts)
+        + [pltpu.VMEM((w_out.shape[0] - w_out.shape[0] // 4, w_out.shape[1]), BF16)],
+        [SMEM] * 3 + [VMEM] * (cuts + 3) + [HBM] * 4,
+        [VMEM] * (4 * cuts + 4 + groups),
+        [pltpu.SemaphoreType.DMA((3 * cuts + 1,))],
+        flops=12 * rows * width * cuts * columns,
+        moved=6 * width * cuts * columns,
+    )(*scalars, *tokens, mine, other, embedding, *in_hbm(*weights, w_out))
+    factors, (mine_gate, other_gate, keep), result = result[:cuts], result[cuts:cuts + 3], result[cuts + 3:]
+    sends, held, out_held = result[:groups], result[groups:-1], result[-1]
+    return factors, mine_gate, other_gate, keep, sends, [held[cut::cuts] for cut in range(cuts)], out_held
+
+
+def later_kernel(added, groups, wanted, tokens_ref, factors_ref, wq_ref, wk_ref, wv_ref, *refs):
+    before, (keep_ref, send_ref) = refs[:added], refs[added:]
     kept = keep_ref.shape[0]
     modulated = modulate(tokens_ref[...], factors_ref[...])
-    for i, weight_ref in enumerate((wq_ref, wk_ref, wv_ref)):
-        columns = weight_ref.shape[1]
-        chunk = min(columns, 512)
-        for start in range(0, columns, chunk):
-            projected = dot(modulated, weight_ref[:, start:start + chunk])
-            sl = slice(i * columns + start, i * columns + start + chunk)
+    for place, group in enumerate(wanted):
+        for i, weight_ref in enumerate((wq_ref, wk_ref, wv_ref)):
+            chunk = weight_ref.shape[1] // groups
+            projected = dot(modulated, weight_ref[:, group * chunk:(group + 1) * chunk])
             keep, send = projected[:kept], projected[kept:]
-            if added:
+            if before:
+                sl = slice((group * 3 + i) * chunk, (group * 3 + i + 1) * chunk)
                 keep, send = before[0][:, sl] + keep, before[1][:, sl] + send
+            sl = slice((place * 3 + i) * chunk, (place * 3 + i + 1) * chunk)
             keep_ref[:, sl] = keep
             send_ref[:, sl] = send
 
 
-def project_later(tokens, factors, weights, before=()):
-    out = pltpu.VMEM((tokens.shape[0], 3 * weights[0].shape[1]), F32)
-    return call(
-        functools.partial(later_kernel, len(before) // 2),
+def project_later(tokens, factors, weights, groups, wanted, before=()):
+    columns = 3 * weights[0].shape[1] // groups * len(wanted)
+    out = pltpu.VMEM((tokens.shape[0], columns), F32)
+    return call(
+        functools.partial(later_kernel, len(before), groups, wanted),
         [out, out],
         [VMEM] * (5 + len(before)),
         [VMEM] * 2,
+        flops=4 * tokens.size * columns,
+        moved=2 * tokens.shape[1] * columns,
     )(tokens, *in_vmem(factors, *weights, *before))
 
 
-def attention_kernel(outs, *refs):
-    refs, out_refs = refs[:-outs], refs[-outs:]
-    blocks = [(refs[i], refs[i + 1]) for i in range(0, len(refs), 2)]
-    width = out_refs[0].shape[1]
-    columns = width * outs
+def attention_kernel(starts, *refs):
+    refs, out_ref = refs[:-1], refs[-1]
+    blocks = [(refs[2 * i], refs[2 * i + 1], start) for i, start in enumerate(starts)]
+    columns = out_ref.shape[1]
 
     def part(which, head):
-        sl = slice(which * columns + head * HD, which * columns + (head + 1) * HD)
-        return jnp.concatenate(
-            [(mine[:, sl] + other[:, sl]).astype(BF16) for mine, other in blocks], axis=0
-        )
+        pieces = []
+        for mine, other, start in blocks:
+            here = which * columns + head * HD
+            there = here + start
+            pieces.append((mine[:, there:there + HD] + other[:, here:here + HD]).astype(BF16))
+        return jnp.concatenate(pieces, axis=0)
 
     heads = columns // HD
     all_scores = [
@@ -238,43 +252,81 @@
         scores = jnp.exp(scores - jnp.max(scores, axis=1, keepdims=True))
         all_probs.append((scores / jnp.sum(scores, axis=1, keepdims=True)).astype(BF16))
     for head, probs in enumerate(all_probs):
-        out, start = divmod(head * HD, width)
-        out_refs[out][:, start:start + HD] = dot(probs, part(2, head)).astype(BF16)
-
-
-def attention(blocks, outs):
-    flat = [array for block in blocks for array in block]
-    rows, columns = flat[0].shape
-    return call(
-        functools.partial(attention_kernel, outs),
-        [pltpu.VMEM((rows * len(blocks), columns // 3 // outs), BF16)] * outs,
+        out_ref[:, head * HD:(head + 1) * HD] = dot(probs, part(2, head)).astype(BF16)
+
+
+def attention(blocks, columns):
+    flat = [array for block in blocks for array in block[:2]]
+    rows = flat[0].shape[0]
+    return call(
+        functools.partial(attention_kernel, [block[2] for block in blocks]),
+        pltpu.VMEM((rows * len(blocks), columns), BF16),
         [VMEM] * len(flat),
-        [VMEM] * outs,
+        VMEM,
+        flops=4 * (rows * len(blocks)) ** 2 * columns,
+        moved=12 * rows * len(blocks) * columns,
     )(*in_vmem(*flat))
 
 
-def project_kernel(cuts, added, *refs):
-    attended_refs, (w_ref, gate_ref, *refs) = refs[:cuts], refs[cuts:]
-    out_refs = refs[added:]
+def project_mine_kernel(cuts, *refs):
+    attended_refs, (gate_ref, held_ref, source_ref, out_ref, rest_ref, sems) = refs[:cuts], refs[cuts:]
+    held_rows, columns = held_ref.shape
+    copies = []
+    size = rest_ref.shape[0] // sems.shape[0]
+    for index in range(sems.shape[0]):
+        sl = pl.ds(index * size, size)
+        there = pl.ds(held_rows + index * size, size)
+        copies.append(pltpu.make_async_copy(source_ref.at[there], rest_ref.at[sl], sems.at[index]))
+        copies[-1].start()
+    chunk = math.gcd(columns, 512)
+    attended = jnp.concatenate([ref[...] for ref in attended_refs], axis=1)
+    slices = [slice(start, start + chunk) for start in range(0, columns, chunk)]
+    partials = [dot(attended[:, :held_rows], held_ref[:, sl]) for sl in slices]
+    for copy in copies:
+        copy.wait()
+    for partial, sl in zip(partials, slices):
+        partial = partial + dot(attended[:, held_rows:], rest_ref[:, sl])
+        out_ref[:, sl] = gate_ref[:, sl] * partial.astype(BF16).astype(F32)
+
+
+def project_mine(attended, held, w_out, gate):
+    lat, columns = attended[0].shape[0], w_out.shape[1]
+    rest = w_out.shape[0] - held.shape[0]
+    return call(
+        functools.partial(project_mine_kernel, len(attended)),
+        [pltpu.VMEM((lat, columns), F32), pltpu.VMEM((rest, columns), BF16)],
+        [VMEM] * (2 + len(attended)) + [HBM],
+        [VMEM] * 2,
+        [pltpu.SemaphoreType.DMA((2,))],
+        flops=2 * lat * w_out.size,
+        moved=2 * w_out.size,
+    )(*attended, *in_vmem(gate, held), *in_hbm(w_out))
+
+
+def project_other_kernel(cuts, *refs):
+    attended_refs, (held_ref, rest_ref, gate_ref, before_ref, *out_refs) = refs[:cuts], refs[cuts:]
+    held_rows = held_ref.shape[0]
     rows, columns = out_refs[0].shape
-    chunk = 512 if columns % 512 == 0 else HD
+    chunk = math.gcd(columns, 512)
     attended = jnp.concatenate([ref[...] for ref in attended_refs], axis=1)
     for start in range(0, columns, chunk):
         sl = slice(start, start + chunk)
-        increment = gate_ref[:, sl] * dot(attended, w_ref[:, sl]).astype(BF16).astype(F32)
-        if added:
-            increment = refs[0][:, sl] + increment
+        partial = dot(attended[:, :held_rows], held_ref[:, sl]) + dot(attended[:, held_rows:], rest_ref[:, sl])
+        increment = before_ref[:, sl] + gate_ref[:, sl] * partial.astype(BF16).astype(F32)
         for block, out_ref in enumerate(out_refs):
             out_ref[:, sl] = increment[block * rows:(block + 1) * rows]
 
 
-def project(attended, w_out, gate, before=(), blocks=1):
-    return call(
-        functools.partial(project_kernel, len(attended), len(before)),
-        [pltpu.VMEM((attended[0].shape[0] // blocks, w_out.shape[1]), F32)] * blocks,
-        [VMEM] * (2 + len(attended) + len(before)),
+def project_other(attended, held, rest, gate, before, blocks):
+    lat, columns = before.shape
+    return call(
+        functools.partial(project_other_kernel, len(attended)),
+        [pltpu.VMEM((lat // blocks, columns), F32)] * blocks,
+        [VMEM] * (4 + len(attended)),
         [VMEM] * blocks,
-    )(*attended, w_out, *in_vmem(gate, *before))
+        flops=4 * lat * held.size,
+        moved=4 * held.size,
+    )(*attended, *in_vmem(held, rest, gate, before))
 
 
 def scan_general(parts):
@@ -339,21 +391,27 @@
     other_modulation = xor_permute(modulation, "branch", 1)
     embedding = embed_half(timesteps, half_width, branch_index)
 
-    factors, mine_gate, other_gate, keep, send, weights = project_first(
+    columns = w_query.shape[1]
+    groups = 2 if columns % (2 * HD) == 0 else 1
+    factors, mine_gate, other_gate, keep, sends, weights, out_held = project_first(
         (branch_index[None], timesteps, guidance_index),
-        normed, modulation, other_modulation, embedding, (w_query, w_key, w_value)
+        normed, modulation, other_modulation, embedding, (w_query, w_key, w_value), w_out, groups
     )
-    blocks = [(keep, xor_permute(send, "branch", 1))]
+    blocks = [
+        [(keep, xor_permute(send, "branch", 1), 3 * columns // groups * group)]
+        for group, send in enumerate(sends)
+    ]
     for block in tokens:
         before = ()
-        for cut in range(cuts):
-            before = project_later(block[cut], factors[cut], weights[cut], before)
-        keep, send = before
-        blocks.append((keep, xor_permute(send, "branch", 1)))
-    attended = attention(blocks, min(2, w_query.shape[1] // HD))
+        for cut in range(cuts - 1):
+            before = project_later(block[cut], factors[cut], weights[cut], groups, range(groups), before)
+        for group in range(groups):
+            keep, send = project_later(block[-1], factors[-1], weights[-1], groups, [group], before)
+            blocks[group].append((keep, xor_permute(send, "branch", 1), 0))
+    attended = [attention(blocks[group], columns // groups) for group in range(groups)]
     attended_other = [xor_permute(array, "branch", 1) for array in attended]
-    increments = project(attended, w_out, mine_gate)
-    parts = project(attended_other, w_out, other_gate, increments, tok_count)
+    increments, out_rest = project_mine(attended, out_held, w_out, mine_gate)
+    parts = project_other(attended_other, out_held, out_rest, other_gate, increments, tok_count)
     pairs = tok_count == 2 and lax.axis_size("tm") % 2 == 0 and rows % 32 == 0
     scan = scan_planes if pairs else scan_general
     return (start_state + scan(parts))[None]

time: 47 us -> 44.5 us (0.947)
  waiting for transfers between devices: 19.7 us -> 14.9 us
  starting transfers between devices: 12.6 us -> 14.7 us
  Pallas kernels: 11 us -> 11.9 us
  local copies, waits for them, and re-layouts: 0.61 us -> 0.01 us
    ppermute x13 -> x15, waiting for transfers between devices: 19.7 us -> 14.9 us  [xor_permute(): lax.ppermute(x, axes, [(i, i ^ mask) for i in range(lax.axis_size(axes))])]
    ppermute x13 -> x15, starting transfers between devices: 12.6 us -> 14.7 us  [xor_permute(): lax.ppermute(x, axes, [(i, i ^ mask) for i in range(lax.axis_size(axes))])]
    pallas_call x6 -> x8, Pallas kernels: 8.75 us -> 9.66 us  [the longest x1 4.53 us: project_first(): call(functools.partial(first_kernel, cuts, groups), [pltpu.VMEM((4, width...]
    unnamed x4 -> x2, local copies, waits for them, and re-layouts: 0.61 us -> 0.01 us
  transfers between devices with their start and end apart: 13 -> 15, of which waited for: 8 -> 7; matrix products, arithmetic and copies ran while one was open for 0% -> 1% of each run, Pallas kernels for 16% -> 22%
where the time goes in v4:
time: 44.5 us; the launch traced here: 44.2 us
  waiting for transfers between devices  14.9 us (33%)
  starting transfers between devices  14.7 us (33%)
  Pallas kernels  11.9 us (27%)
  between operations  1.48 us (3%)
  other arithmetic  1.34 us (3%)
    ppermute x15, waiting for transfers between devices, xor_permute(): lax.ppermute(x, axes, [(i, i ^ mask) for i in range(lax.axis_size(axes))])  14.9 us
    ppermute x15, starting transfers between devices, xor_permute(): lax.ppermute(x, axes, [(i, i ^ mask) for i in range(lax.axis_size(axes))])  14.7 us
    pallas_call x1, Pallas kernels, project_first(): call(functools.partial(first_kernel, cuts, groups), [pltpu.VMEM((4, width...  4.53 us
    pallas_call x3, Pallas kernels, project_later(): call(functools.partial(later_kernel, len(before), groups, wanted), [out,...  1.78 us
    pallas_call x1, Pallas kernels, project_mine(): call(functools.partial(project_mine_kernel, len(attended)), [pltpu.VMEM((...  1.72 us
    pallas_call x1, Pallas kernels, normed_half(): call(functools.partial(norm_kernel, pieces), [pltpu.VMEM((rows, width //...  1.43 us
    pallas_call x2, Pallas kernels, attention(): call(functools.partial(attention_kernel, [block[2] for block in blocks]),...  1.05 us
  transfers between devices with their start and end apart: 15, of which 7 were waited for; matrix products, arithmetic and copies ran while one was open for 1% of the time, Pallas kernels for 22%

profile of v4, /device:TPU:0, one launch (start us, length us, event | category | flops | bytes accessed | tf_op | source)
XLA Modules:
  0.0 44.2 jit_solution(15312618634674935205)
XLA Ops:
  0.0 1.4 %shard_map.91 = (f32[64,768]{1,0:T(8,128)S(1)}, f32[64,768]{1,0:T(8,128)S(1)}) custom-call(s32[1]{0:T(128)} %bitcast.branch_ref, f32[64,3072]{1,0:T(8,128)} %bitcast.6), custom_call_target="tpu_custom_call" | custom-call | bytes 786432 | tf_op jit(solution)/shard_map/pallas_call | solution.py:83
  1.4 3.0 %collective-permute-start.3 = (f32[64,768]{1,0:T(8,128)S(1)}, f32[64,768]{1,0:T(8,128)S(1)}, u32[]{:S(2)}, u32[]{:S(2)}) collective-permute-start(f32[64,768]{1,0:T(8,128)S(1)} %get-tuple-element.31._.refs_0_), channel_id=1, source_target_pairs={{0,1},{1,0},{2,3},{3,2},{4,5},{5,4},{6,7},{7,6},{8,9},{9,8},{10,11... | collective-permute-start | bytes 589832 | tf_op jit(solution)/shard_map/ppermute | solution.py:22
  4.4 0.8 %shard_map.92.refs_2_ = f32[3,1,3072]{2,1,0:T(1,128)S(1)} custom-call(f32[3,1,3072]{2,1,0:T(1,128)} %bitcast.7, f32[64,768]{1,0:T(8,128)S(1)} %get-tuple-element.31._.refs_0_), custom_call_target="tpu_custom_call" | custom-call | bytes 36864 | tf_op jit(solution)/shard_map/pallas_call | solution.py:100
  6.0 0.2 broadcast_select_fusion.refs_4_
  6.9 4.5 %shard_map.93 = (f32[4,768]{1,0:T(4,128)S(1)}, f32[4,768]{1,0:T(4,128)S(1)}, f32[1,1536]{1,0:T(1,128)S(1)}, f32[1,1536]{1,0:T(1,128)S(1)}, f32[64,3072]{1,0:T(8,...) custom-call(s32[1]{0:T(128)} %bitcast.branch_ref, ...), custom_call_target="tpu_custom_call" | custom-call | flops 1207959552 | bytes 9437184 | tf_op jit(solution)/shard_map/pallas_call | solution.py:181
  11.4 0.5 %collective-permute-start.6 = (f32[64,1536]{1,0:T(8,128)S(1)}, f32[64,1536]{1,0:T(8,128)S(1)}, u32[]{:S(2)}, u32[]{:S(2)}) collective-permute-start(f32[64,1536]{1,0:T(8,128)S(1)} %get-tuple-element.47), channel_id=1, source_target_pairs={{0,16},{16,0},{1,17},{17,1},{2,18},{18,2},{3,19},{19,3},{4,20},{20... | collective-permute-start | bytes 1179656 | tf_op jit(solution)/shard_map/ppermute | solution.py:22
  11.9 0.1 collective-permute-start.1
  12.0 0.8 %shard_map.94 = (f32[64,3072]{1,0:T(8,128)S(1)}, f32[64,3072]{1,0:T(8,128)S(1)}) custom-call(f32[64,768]{1,0:T(8,128)S(1)} %collective-permute-done.3.tokens_ref, f32[4,768]{1,0:T(4,128)S(1)} %get-tuple-element.39.factors_ref, bf16[768,1024]{1,0:T(8,128)(2,1)S(1)} %get-tuple-element.40.wq_ref, bf16[768,1024]{1,0:T(8,128)(2,1)S(1)} %get-tuple-element.41.wk_ref, ...), custom_call_target="tpu_custom_call" | custom-call | flops 603979776 | bytes 4718592 | tf_op jit(solution)/shard_map/pallas_call | solution.py:219
  12.8 0.7 %collective-permute-done.2.tokens_ref = f32[64,768]{1,0:T(8,128)S(1)} collective-permute-done((f32[64,768]{1,0:T(8,128)S(1)}, f32[64,768]{1,0:T(8,128)S(1)}, u32[]{:S(2)}, u32[]{:S(2)}) %collective-permute-start.2) | collective-permute-done | bytes 196640 | tf_op jit(solution)/shard_map/ppermute | solution.py:22
  13.6 0.5 %shard_map.97 = (f32[64,1536]{1,0:T(8,128)S(1)}, f32[64,1536]{1,0:T(8,128)S(1)}) custom-call(f32[64,768]{1,0:T(8,128)S(1)} %collective-permute-done.2.tokens_ref, f32[4,768]{1,0:T(4,128)S(1)} %get-tuple-element.35.factors_ref, bf16[768,1024]{1,0:T(8,128)(2,1)S(1)} %get-tuple-element.36.wq_ref, bf16[768,1024]{1,0:T(8,128)(2,1)S(1)} %get-tuple-element.37.wk_ref, ...), custom_call_target="tpu_custom_call" | custom-call | flops 301989888 | bytes 2359296 | tf_op jit(solution)/shard_map/pallas_call | solution.py:219
  14.1 0.5 %shard_map.95 = (f32[64,1536]{1,0:T(8,128)S(1)}, f32[64,1536]{1,0:T(8,128)S(1)}) custom-call(f32[64,768]{1,0:T(8,128)S(1)} %collective-permute-done.2.tokens_ref, f32[4,768]{1,0:T(4,128)S(1)} %get-tuple-element.35.factors_ref, bf16[768,1024]{1,0:T(8,128)(2,1)S(1)} %get-tuple-element.36.wq_ref, bf16[768,1024]{1,0:T(8,128)(2,1)S(1)} %get-tuple-element.37.wk_ref, ...), custom_call_target="tpu_custom_call" | custom-call | flops 301989888 | bytes 2359296 | tf_op jit(solution)/shard_map/pallas_call | solution.py:219
  14.6 0.6 %collective-permute-start.4 = (f32[64,1536]{1,0:T(8,128)S(1)}, f32[64,1536]{1,0:T(8,128)S(1)}, u32[]{:S(2)}, u32[]{:S(2)}) collective-permute-start(f32[64,1536]{1,0:T(8,128)S(1)} %get-tuple-element.46), channel_id=1, source_target_pairs={{0,16},{16,0},{1,17},{17,1},{2,18},{18,2},{3,19},{19,3},{4,20},{20... | collective-permute-start | bytes 1179656 | tf_op jit(solution)/shard_map/ppermute | solution.py:22
  15.2 0.7 %collective-permute-done.7.refs_3_ = f32[64,1536]{1,0:T(8,128)S(1)} collective-permute-done((f32[64,1536]{1,0:T(8,128)S(1)}, f32[64,1536]{1,0:T(8,128)S(1)}, u32[]{:S(2)}, u32[]{:S(2)}) %collective-permute-start.7) | collective-permute-done | bytes 393248 | tf_op jit(solution)/shard_map/ppermute | solution.py:22
  15.8 0.5 %shard_map.98.refs_1_ = bf16[128,512]{1,0:T(8,128)(2,1)S(1)} custom-call(f32[64,3072]{1,0:T(8,128)S(1)} %get-tuple-element.33.refs_0_, f32[64,1536]{1,0:T(8,128)S(1)} %collective-permute-done.6.refs_1_, f32[64,1536]{1,0:T(8,128)S(1)} %get-tuple-element.48.refs_2_, f32[64,1536]{1,0:T(8,128)S(1)} %collective-permute-done.7.refs_3_), custom_call_target="tpu_custom_call" | custom-call | flops 33554432 | bytes 786432 | tf_op jit(solution)/shard_map/pallas_call | solution.py:261
  16.4 0.2 collective-permute-start.8
  16.6 0.5 %shard_map.96.refs_0_ = bf16[128,512]{1,0:T(8,128)(2,1)S(1)} custom-call(f32[64,3072]{1,0:T(8,128)S(1)} %get-tuple-element.33.refs_0_, f32[64,1536]{1,0:T(8,128)S(1)} %collective-permute-done.1.refs_1_, f32[64,1536]{1,0:T(8,128)S(1)} %get-tuple-element.45.refs_2_, f32[64,1536]{1,0:T(8,128)S(1)} %collective-permute-done.4.refs_3_), custom_call_target="tpu_custom_call" | custom-call | flops 33554432 | bytes 786432 | tf_op jit(solution)/shard_map/pallas_call | solution.py:261
  17.1 0.4 collective-permute-start.5
  17.6 1.7 %shard_map.99 = (f32[128,1536]{1,0:T(8,128)S(1)}, bf16[256,1536]{1,0:T(8,128)(2,1)S(1)}) custom-call(bf16[128,512]{1,0:T(8,128)(2,1)S(1)} %shard_map.96.refs_0_, bf16[128,512]{1,0:T(8,128)(2,1)S(1)} %shard_map.98.refs_1_, f32[1,1536]{1,0:T(1,128)S(1)} %get-tuple-element.51.refs_2_, bf16[768,1536]{1,0:T(8,128)(2,1)S(1)} %get-tuple-element.50.refs_3_.refs_2_, ...), custom_call_target="tpu_custom_call" | custom-call | flops 402653184 | bytes 3145728 | tf_op jit(solution)/shard_map/pallas_call | solution.py:295
  19.3 0.6 %shard_map.100 = (f32[64,1536]{1,0:T(8,128)S(1)}, f32[64,1536]{1,0:T(8,128)S(1)}) custom-call(bf16[128,512]{1,0:T(8,128)(2,1)S(1)} %collective-permute-done.5.refs_0_, bf16[128,512]{1,0:T(8,128)(2,1)S(1)} %collective-permute-done.8.refs_1_, bf16[768,1536]{1,0:T(8,128)(2,1)S(1)} %get-tuple-element.50.refs_3_.refs_2_, ...), custom_call_target="tpu_custom_call" | custom-call | flops 603979776 | bytes 4718592 | tf_op jit(solution)/shard_map/pallas_call | solution.py:322
  19.9 2.7 %collective-permute-start.11 = (bf16[32,1536]{1,0:T(8,128)(2,1)S(1)}, bf16[32,1536]{1,0:T(8,128)(2,1)S(1)}, u32[]{:S(2)}, u32[]{:S(2)}) collective-permute-start(bf16[32,1536]{1,0:T(8,128)(2,1)S(1)} %get-tuple-element.62), channel_id=1, source_target_pairs={{0,3},{1,2},{2,1},{3,0},{4,7},{5,6},{6,5},{7,4},{8,11},{9,10},{10,... | collective-permute-start | bytes 294920 | tf_op jit(solution)/shard_map/ppermute | solution.py:22
  22.7 0.5 %collective-permute-start.9 = (bf16[32,1536]{1,0:T(8,128)(2,1)S(1)}, bf16[32,1536]{1,0:T(8,128)(2,1)S(1)}, u32[]{:S(2)}, u32[]{:S(2)}) collective-permute-start(bf16[32,1536]{1,0:T(8,128)(2,1)S(1)} %get-tuple-element.61), channel_id=1, source_target_pairs={{0,1},{1,0},{2,3},{3,2},{4,5},{5,4},{6,7},{7,6},{8,9},{9,8},{10,11... | collective-permute-start | bytes 294920 | tf_op jit(solution)/shard_map/ppermute | solution.py:22
  23.2 0.3 collective-permute-start.10
  23.6 2.9 %collective-permute-done.11 = bf16[32,1536]{1,0:T(8,128)(2,1)S(1)} collective-permute-done((bf16[32,1536]{1,0:T(8,128)(2,1)S(1)}, bf16[32,1536]{1,0:T(8,128)(2,1)S(1)}, u32[]{:S(2)}, u32[]{:S(2)}) %collective-permute-start.11) | collective-permute-done | bytes 98336 | tf_op jit(solution)/shard_map/ppermute | solution.py:22
  26.5 1.6 %collective-permute-done.9 = bf16[32,1536]{1,0:T(8,128)(2,1)S(1)} collective-permute-done((bf16[32,1536]{1,0:T(8,128)(2,1)S(1)}, bf16[32,1536]{1,0:T(8,128)(2,1)S(1)}, u32[]{:S(2)}, u32[]{:S(2)}) %collective-permute-start.9) | collective-permute-done | bytes 98336 | tf_op jit(solution)/shard_map/ppermute | solution.py:22
  28.2 1.7 %collective-permute-start.12 = (bf16[32,1536]{1,0:T(8,128)(2,1)S(1)}, bf16[32,1536]{1,0:T(8,128)(2,1)S(1)}, u32[]{:S(2)}, u32[]{:S(2)}) collective-permute-start(bf16[32,1536]{1,0:T(8,128)(2,1)S(1)} %get-tuple-element.59), channel_id=1, source_target_pairs={{0,4},{2,6},{4,0},{6,2},{8,12},{10,14},{12,8},{14,10},{1,5},{3,7},... | collective-permute-start | bytes 294920 | tf_op jit(solution)/shard_map/ppermute | solution.py:22
  29.9 2.9 %collective-permute-done.12 = bf16[32,1536]{1,0:T(8,128)(2,1)S(1)} collective-permute-done((bf16[32,1536]{1,0:T(8,128)(2,1)S(1)}, bf16[32,1536]{1,0:T(8,128)(2,1)S(1)}, u32[]{:S(2)}, u32[]{:S(2)}) %collective-permute-start.12) | collective-permute-done | bytes 98336 | tf_op jit(solution)/shard_map/ppermute | solution.py:22
  32.9 2.8 %collective-permute-start.13 = (bf16[32,1536]{1,0:T(8,128)(2,1)S(1)}, bf16[32,1536]{1,0:T(8,128)(2,1)S(1)}, u32[]{:S(2)}, u32[]{:S(2)}) collective-permute-start(bf16[32,1536]{1,0:T(8,128)(2,1)S(1)} %fusion.2), channel_id=1, source_target_pairs={{0,8},{2,10},{4,12},{6,14},{8,0},{10,2},{12,4},{14,6},{1,9},{3,11}... | collective-permute-start | bytes 294920 | tf_op jit(solution)/shard_map/ppermute | solution.py:22
  35.7 2.8 %collective-permute-done.13 = bf16[32,1536]{1,0:T(8,128)(2,1)S(1)} collective-permute-done((bf16[32,1536]{1,0:T(8,128)(2,1)S(1)}, bf16[32,1536]{1,0:T(8,128)(2,1)S(1)}, u32[]{:S(2)}, u32[]{:S(2)}) %collective-permute-start.13) | collective-permute-done | bytes 98336 | tf_op jit(solution)/shard_map/ppermute | solution.py:22
  38.6 1.5 %collective-permute-start.14 = (bf16[32,1536]{1,0:T(8,128)(2,1)S(1)}, bf16[32,1536]{1,0:T(8,128)(2,1)S(1)}, u32[]{:S(2)}, u32[]{:S(2)}) collective-permute-start(bf16[32,1536]{1,0:T(8,128)(2,1)S(1)} %add_convert_fusion), channel_id=1, source_target_pairs={{0,2},{2,0},{4,6},{6,4},{8,10},{10,8},{12,14},{14,12},{1,3},{3,1},... | collective-permute-start | bytes 294920 | tf_op jit(solution)/shard_map/ppermute | solution.py:22
  40.1 3.1 %collective-permute-done.14 = bf16[32,1536]{1,0:T(8,128)(2,1)S(1)} collective-permute-done((bf16[32,1536]{1,0:T(8,128)(2,1)S(1)}, bf16[32,1536]{1,0:T(8,128)(2,1)S(1)}, u32[]{:S(2)}, u32[]{:S(2)}) %collective-permute-start.14) | collective-permute-done | bytes 98336 | tf_op jit(solution)/shard_map/ppermute | solution.py:22
  43.3 0.1 convert_select_fusion.1
  43.4 0.8 %fusion = f32[1,64,1536]{2,1,0:T(8,128)} fusion(f32[64,1536]{1,0:T(8,128)S(1)} %copy-done, f32[32,1536]{1,0:T(8,128)S(1)} %convert_select_fusion, f32[32,1536]{1,0:T(8,128)S(1)} %get-tuple-element.57), kind=kLoop, calls=%fused_computation.1 | loop fusion | flops 196608 | bytes 1179648 | tf_op jit(solution)/shard_map/broadcast_in_dim | solution.py:417
  (19 shorter events, 0.5 us)
Async XLA Ops:
  1.4 10.6 %collective-permute-start.3 = (f32[64,768]{1,0:T(8,128)S(1)}, f32[64,768]{1,0:T(8,128)S(1)}, u32[]{:S(2)}, u32[]{:S(2)}) collective-permute-start(f32[64,768]{1,0:T(8,128)S(1)} %get-tuple-element.31._.refs_0_), channel_id=1, source_target_pairs={{0,1},{1,0},{2,3},{3,2},{4,5},{5,4},{6,7},{7,6},{8,9},{9,8},{10,11... | collective-permute-start | bytes 589832 | tf_op jit(solution)/shard_map/ppermute | solution.py:22
  5.2 1.7 %collective-permute-start = (f32[3,1,3072]{2,1,0:T(1,128)S(1)}, f32[3,1,3072]{2,1,0:T(1,128)S(1)}, u32[]{:S(2)}, u32[]{:S(2)}) collective-permute-start(f32[3,1,3072]{2,1,0:T(1,128)S(1)} %shard_map.92.refs_2_), channel_id=1, source_target_pairs={{0,16},{16,0},{1,17},{17,1},{2,18},{18,2},{3,19},{19,3},{4,20},{20... | collective-permute-start | bytes 110600 | tf_op jit(solution)/shard_map/ppermute | solution.py:22
  5.3 8.3 %collective-permute-start.2 = (f32[64,768]{1,0:T(8,128)S(1)}, f32[64,768]{1,0:T(8,128)S(1)}, u32[]{:S(2)}, u32[]{:S(2)}) collective-permute-start(f32[64,768]{1,0:T(8,128)S(1)} %get-tuple-element.32.refs_1_), channel_id=1, source_target_pairs={{0,1},{1,0},{2,3},{3,2},{4,5},{5,4},{6,7},{7,6},{8,9},{9,8},{10,11... | collective-permute-start | bytes 589832 | tf_op jit(solution)/shard_map/ppermute | solution.py:22
  11.4 3.7 %collective-permute-start.6 = (f32[64,1536]{1,0:T(8,128)S(1)}, f32[64,1536]{1,0:T(8,128)S(1)}, u32[]{:S(2)}, u32[]{:S(2)}) collective-permute-start(f32[64,1536]{1,0:T(8,128)S(1)} %get-tuple-element.47), channel_id=1, source_target_pairs={{0,16},{16,0},{1,17},{17,1},{2,18},{18,2},{3,19},{19,3},{4,20},{20... | collective-permute-start | bytes 1179656 | tf_op jit(solution)/shard_map/ppermute | solution.py:22
  11.9 4.7 %collective-permute-start.1 = (f32[64,1536]{1,0:T(8,128)S(1)}, f32[64,1536]{1,0:T(8,128)S(1)}, u32[]{:S(2)}, u32[]{:S(2)}) collective-permute-start(f32[64,1536]{1,0:T(8,128)S(1)} %get-tuple-element.34), channel_id=1, source_target_pairs={{0,16},{16,0},{1,17},{17,1},{2,18},{18,2},{3,19},{19,3},{4,20},{20... | collective-permute-start | bytes 1179656 | tf_op jit(solution)/shard_map/ppermute | solution.py:22
  14.1 1.8 %collective-permute-start.7 = (f32[64,1536]{1,0:T(8,128)S(1)}, f32[64,1536]{1,0:T(8,128)S(1)}, u32[]{:S(2)}, u32[]{:S(2)}) collective-permute-start(f32[64,1536]{1,0:T(8,128)S(1)} %get-tuple-element.49), channel_id=1, source_target_pairs={{0,16},{16,0},{1,17},{17,1},{2,18},{18,2},{3,19},{19,3},{4,20},{20... | collective-permute-start | bytes 1179656 | tf_op jit(solution)/shard_map/ppermute | solution.py:22
  14.6 2.0 %collective-permute-start.4 = (f32[64,1536]{1,0:T(8,128)S(1)}, f32[64,1536]{1,0:T(8,128)S(1)}, u32[]{:S(2)}, u32[]{:S(2)}) collective-permute-start(f32[64,1536]{1,0:T(8,128)S(1)} %get-tuple-element.46), channel_id=1, source_target_pairs={{0,16},{16,0},{1,17},{17,1},{2,18},{18,2},{3,19},{19,3},{4,20},{20... | collective-permute-start | bytes 1179656 | tf_op jit(solution)/shard_map/ppermute | solution.py:22
  16.4 2.9 %collective-permute-start.8 = (bf16[128,512]{1,0:T(8,128)(2,1)S(1)}, bf16[128,512]{1,0:T(8,128)(2,1)S(1)}, u32[]{:S(2)}, u32[]{:S(2)}) collective-permute-start(bf16[128,512]{1,0:T(8,128)(2,1)S(1)} %shard_map.98.refs_1_), channel_id=1, source_target_pairs={{0,16},{16,0},{1,17},{17,1},{2,18},{18,2},{3,19},{19,3},{4,20},{20... | collective-permute-start | bytes 393224 | tf_op jit(solution)/shard_map/ppermute | solution.py:22
  17.1 2.2 %collective-permute-start.5 = (bf16[128,512]{1,0:T(8,128)(2,1)S(1)}, bf16[128,512]{1,0:T(8,128)(2,1)S(1)}, u32[]{:S(2)}, u32[]{:S(2)}) collective-permute-start(bf16[128,512]{1,0:T(8,128)(2,1)S(1)} %shard_map.96.refs_0_), channel_id=1, source_target_pairs={{0,16},{16,0},{1,17},{17,1},{2,18},{18,2},{3,19},{19,3},{4,20},{20... | collective-permute-start | bytes 393224 | tf_op jit(solution)/shard_map/ppermute | solution.py:22
  19.9 6.6 %collective-permute-start.11 = (bf16[32,1536]{1,0:T(8,128)(2,1)S(1)}, bf16[32,1536]{1,0:T(8,128)(2,1)S(1)}, u32[]{:S(2)}, u32[]{:S(2)}) collective-permute-start(bf16[32,1536]{1,0:T(8,128)(2,1)S(1)} %get-tuple-element.62), channel_id=1, source_target_pairs={{0,3},{1,2},{2,1},{3,0},{4,7},{5,6},{6,5},{7,4},{8,11},{9,10},{10,... | collective-permute-start | bytes 294920 | tf_op jit(solution)/shard_map/ppermute | solution.py:22
  22.7 5.4 %collective-permute-start.9 = (bf16[32,1536]{1,0:T(8,128)(2,1)S(1)}, bf16[32,1536]{1,0:T(8,128)(2,1)S(1)}, u32[]{:S(2)}, u32[]{:S(2)}) collective-permute-start(bf16[32,1536]{1,0:T(8,128)(2,1)S(1)} %get-tuple-element.61), channel_id=1, source_target_pairs={{0,1},{1,0},{2,3},{3,2},{4,5},{5,4},{6,7},{7,6},{8,9},{9,8},{10,11... | collective-permute-start | bytes 294920 | tf_op jit(solution)/shard_map/ppermute | solution.py:22
  23.2 4.9 %collective-permute-start.10 = (bf16[32,1536]{1,0:T(8,128)(2,1)S(1)}, bf16[32,1536]{1,0:T(8,128)(2,1)S(1)}, u32[]{:S(2)}, u32[]{:S(2)}) collective-permute-start(bf16[32,1536]{1,0:T(8,128)(2,1)S(1)} %select_convert_fusion.1), channel_id=1, source_target_pairs={{0,2},{1,3},{2,0},{3,1},{4,6},{5,7},{6,4},{7,5},{8,10},{9,11},{10,... | collective-permute-start | bytes 294920 | tf_op jit(solution)/shard_map/ppermute | solution.py:22
  28.2 15.2 %copy-start = (f32[64,1536]{1,0:T(8,128)S(1)}, f32[64,1536]{1,0:T(8,128)}, u32[]{:S(2)}) copy-start(f32[64,1536]{1,0:T(8,128)} %param.10) | copy-start | bytes 1179652
  28.2 4.7 %collective-permute-start.12 = (bf16[32,1536]{1,0:T(8,128)(2,1)S(1)}, bf16[32,1536]{1,0:T(8,128)(2,1)S(1)}, u32[]{:S(2)}, u32[]{:S(2)}) collective-permute-start(bf16[32,1536]{1,0:T(8,128)(2,1)S(1)} %get-tuple-element.59), channel_id=1, source_target_pairs={{0,4},{2,6},{4,0},{6,2},{8,12},{10,14},{12,8},{14,10},{1,5},{3,7},... | collective-permute-start | bytes 294920 | tf_op jit(solution)/shard_map/ppermute | solution.py:22
  32.9 5.6 %collective-permute-start.13 = (bf16[32,1536]{1,0:T(8,128)(2,1)S(1)}, bf16[32,1536]{1,0:T(8,128)(2,1)S(1)}, u32[]{:S(2)}, u32[]{:S(2)}) collective-permute-start(bf16[32,1536]{1,0:T(8,128)(2,1)S(1)} %fusion.2), channel_id=1, source_target_pairs={{0,8},{2,10},{4,12},{6,14},{8,0},{10,2},{12,4},{14,6},{1,9},{3,11}... | collective-permute-start | bytes 294920 | tf_op jit(solution)/shard_map/ppermute | solution.py:22
  38.6 4.7 %collective-permute-start.14 = (bf16[32,1536]{1,0:T(8,128)(2,1)S(1)}, bf16[32,1536]{1,0:T(8,128)(2,1)S(1)}, u32[]{:S(2)}, u32[]{:S(2)}) collective-permute-start(bf16[32,1536]{1,0:T(8,128)(2,1)S(1)} %add_convert_fusion), channel_id=1, source_target_pairs={{0,2},{2,0},{4,6},{6,4},{8,10},{10,8},{12,14},{14,12},{1,3},{3,1},... | collective-permute-start | bytes 294920 | tf_op jit(solution)/shard_map/ppermute | solution.py:22

commit v5 on v4

--- a/solution.py
+++ b/solution.py
@@ -14,7 +14,6 @@
 BF16 = jnp.bfloat16
 VMEM = pl.BlockSpec(memory_space=pltpu.VMEM)
 SMEM = pl.BlockSpec(memory_space=pltpu.SMEM)
-ANY = pl.BlockSpec(memory_space=pl.ANY)
 HBM = pl.BlockSpec(memory_space=pltpu.HBM)
 
 
@@ -52,7 +51,7 @@
     )
 
 
-def norm_kernel(pieces, branch_ref, states_ref, *refs):
+def norm_kernel(pieces, branch_ref, states_ref, modulation_ref, held_ref, *refs):
     out_refs, (tokens_ref, sems) = refs[:-2], refs[-2:]
     width = out_refs[0].shape[1]
     rows, model_width = tokens_ref.shape
@@ -63,6 +62,8 @@
         copy = pltpu.make_async_copy(states_ref.at[sl], tokens_ref.at[sl], sems.at[piece])
         copy.start()
         copies.append(copy)
+    held = pltpu.make_async_copy(modulation_ref, held_ref, sems.at[pieces])
+    held.start()
     for piece in range(pieces):
         sl = slice(piece * size, (piece + 1) * size)
         copies[piece].wait()
@@ -75,32 +76,20 @@
             start = branch_ref[0] * (model_width // 2) + index * width
             columns = pl.ds(pl.multiple_of(start, HD), width)
             out_ref[sl, :] = (tokens_ref[sl, columns] - mean) * inverse
-
-
-def normed_half(states, branch_index, cuts):
+    held.wait()
+
+
+def normed_half(states, modulation, branch_index, cuts):
     rows, width = states.shape
     pieces = 1
     return call(
         functools.partial(norm_kernel, pieces),
-        [pltpu.VMEM((rows, width // 2 // cuts), F32)] * cuts,
-        [SMEM, HBM],
-        [VMEM] * cuts,
-        [pltpu.VMEM((rows, width), F32), pltpu.SemaphoreType.DMA((pieces,))],
+        [pltpu.VMEM(modulation.shape, F32)] + [pltpu.VMEM((rows, width // 2 // cuts), F32)] * cuts,
+        [SMEM, HBM, HBM],
+        [VMEM] * (1 + cuts),
+        [pltpu.VMEM((rows, width), F32), pltpu.SemaphoreType.DMA((pieces + 1,))],
         moved=4 * rows * width,
-    )(branch_index[None], *in_hbm(states))
-
-
-def copy_kernel(source_ref, _, target_ref, sem):
-    copy = pltpu.make_async_copy(source_ref, target_ref, sem)
-    copy.start()
-    copy.wait()
-
-
-def into_vmem(array, after):
-    return call(
-        copy_kernel, pltpu.VMEM(array.shape, array.dtype), [HBM, ANY], VMEM, [pltpu.SemaphoreType.DMA],
-        moved=4 * array.size,
-    )(*in_hbm(array), after)
+    )(branch_index[None], *in_hbm(states, modulation))
 
 
 def modulate(tokens, factors):
@@ -113,12 +102,12 @@
     )
 
 
-def first_kernel(cuts, groups, branch_ref, step_ref, guidance_ref, *refs):
+def first_kernel(cuts, groups, branch_ref, *refs):
     tokens_refs, refs = refs[:cuts], refs[cuts:]
     mine_ref, other_ref, embedding_ref, *sources, out_source = refs[:7]
     factor_refs, refs = refs[7:7 + cuts], refs[7 + cuts:]
-    mine_gate_ref, other_gate_ref, keep_ref = refs[:3]
-    send_refs, targets, (out_target, sems) = refs[3:3 + groups], refs[3 + groups:-2], refs[-2:]
+    keep_ref, refs = refs[0], refs[1:]
+    send_refs, targets, (out_target, sems) = refs[:groups], refs[groups:-2], refs[-2:]
     width = tokens_refs[0].shape[1]
     copies = []
     for i, source in enumerate(sources):
@@ -133,14 +122,7 @@
     for copy in copies:
         copy.start()
 
-    first = branch_ref[0] == 0
-    step = 2.0 * (1.0 + step_ref[0].astype(F32)) / NSTEPS
-    scale = 1.5 + 0.5 * guidance_ref[0].astype(F32)
-    conditional, unconditional = step * scale, step * (1.0 - scale)
     base = branch_ref[0] * (width * cuts)
-    half = pl.ds(pl.multiple_of(base, HD), width * cuts)
-    mine_gate_ref[...] = jnp.where(first, conditional, unconditional) * (1.0 + mine_ref[2, :, half])
-    other_gate_ref[...] = jnp.where(first, unconditional, conditional) * (1.0 + other_ref[2, :, half])
     modulated = []
     for cut in range(cuts):
         columns = pl.ds(pl.multiple_of(base + cut * width, HD), width)
@@ -171,29 +153,28 @@
     return jnp.concatenate(rows, axis=0)
 
 
-def project_first(scalars, tokens, mine, other, embedding, weights, w_out, groups):
+def project_first(branch_index, tokens, mine, other, embedding, weights, w_out, groups):
     cuts = len(tokens)
     rows, width = tokens[0].shape
     columns = weights[0].shape[1]
     keep = pltpu.VMEM((rows, 3 * columns), F32)
     send = pltpu.VMEM((rows, 3 * columns // groups), F32)
-    gate = pltpu.VMEM((1, width * cuts), F32)
     result = call(
         functools.partial(first_kernel, cuts, groups),
         [pltpu.VMEM((4, width), F32)] * cuts
-        + [gate, gate, keep]
+        + [keep]
         + [send] * groups
         + [pltpu.VMEM((width, columns), BF16)] * (3 * cuts)
         + [pltpu.VMEM((w_out.shape[0] - w_out.shape[0] // 4, w_out.shape[1]), BF16)],
-        [SMEM] * 3 + [VMEM] * (cuts + 3) + [HBM] * 4,
-        [VMEM] * (4 * cuts + 4 + groups),
+        [SMEM] + [VMEM] * (cuts + 3) + [HBM] * 4,
+        [VMEM] * (4 * cuts + 2 + groups),
         [pltpu.SemaphoreType.DMA((3 * cuts + 1,))],
         flops=12 * rows * width * cuts * columns,
         moved=6 * width * cuts * columns,
-    )(*scalars, *tokens, mine, other, embedding, *in_hbm(*weights, w_out))
-    factors, (mine_gate, other_gate, keep), result = result[:cuts], result[cuts:cuts + 3], result[cuts + 3:]
+    )(branch_index[None], *tokens, mine, other, embedding, *in_hbm(*weights, w_out))
+    factors, keep, result = result[:cuts], result[cuts], result[cuts + 1:]
     sends, held, out_held = result[:groups], result[groups:-1], result[-1]
-    return factors, mine_gate, other_gate, keep, sends, [held[cut::cuts] for cut in range(cuts)], out_held
+    return factors, keep, sends, [held[cut::cuts] for cut in range(cuts)], out_held
 
 
 def later_kernel(added, groups, wanted, tokens_ref, factors_ref, wq_ref, wk_ref, wv_ref, *refs):
@@ -268,8 +249,18 @@
     )(*in_vmem(*flat))
 
 
+def gate_of(mine, branch_ref, step_ref, guidance_ref, modulation_ref, columns):
+    step = 2.0 * (1.0 + step_ref[0].astype(F32)) / NSTEPS
+    scale = 1.5 + 0.5 * guidance_ref[0].astype(F32)
+    conditional = (branch_ref[0] == 0) == mine
+    share = jnp.where(conditional, step * scale, step * (1.0 - scale))
+    half = pl.ds(pl.multiple_of(branch_ref[0] * columns, HD), columns)
+    return share * (1.0 + modulation_ref[2, :, half])
+
+
 def project_mine_kernel(cuts, *refs):
-    attended_refs, (gate_ref, held_ref, source_ref, out_ref, rest_ref, sems) = refs[:cuts], refs[cuts:]
+    scalar_refs, attended_refs, refs = refs[:3], refs[3:3 + cuts], refs[3 + cuts:]
+    modulation_ref, held_ref, source_ref, out_ref, rest_ref, sems = refs
     held_rows, columns = held_ref.shape
     copies = []
     size = rest_ref.shape[0] // sems.shape[0]
@@ -282,51 +273,54 @@
     attended = jnp.concatenate([ref[...] for ref in attended_refs], axis=1)
     slices = [slice(start, start + chunk) for start in range(0, columns, chunk)]
     partials = [dot(attended[:, :held_rows], held_ref[:, sl]) for sl in slices]
+    gate = gate_of(True, *scalar_refs, modulation_ref, columns)
     for copy in copies:
         copy.wait()
     for partial, sl in zip(partials, slices):
         partial = partial + dot(attended[:, held_rows:], rest_ref[:, sl])
-        out_ref[:, sl] = gate_ref[:, sl] * partial.astype(BF16).astype(F32)
-
-
-def project_mine(attended, held, w_out, gate):
+        out_ref[:, sl] = gate[:, sl] * partial.astype(BF16).astype(F32)
+
+
+def project_mine(scalars, attended, held, w_out, modulation):
     lat, columns = attended[0].shape[0], w_out.shape[1]
     rest = w_out.shape[0] - held.shape[0]
     return call(
         functools.partial(project_mine_kernel, len(attended)),
         [pltpu.VMEM((lat, columns), F32), pltpu.VMEM((rest, columns), BF16)],
-        [VMEM] * (2 + len(attended)) + [HBM],
+        [SMEM] * 3 + [VMEM] * (2 + len(attended)) + [HBM],
         [VMEM] * 2,
         [pltpu.SemaphoreType.DMA((2,))],
         flops=2 * lat * w_out.size,
         moved=2 * w_out.size,
-    )(*attended, *in_vmem(gate, held), *in_hbm(w_out))
+    )(*scalars, *attended, modulation, *in_vmem(held), *in_hbm(w_out))
 
 
 def project_other_kernel(cuts, *refs):
-    attended_refs, (held_ref, rest_ref, gate_ref, before_ref, *out_refs) = refs[:cuts], refs[cuts:]
+    scalar_refs, attended_refs, refs = refs[:3], refs[3:3 + cuts], refs[3 + cuts:]
+    modulation_ref, held_ref, rest_ref, before_ref, *out_refs = refs
     held_rows = held_ref.shape[0]
     rows, columns = out_refs[0].shape
     chunk = math.gcd(columns, 512)
+    gate = gate_of(False, *scalar_refs, modulation_ref, columns)
     attended = jnp.concatenate([ref[...] for ref in attended_refs], axis=1)
     for start in range(0, columns, chunk):
         sl = slice(start, start + chunk)
         partial = dot(attended[:, :held_rows], held_ref[:, sl]) + dot(attended[:, held_rows:], rest_ref[:, sl])
-        increment = before_ref[:, sl] + gate_ref[:, sl] * partial.astype(BF16).astype(F32)
+        increment = before_ref[:, sl] + gate[:, sl] * partial.astype(BF16).astype(F32)
         for block, out_ref in enumerate(out_refs):
             out_ref[:, sl] = increment[block * rows:(block + 1) * rows]
 
 
-def project_other(attended, held, rest, gate, before, blocks):
+def project_other(scalars, attended, held, rest, modulation, before, blocks):
     lat, columns = before.shape
     return call(
         functools.partial(project_other_kernel, len(attended)),
         [pltpu.VMEM((lat // blocks, columns), F32)] * blocks,
-        [VMEM] * (4 + len(attended)),
+        [SMEM] * 3 + [VMEM] * (4 + len(attended)),
         [VMEM] * blocks,
         flops=4 * lat * held.size,
         moved=4 * held.size,
-    )(*attended, *in_vmem(held, rest, gate, before))
+    )(*scalars, *attended, modulation, *in_vmem(held, rest, before))
 
 
 def scan_general(parts):
@@ -382,20 +376,22 @@
     branch_index = lax.axis_index("branch")
     rows, model_width = states.shape[1:]
     half_width = model_width // 2
-    cuts = 2
-    normed = normed_half(states[0], branch_index, cuts)
-    modulation = into_vmem(jnp.transpose(modulation, (1, 0, 2)), normed[0])
+    cuts = 1
+    modulation, *normed = normed_half(
+        states[0], jnp.transpose(modulation, (1, 0, 2)), branch_index, cuts
+    )
     tokens = [
-        [xor_permute(piece, "tok", mask) for piece in normed] for mask in range(1, tok_count)
+        [xor_permute(piece.astype(jnp.float16), "tok", mask).astype(F32) for piece in normed]
+        for mask in range(1, tok_count)
     ]
     other_modulation = xor_permute(modulation, "branch", 1)
     embedding = embed_half(timesteps, half_width, branch_index)
 
     columns = w_query.shape[1]
     groups = 2 if columns % (2 * HD) == 0 else 1
-    factors, mine_gate, other_gate, keep, sends, weights, out_held = project_first(
-        (branch_index[None], timesteps, guidance_index),
-        normed, modulation, other_modulation, embedding, (w_query, w_key, w_value), w_out, groups
+    factors, keep, sends, weights, out_held = project_first(
+        branch_index, normed, modulation, other_modulation, embedding,
+        (w_query, w_key, w_value), w_out, groups
     )
     blocks = [
         [(keep, xor_permute(send, "branch", 1), 3 * columns // groups * group)]
@@ -410,8 +406,11 @@
             blocks[group].append((keep, xor_permute(send, "branch", 1), 0))
     attended = [attention(blocks[group], columns // groups) for group in range(groups)]
     attended_other = [xor_permute(array, "branch", 1) for array in attended]
-    increments, out_rest = project_mine(attended, out_held, w_out, mine_gate)
-    parts = project_other(attended_other, out_held, out_rest, other_gate, increments, tok_count)
+    scalars = (branch_index[None], timesteps, guidance_index)
+    increments, out_rest = project_mine(scalars, attended, out_held, w_out, modulation)
+    parts = project_other(
+        scalars, attended_other, out_held, out_rest, other_modulation, increments, tok_count
+    )
     pairs = tok_count == 2 and lax.axis_size("tm") % 2 == 0 and rows % 32 == 0
     scan = scan_planes if pairs else scan_general
     return (start_state + scan(parts))[None]

time: 44.5 us -> 42.5 us (0.955)
  Pallas kernels: 11.9 us -> 10.9 us
  waiting for transfers between devices: 14.9 us -> 14.2 us
    pallas_call x2 -> x1, Pallas kernels: 2.2 us -> 1.43 us  [normed_half(): call(functools.partial(norm_kernel, pieces), [pltpu.VMEM(modulation.shape...]
    ppermute x15 -> x14, waiting for transfers between devices: 14.9 us -> 14.2 us  [xor_permute(): lax.ppermute(x, axes, [(i, i ^ mask) for i in range(lax.axis_size(axes))])]
    ppermute x15 -> x14, starting transfers between devices: 14.7 us -> 14.4 us  [xor_permute(): lax.ppermute(x, axes, [(i, i ^ mask) for i in range(lax.axis_size(axes))])]
    pallas_call x3 -> x2, Pallas kernels: 1.78 us -> 1.63 us  [project_later(): call(functools.partial(later_kernel, len(before), groups, wanted), [out,...]
  transfers between devices with their start and end apart: 15 -> 14, of which waited for: 7 -> 8; matrix products, arithmetic and copies ran while one was open for 1% -> 1% of each run, Pallas kernels for 22% -> 21%
where the time goes in v5:
time: 42.5 us; the launch traced here: 42.4 us
  starting transfers between devices  14.4 us (34%)
  waiting for transfers between devices  14.2 us (33%)
  Pallas kernels  10.9 us (26%)
  between operations  1.46 us (3%)
  other arithmetic  1.4 us (3%)
    ppermute x14, starting transfers between devices, xor_permute(): lax.ppermute(x, axes, [(i, i ^ mask) for i in range(lax.axis_size(axes))])  14.4 us
    ppermute x14, waiting for transfers between devices, xor_permute(): lax.ppermute(x, axes, [(i, i ^ mask) for i in range(lax.axis_size(axes))])  14.2 us
    pallas_call x1, Pallas kernels, project_first(): call(functools.partial(first_kernel, cuts, groups), [pltpu.VMEM((4, width...  4.47 us
    pallas_call x1, Pallas kernels, project_mine(): call(functools.partial(project_mine_kernel, len(attended)), [pltpu.VMEM((...  1.73 us
    pallas_call x2, Pallas kernels, project_later(): call(functools.partial(later_kernel, len(before), groups, wanted), [out,...  1.63 us
    pallas_call x1, Pallas kernels, normed_half(): call(functools.partial(norm_kernel, pieces), [pltpu.VMEM(modulation.shape...  1.43 us
    pallas_call x2, Pallas kernels, attention(): call(functools.partial(attention_kernel, [block[2] for block in blocks]),...  1.05 us
  transfers between devices with their start and end apart: 14, of which 8 were waited for; matrix products, arithmetic and copies ran while one was open for 1% of the time, Pallas kernels for 21%

profile of v5, /device:TPU:0, one launch (start us, length us, event | category | flops | bytes accessed | tf_op | source)
XLA Modules:
  0.0 42.4 jit_solution(12159608826674612145)
XLA Ops:
  0.0 1.4 %shard_map.91 = (f32[3,1,3072]{2,1,0:T(1,128)S(1)}, f32[64,1536]{1,0:T(8,128)S(1)}) custom-call(s32[1]{0:T(128)} %bitcast.branch_ref.refs_0_, f32[64,3072]{1,0:T(8,128)} %bitcast.6, f32[3,1,3072]{2,1,0:T(1,128)} %bitcast.7), custom_call_target="tpu_custom_call" | custom-call | bytes 786432 | tf_op jit(solution)/shard_map/pallas_call | solution.py:85
  1.4 0.5 %collective-permute-start = (f32[3,1,3072]{2,1,0:T(1,128)S(1)}, f32[3,1,3072]{2,1,0:T(1,128)S(1)}, u32[]{:S(2)}, u32[]{:S(2)}) collective-permute-start(f32[3,1,3072]{2,1,0:T(1,128)S(1)} %get-tuple-element.24.refs_1_.refs_5_), channel_id=1, source_target_pairs={{0,16},{16,0},{1,17},{17,1},{2,18},{18,2},{3,19},{19,3},{4,20},{20... | collective-permute-start | bytes 110600 | tf_op jit(solution)/shard_map/ppermute | solution.py:21
  2.0 2.6 %collective-permute-start.2 = (f16[64,1536]{1,0:T(8,128)(2,1)S(1)}, f16[64,1536]{1,0:T(8,128)(2,1)S(1)}, u32[]{:S(2)}, u32[]{:S(2)}) collective-permute-start(f16[64,1536]{1,0:T(8,128)(2,1)S(1)} %convert_element_type.46), channel_id=1, source_target_pairs={{0,1},{1,0},{2,3},{3,2},{4,5},{5,4},{6,7},{7,6},{8,9},{9,8},{10,11... | collective-permute-start | bytes 589832 | tf_op jit(solution)/shard_map/ppermute | solution.py:21
  5.2 0.2 broadcast_select_fusion.refs_3_
  5.4 4.5 %shard_map.92 = (f32[4,1536]{1,0:T(4,128)S(1)}, f32[64,3072]{1,0:T(8,128)S(1)}, f32[64,1536]{1,0:T(8,128)S(1)}, f32[64,1536]{1,0:T(8,128)S(1)}, bf16[1536,1024]{...) custom-call(s32[1]{0:T(128)} %bitcast.branch_ref.refs_0_, ...), custom_call_target="tpu_custom_call" | custom-call | flops 1207959552 | bytes 9437184 | tf_op jit(solution)/shard_map/pallas_call | solution.py:162
  9.9 0.3 collective-permute-start.5
  10.2 0.3 collective-permute-start.1
  10.5 0.8 %shard_map.95 = (f32[64,1536]{1,0:T(8,128)S(1)}, f32[64,1536]{1,0:T(8,128)S(1)}) custom-call(f32[64,1536]{1,0:T(8,128)S(1)} %convert_element_type.47.tokens_ref, f32[4,1536]{1,0:T(4,128)S(1)} %get-tuple-element.27.factors_ref, bf16[1536,1024]{1,0:T(8,128)(2,1)S(1)} %get-tuple-element.28.wq_ref, bf16[1536,1024]{1,0:T(8,128)(2,1)S(1)} %get-tuple-element.29.wk_ref, ...), custom_call_target="tpu_custom_call" | custom-call | flops 603979776 | bytes 4718592 | tf_op jit(solution)/shard_map/pallas_call | solution.py:200
  11.3 0.3 collective-permute-start.6
  11.6 0.8 %shard_map.93 = (f32[64,1536]{1,0:T(8,128)S(1)}, f32[64,1536]{1,0:T(8,128)S(1)}) custom-call(f32[64,1536]{1,0:T(8,128)S(1)} %convert_element_type.47.tokens_ref, f32[4,1536]{1,0:T(4,128)S(1)} %get-tuple-element.27.factors_ref, bf16[1536,1024]{1,0:T(8,128)(2,1)S(1)} %get-tuple-element.28.wq_ref, bf16[1536,1024]{1,0:T(8,128)(2,1)S(1)} %get-tuple-element.29.wk_ref, ...), custom_call_target="tpu_custom_call" | custom-call | flops 603979776 | bytes 4718592 | tf_op jit(solution)/shard_map/pallas_call | solution.py:200
  12.5 0.4 collective-permute-start.3
  12.8 0.3 collective-permute-done.6.refs_3_
  13.1 0.5 %shard_map.96.refs_4_ = bf16[128,512]{1,0:T(8,128)(2,1)S(1)} custom-call(f32[64,3072]{1,0:T(8,128)S(1)} %get-tuple-element.25.refs_0_, f32[64,1536]{1,0:T(8,128)S(1)} %collective-permute-done.5.refs_1_, f32[64,1536]{1,0:T(8,128)S(1)} %get-tuple-element.34.refs_2_, f32[64,1536]{1,0:T(8,128)S(1)} %collective-permute-done.6.refs_3_), custom_call_target="tpu_custom_call" | custom-call | flops 33554432 | bytes 786432 | tf_op jit(solution)/shard_map/pallas_call | solution.py:242
  13.7 0.3 collective-permute-start.7
  14.0 0.3 collective-permute-done.3.refs_3_
  14.2 0.5 %shard_map.94.refs_3_ = bf16[128,512]{1,0:T(8,128)(2,1)S(1)} custom-call(f32[64,3072]{1,0:T(8,128)S(1)} %get-tuple-element.25.refs_0_, f32[64,1536]{1,0:T(8,128)S(1)} %collective-permute-done.1.refs_1_, f32[64,1536]{1,0:T(8,128)S(1)} %get-tuple-element.31.refs_2_, f32[64,1536]{1,0:T(8,128)S(1)} %collective-permute-done.3.refs_3_), custom_call_target="tpu_custom_call" | custom-call | flops 33554432 | bytes 786432 | tf_op jit(solution)/shard_map/pallas_call | solution.py:242
  14.8 0.4 collective-permute-start.4
  15.8 1.7 %shard_map.97 = (f32[128,1536]{1,0:T(8,128)S(1)}, bf16[256,1536]{1,0:T(8,128)(2,1)S(1)}) custom-call(s32[1]{0:T(128)} %bitcast.branch_ref.refs_0_, s32[1]{0:T(128)S(6)} %copy.10.refs_1_, s32[1]{0:T(128)S(6)} %copy.11.refs_2_, bf16[128,512]{1,0:T(8,128)(2,1)S(1)} %shard_map.94.refs_3_, bf16[128,512]{1,0:T(8,128)(2,1)S(1)} %shard_map.96.refs_4_, ...), custom_call_target="tpu_custom_call" | custom-call | flops 402653184 | bytes 3145728 | tf_op jit(solution)/shard_map/pallas_call | solution.py:287
  17.5 0.6 %shard_map.98 = (f32[64,1536]{1,0:T(8,128)S(1)}, f32[64,1536]{1,0:T(8,128)S(1)}) custom-call(s32[1]{0:T(128)} %bitcast.branch_ref.refs_0_, s32[1]{0:T(128)S(6)} %copy.10.refs_1_, s32[1]{0:T(128)S(6)} %copy.11.refs_2_, bf16[128,512]{1,0:T(8,128)(2,1)S(1)} %collective-permute-done.4.refs_3_, bf16[128,512]{1,0:T(8,128)(2,1)S(1)} %collective-permute-done.7.refs_4_, ...), custom_call_target="tpu_custom_call" | custom-call | flops 603979776 | bytes 4718592 | tf_op jit(solution)/shard_map/pallas_call | solution.py:316
  18.2 2.4 %collective-permute-start.10 = (bf16[32,1536]{1,0:T(8,128)(2,1)S(1)}, bf16[32,1536]{1,0:T(8,128)(2,1)S(1)}, u32[]{:S(2)}, u32[]{:S(2)}) collective-permute-start(bf16[32,1536]{1,0:T(8,128)(2,1)S(1)} %get-tuple-element.46), channel_id=1, source_target_pairs={{0,3},{1,2},{2,1},{3,0},{4,7},{5,6},{6,5},{7,4},{8,11},{9,10},{10,... | collective-permute-start | bytes 294920 | tf_op jit(solution)/shard_map/ppermute | solution.py:21
  20.6 0.7 %collective-permute-start.8 = (bf16[32,1536]{1,0:T(8,128)(2,1)S(1)}, bf16[32,1536]{1,0:T(8,128)(2,1)S(1)}, u32[]{:S(2)}, u32[]{:S(2)}) collective-permute-start(bf16[32,1536]{1,0:T(8,128)(2,1)S(1)} %get-tuple-element.45), channel_id=1, source_target_pairs={{0,1},{1,0},{2,3},{3,2},{4,5},{5,4},{6,7},{7,6},{8,9},{9,8},{10,11... | collective-permute-start | bytes 294920 | tf_op jit(solution)/shard_map/ppermute | solution.py:21
  21.3 0.6 %collective-permute-start.9 = (bf16[32,1536]{1,0:T(8,128)(2,1)S(1)}, bf16[32,1536]{1,0:T(8,128)(2,1)S(1)}, u32[]{:S(2)}, u32[]{:S(2)}) collective-permute-start(bf16[32,1536]{1,0:T(8,128)(2,1)S(1)} %select_convert_fusion.1), channel_id=1, source_target_pairs={{0,2},{1,3},{2,0},{3,1},{4,6},{5,7},{6,4},{7,5},{8,10},{9,11},{10,... | collective-permute-start | bytes 294920 | tf_op jit(solution)/shard_map/ppermute | solution.py:21
  21.8 2.9 %collective-permute-done.10 = bf16[32,1536]{1,0:T(8,128)(2,1)S(1)} collective-permute-done((bf16[32,1536]{1,0:T(8,128)(2,1)S(1)}, bf16[32,1536]{1,0:T(8,128)(2,1)S(1)}, u32[]{:S(2)}, u32[]{:S(2)}) %collective-permute-start.10) | collective-permute-done | bytes 98336 | tf_op jit(solution)/shard_map/ppermute | solution.py:21
  24.8 1.4 %collective-permute-done.8 = bf16[32,1536]{1,0:T(8,128)(2,1)S(1)} collective-permute-done((bf16[32,1536]{1,0:T(8,128)(2,1)S(1)}, bf16[32,1536]{1,0:T(8,128)(2,1)S(1)}, u32[]{:S(2)}, u32[]{:S(2)}) %collective-permute-start.8) | collective-permute-done | bytes 98336 | tf_op jit(solution)/shard_map/ppermute | solution.py:21
  26.3 1.6 %collective-permute-start.11 = (bf16[32,1536]{1,0:T(8,128)(2,1)S(1)}, bf16[32,1536]{1,0:T(8,128)(2,1)S(1)}, u32[]{:S(2)}, u32[]{:S(2)}) collective-permute-start(bf16[32,1536]{1,0:T(8,128)(2,1)S(1)} %get-tuple-element.43), channel_id=1, source_target_pairs={{0,4},{2,6},{4,0},{6,2},{8,12},{10,14},{12,8},{14,10},{1,5},{3,7},... | collective-permute-start | bytes 294920 | tf_op jit(solution)/shard_map/ppermute | solution.py:21
  28.0 3.0 %collective-permute-done.11 = bf16[32,1536]{1,0:T(8,128)(2,1)S(1)} collective-permute-done((bf16[32,1536]{1,0:T(8,128)(2,1)S(1)}, bf16[32,1536]{1,0:T(8,128)(2,1)S(1)}, u32[]{:S(2)}, u32[]{:S(2)}) %collective-permute-start.11) | collective-permute-done | bytes 98336 | tf_op jit(solution)/shard_map/ppermute | solution.py:21
  31.1 2.7 %collective-permute-start.12 = (bf16[32,1536]{1,0:T(8,128)(2,1)S(1)}, bf16[32,1536]{1,0:T(8,128)(2,1)S(1)}, u32[]{:S(2)}, u32[]{:S(2)}) collective-permute-start(bf16[32,1536]{1,0:T(8,128)(2,1)S(1)} %fusion.2), channel_id=1, source_target_pairs={{0,8},{2,10},{4,12},{6,14},{8,0},{10,2},{12,4},{14,6},{1,9},{3,11}... | collective-permute-start | bytes 294920 | tf_op jit(solution)/shard_map/ppermute | solution.py:21
  33.7 2.9 %collective-permute-done.12 = bf16[32,1536]{1,0:T(8,128)(2,1)S(1)} collective-permute-done((bf16[32,1536]{1,0:T(8,128)(2,1)S(1)}, bf16[32,1536]{1,0:T(8,128)(2,1)S(1)}, u32[]{:S(2)}, u32[]{:S(2)}) %collective-permute-start.12) | collective-permute-done | bytes 98336 | tf_op jit(solution)/shard_map/ppermute | solution.py:21
  36.7 1.5 %collective-permute-start.13 = (bf16[32,1536]{1,0:T(8,128)(2,1)S(1)}, bf16[32,1536]{1,0:T(8,128)(2,1)S(1)}, u32[]{:S(2)}, u32[]{:S(2)}) collective-permute-start(bf16[32,1536]{1,0:T(8,128)(2,1)S(1)} %add_convert_fusion), channel_id=1, source_target_pairs={{0,2},{2,0},{4,6},{6,4},{8,10},{10,8},{12,14},{14,12},{1,3},{3,1},... | collective-permute-start | bytes 294920 | tf_op jit(solution)/shard_map/ppermute | solution.py:21
  38.2 3.2 %collective-permute-done.13 = bf16[32,1536]{1,0:T(8,128)(2,1)S(1)} collective-permute-done((bf16[32,1536]{1,0:T(8,128)(2,1)S(1)}, bf16[32,1536]{1,0:T(8,128)(2,1)S(1)}, u32[]{:S(2)}, u32[]{:S(2)}) %collective-permute-start.13) | collective-permute-done | bytes 98336 | tf_op jit(solution)/shard_map/ppermute | solution.py:21
  41.4 0.1 convert_select_fusion.1
  41.6 0.8 %fusion = f32[1,64,1536]{2,1,0:T(8,128)} fusion(f32[64,1536]{1,0:T(8,128)S(1)} %copy-done, f32[32,1536]{1,0:T(8,128)S(1)} %convert_select_fusion, f32[32,1536]{1,0:T(8,128)S(1)} %get-tuple-element.41), kind=kLoop, calls=%fused_computation.1 | loop fusion | flops 196608 | bytes 1179648 | tf_op jit(solution)/shard_map/broadcast_in_dim | solution.py:416
  (17 shorter events, 0.4 us)
Async XLA Ops:
  1.4 4.0 %collective-permute-start = (f32[3,1,3072]{2,1,0:T(1,128)S(1)}, f32[3,1,3072]{2,1,0:T(1,128)S(1)}, u32[]{:S(2)}, u32[]{:S(2)}) collective-permute-start(f32[3,1,3072]{2,1,0:T(1,128)S(1)} %get-tuple-element.24.refs_1_.refs_5_), channel_id=1, source_target_pairs={{0,16},{16,0},{1,17},{17,1},{2,18},{18,2},{3,19},{19,3},{4,20},{20... | collective-permute-start | bytes 110600 | tf_op jit(solution)/shard_map/ppermute | solution.py:21
  2.0 8.5 %collective-permute-start.2 = (f16[64,1536]{1,0:T(8,128)(2,1)S(1)}, f16[64,1536]{1,0:T(8,128)(2,1)S(1)}, u32[]{:S(2)}, u32[]{:S(2)}) collective-permute-start(f16[64,1536]{1,0:T(8,128)(2,1)S(1)} %convert_element_type.46), channel_id=1, source_target_pairs={{0,1},{1,0},{2,3},{3,2},{4,5},{5,4},{6,7},{7,6},{8,9},{9,8},{10,11... | collective-permute-start | bytes 589832 | tf_op jit(solution)/shard_map/ppermute | solution.py:21
  9.9 2.9 %collective-permute-start.5 = (f32[64,1536]{1,0:T(8,128)S(1)}, f32[64,1536]{1,0:T(8,128)S(1)}, u32[]{:S(2)}, u32[]{:S(2)}) collective-permute-start(f32[64,1536]{1,0:T(8,128)S(1)} %get-tuple-element.33), channel_id=1, source_target_pairs={{0,16},{16,0},{1,17},{17,1},{2,18},{18,2},{3,19},{19,3},{4,20},{20... | collective-permute-start | bytes 1179656 | tf_op jit(solution)/shard_map/ppermute | solution.py:21
  10.2 3.8 %collective-permute-start.1 = (f32[64,1536]{1,0:T(8,128)S(1)}, f32[64,1536]{1,0:T(8,128)S(1)}, u32[]{:S(2)}, u32[]{:S(2)}) collective-permute-start(f32[64,1536]{1,0:T(8,128)S(1)} %get-tuple-element.26), channel_id=1, source_target_pairs={{0,16},{16,0},{1,17},{17,1},{2,18},{18,2},{3,19},{19,3},{4,20},{20... | collective-permute-start | bytes 1179656 | tf_op jit(solution)/shard_map/ppermute | solution.py:21
  11.3 1.8 %collective-permute-start.6 = (f32[64,1536]{1,0:T(8,128)S(1)}, f32[64,1536]{1,0:T(8,128)S(1)}, u32[]{:S(2)}, u32[]{:S(2)}) collective-permute-start(f32[64,1536]{1,0:T(8,128)S(1)} %get-tuple-element.35), channel_id=1, source_target_pairs={{0,16},{16,0},{1,17},{17,1},{2,18},{18,2},{3,19},{19,3},{4,20},{20... | collective-permute-start | bytes 1179656 | tf_op jit(solution)/shard_map/ppermute | solution.py:21
  12.5 1.8 %collective-permute-start.3 = (f32[64,1536]{1,0:T(8,128)S(1)}, f32[64,1536]{1,0:T(8,128)S(1)}, u32[]{:S(2)}, u32[]{:S(2)}) collective-permute-start(f32[64,1536]{1,0:T(8,128)S(1)} %get-tuple-element.32), channel_id=1, source_target_pairs={{0,16},{16,0},{1,17},{17,1},{2,18},{18,2},{3,19},{19,3},{4,20},{20... | collective-permute-start | bytes 1179656 | tf_op jit(solution)/shard_map/ppermute | solution.py:21
  13.7 3.9 %collective-permute-start.7 = (bf16[128,512]{1,0:T(8,128)(2,1)S(1)}, bf16[128,512]{1,0:T(8,128)(2,1)S(1)}, u32[]{:S(2)}, u32[]{:S(2)}) collective-permute-start(bf16[128,512]{1,0:T(8,128)(2,1)S(1)} %shard_map.96.refs_4_), channel_id=1, source_target_pairs={{0,16},{16,0},{1,17},{17,1},{2,18},{18,2},{3,19},{19,3},{4,20},{20... | collective-permute-start | bytes 393224 | tf_op jit(solution)/shard_map/ppermute | solution.py:21
  14.8 2.8 %collective-permute-start.4 = (bf16[128,512]{1,0:T(8,128)(2,1)S(1)}, bf16[128,512]{1,0:T(8,128)(2,1)S(1)}, u32[]{:S(2)}, u32[]{:S(2)}) collective-permute-start(bf16[128,512]{1,0:T(8,128)(2,1)S(1)} %shard_map.94.refs_3_), channel_id=1, source_target_pairs={{0,16},{16,0},{1,17},{17,1},{2,18},{18,2},{3,19},{19,3},{4,20},{20... | collective-permute-start | bytes 393224 | tf_op jit(solution)/shard_map/ppermute | solution.py:21
  18.1 23.4 %copy-start = (f32[64,1536]{1,0:T(8,128)S(1)}, f32[64,1536]{1,0:T(8,128)}, u32[]{:S(2)}) copy-start(f32[64,1536]{1,0:T(8,128)} %param.10) | copy-start | bytes 1179652
  18.2 6.6 %collective-permute-start.10 = (bf16[32,1536]{1,0:T(8,128)(2,1)S(1)}, bf16[32,1536]{1,0:T(8,128)(2,1)S(1)}, u32[]{:S(2)}, u32[]{:S(2)}) collective-permute-start(bf16[32,1536]{1,0:T(8,128)(2,1)S(1)} %get-tuple-element.46), channel_id=1, source_target_pairs={{0,3},{1,2},{2,1},{3,0},{4,7},{5,6},{6,5},{7,4},{8,11},{9,10},{10,... | collective-permute-start | bytes 294920 | tf_op jit(solution)/shard_map/ppermute | solution.py:21
  20.6 5.7 %collective-permute-start.8 = (bf16[32,1536]{1,0:T(8,128)(2,1)S(1)}, bf16[32,1536]{1,0:T(8,128)(2,1)S(1)}, u32[]{:S(2)}, u32[]{:S(2)}) collective-permute-start(bf16[32,1536]{1,0:T(8,128)(2,1)S(1)} %get-tuple-element.45), channel_id=1, source_target_pairs={{0,1},{1,0},{2,3},{3,2},{4,5},{5,4},{6,7},{7,6},{8,9},{9,8},{10,11... | collective-permute-start | bytes 294920 | tf_op jit(solution)/shard_map/ppermute | solution.py:21
  21.3 5.0 %collective-permute-start.9 = (bf16[32,1536]{1,0:T(8,128)(2,1)S(1)}, bf16[32,1536]{1,0:T(8,128)(2,1)S(1)}, u32[]{:S(2)}, u32[]{:S(2)}) collective-permute-start(bf16[32,1536]{1,0:T(8,128)(2,1)S(1)} %select_convert_fusion.1), channel_id=1, source_target_pairs={{0,2},{1,3},{2,0},{3,1},{4,6},{5,7},{6,4},{7,5},{8,10},{9,11},{10,... | collective-permute-start | bytes 294920 | tf_op jit(solution)/shard_map/ppermute | solution.py:21
  26.3 4.7 %collective-permute-start.11 = (bf16[32,1536]{1,0:T(8,128)(2,1)S(1)}, bf16[32,1536]{1,0:T(8,128)(2,1)S(1)}, u32[]{:S(2)}, u32[]{:S(2)}) collective-permute-start(bf16[32,1536]{1,0:T(8,128)(2,1)S(1)} %get-tuple-element.43), channel_id=1, source_target_pairs={{0,4},{2,6},{4,0},{6,2},{8,12},{10,14},{12,8},{14,10},{1,5},{3,7},... | collective-permute-start | bytes 294920 | tf_op jit(solution)/shard_map/ppermute | solution.py:21
  31.1 5.6 %collective-permute-start.12 = (bf16[32,1536]{1,0:T(8,128)(2,1)S(1)}, bf16[32,1536]{1,0:T(8,128)(2,1)S(1)}, u32[]{:S(2)}, u32[]{:S(2)}) collective-permute-start(bf16[32,1536]{1,0:T(8,128)(2,1)S(1)} %fusion.2), channel_id=1, source_target_pairs={{0,8},{2,10},{4,12},{6,14},{8,0},{10,2},{12,4},{14,6},{1,9},{3,11}... | collective-permute-start | bytes 294920 | tf_op jit(solution)/shard_map/ppermute | solution.py:21
  36.7 4.7 %collective-permute-start.13 = (bf16[32,1536]{1,0:T(8,128)(2,1)S(1)}, bf16[32,1536]{1,0:T(8,128)(2,1)S(1)}, u32[]{:S(2)}, u32[]{:S(2)}) collective-permute-start(bf16[32,1536]{1,0:T(8,128)(2,1)S(1)} %add_convert_fusion), channel_id=1, source_target_pairs={{0,2},{2,0},{4,6},{6,4},{8,10},{10,8},{12,14},{14,12},{1,3},{3,1},... | collective-permute-start | bytes 294920 | tf_op jit(solution)/shard_map/ppermute | solution.py:21

commit v6 on v5

v6 whole, which is shorter than its diff:
```python
import functools
import math

import jax
import jax.numpy as jnp
from jax import lax
from jax.experimental import pallas as pl
from jax.experimental.pallas import tpu as pltpu
from jax.sharding import PartitionSpec as P

HD = 128
NSTEPS = 50
F32 = jnp.float32
BF16 = jnp.bfloat16
VMEM = pl.BlockSpec(memory_space=pltpu.VMEM)
SMEM = pl.BlockSpec(memory_space=pltpu.SMEM)
ANY = pl.BlockSpec(memory_space=pl.ANY)
HBM = pl.BlockSpec(memory_space=pltpu.HBM)


def xor_permute(x, axes, mask):
    return lax.ppermute(x, axes, [(i, i ^ mask) for i in range(lax.axis_size(axes))])


def dot(a, b):
    return jnp.dot(a, b, preferred_element_type=F32)


def embed_half(step_ids, half_width, branch_index):
    frequency = jnp.exp(-math.log(10000.0) * jnp.arange(half_width, dtype=F32) / half_width)
    phases = step_ids.astype(F32)[:, None] * frequency[None, :]
    return jnp.where(branch_index == 0, jnp.sin(phases), jnp.cos(phases))


def in_vmem(*arrays):
    return [pltpu.with_memory_space_constraint(array, pltpu.VMEM) for array in arrays]


def in_hbm(*arrays):
    return [pltpu.with_memory_space_constraint(array, pltpu.HBM) for array in arrays]


def call(kernel, out_shape, in_specs, out_specs, scratch_shapes=(), aliases=None, flops=0, moved=0):
    return pl.pallas_call(
        kernel,
        out_shape=out_shape,
        in_specs=in_specs,
        out_specs=out_specs,
        scratch_shapes=scratch_shapes,
        input_output_aliases=aliases or {},
        cost_estimate=pl.CostEstimate(flops=flops, bytes_accessed=moved, transcendentals=0),
        compiler_params=pltpu.CompilerParams(vmem_limit_bytes=6 << 20),
    )


def norm_kernel(branch_ref, states_ref, modulation_ref, held_ref, *refs):
    out_refs, (tokens_ref, sems) = refs[:-2], refs[-2:]
    rows, model_width = tokens_ref.shape
    pieces = sems.shape[0] - 1
    size = rows // pieces
    copies = []
    for piece in range(pieces):
        sl = pl.ds(piece * size, size)
        copies.append(pltpu.make_async_copy(states_ref.at[sl], tokens_ref.at[sl], sems.at[piece]))
    copies.append(pltpu.make_async_copy(modulation_ref, held_ref, sems.at[pieces]))
    for copy in copies:
        copy.start()
    for copy in copies:
        copy.wait()
    tokens = tokens_ref[...]
    mean = jnp.sum(tokens, axis=1, keepdims=True) * (1.0 / model_width)
    centered = tokens - mean
    variance = jnp.sum(centered * centered, axis=1, keepdims=True) * (1.0 / model_width)
    inverse = 1.0 / jnp.sqrt(variance + 1e-06)
    start = branch_ref[0] * (model_width // 2)
    for out_ref in out_refs:
        width = out_ref.shape[1]
        columns = pl.ds(pl.multiple_of(start, HD), width)
        out_ref[...] = (tokens_ref[:, columns] - mean) * inverse
        start = start + width


def normed_half(states, modulation, branch_index, widths):
    rows, width = states.shape
    pieces = 1
    return call(
        norm_kernel,
        [pltpu.VMEM(modulation.shape, F32)] + [pltpu.VMEM((rows, size), F32) for size in widths],
        [SMEM, HBM, HBM],
        [VMEM] * (1 + len(widths)),
        [pltpu.VMEM((rows, width), F32), pltpu.SemaphoreType.DMA((pieces + 1,))],
        moved=4 * rows * width,
    )(branch_index[None], *in_hbm(states, modulation))


def same_kernel(array_ref, _, out_ref):
    pass


def same(array, after):
    return call(
        same_kernel, pltpu.VMEM(array.shape, array.dtype), [VMEM, ANY], VMEM, aliases={0: 0}
    )(*in_vmem(array), after)


def modulate(tokens, factors):
    return jnp.concatenate(
        [
            (tokens * factors[i:i + 1] + factors[i + 1:i + 2] + factors[4:5]).astype(BF16)
            for i in (0, 2)
        ],
        axis=0,
    )


def first_kernel(groups, cuts, branch_ref, *refs):
    tokens_refs, refs = refs[:cuts], refs[cuts:]
    mine_ref, other_ref, embedding_ref, *sources = refs[:7]
    factors_refs, (keep_ref, *refs) = refs[7:7 + cuts], refs[7 + cuts:]
    send_refs, targets, sems = refs[:groups], refs[groups:-1], refs[-1]
    kept = keep_ref.shape[0]
    width = embedding_ref.shape[1]
    pieces = sems.shape[0] // len(sources)
    copies = []
    for source, target in zip(sources, targets):
        size = target.shape[0] // pieces
        for piece in range(pieces):
            sl = pl.ds(piece * size, size)
            copies.append(pltpu.make_async_copy(source.at[sl], target.at[sl], sems.at[len(copies)]))
    for copy in copies:
        copy.start()

    start = 0
    modulated = []
    for tokens_ref, factors_ref in zip(tokens_refs, factors_refs):
        size = tokens_ref.shape[1]
        columns = pl.ds(pl.multiple_of(branch_ref[0] * width + start, HD), size)
        embedding = embedding_ref[:, start:start + size]
        rows = []
        for mod_ref in (mine_ref, other_ref):
            rows += [1.0 + mod_ref[1, :, columns], mod_ref[0, :, columns]]
        rows.append(embedding)
        for i, row in enumerate(rows):
            factors_ref[i:i + 1, :] = row
        modulated.append(modulate(tokens_ref[...], rows_of(rows)))
        start += size
    modulated = jnp.concatenate(modulated, axis=1)
    size = width // pieces
    for i, weight_ref in enumerate(targets[:3]):
        projected = None
        for piece in range(pieces):
            copies[i * pieces + piece].wait()
            sl = slice(piece * size, (piece + 1) * size)
            partial = dot(modulated[:, sl], weight_ref[sl, :])
            projected = partial if projected is None else projected + partial
        chunk = weight_ref.shape[1] // groups
        for group in range(groups):
            columns = slice(group * chunk, (group + 1) * chunk)
            here = (group * 3 + i) * chunk
            keep_ref[:, here:here + chunk] = projected[:kept, columns]
            send_refs[group][:, i * chunk:(i + 1) * chunk] = projected[kept:, columns]
    for copy in copies[3 * pieces:]:
        copy.wait()


def rows_of(rows):
    return jnp.concatenate(rows, axis=0)


def project_first(branch_index, tokens, mine, other, embedding, weights, w_out, groups):
    rows = tokens[0].shape[0]
    width, columns = weights[0].shape
    cuts = len(tokens)
    factors = [pltpu.VMEM((5, piece.shape[1]), F32) for piece in tokens]
    keep = pltpu.VMEM((rows, 3 * columns), F32)
    send = pltpu.VMEM((rows, 3 * columns // groups), F32)
    held = [pltpu.VMEM(w.shape, BF16) for w in weights]
    out_held = pltpu.VMEM((w_out.shape[0] - w_out.shape[0] // 4, w_out.shape[1]), BF16)
    result = call(
        functools.partial(first_kernel, groups, cuts),
        factors + [keep] + [send] * groups + held + [out_held],
        [SMEM] + [VMEM] * (3 + cuts) + [HBM] * 4,
        [VMEM] * (5 + cuts + groups),
        [pltpu.SemaphoreType.DMA((12,))],
        flops=12 * rows * width * columns,
        moved=6 * width * columns,
    )(branch_index[None], *tokens, mine, other, embedding, *in_hbm(*weights, w_out))
    factors, (keep, *result) = result[:cuts], result[cuts:]
    return factors, keep, result[:groups], result[groups:-1], result[-1]


def later_kernel(added, groups, wanted, first_row, tokens_ref, factors_ref, wq_ref, wk_ref, wv_ref, *refs):
    before, (keep_ref, send_ref) = refs[:added], refs[-2:]
    rows = slice(first_row, first_row + tokens_ref.shape[1])
    kept = keep_ref.shape[0]
    modulated = modulate(tokens_ref[...], factors_ref[...])
    for place, group in enumerate(wanted):
        for i, weight_ref in enumerate((wq_ref, wk_ref, wv_ref)):
            chunk = weight_ref.shape[1] // groups
            projected = dot(modulated, weight_ref[rows, group * chunk:(group + 1) * chunk])
            keep, send = projected[:kept], projected[kept:]
            if before:
                sl = slice((group * 3 + i) * chunk, (group * 3 + i + 1) * chunk)
                keep, send = before[0][:, sl] + keep, before[1][:, sl] + send
            sl = slice((place * 3 + i) * chunk, (place * 3 + i + 1) * chunk)
            keep_ref[:, sl] = keep
            send_ref[:, sl] = send


def project_later(tokens, factors, weights, groups, wanted, first_row, before=(), scalars=()):
    columns = 3 * weights[0].shape[1] // groups * len(wanted)
    out = pltpu.VMEM((tokens.shape[0], columns), F32)
    return call(
        functools.partial(later_kernel, len(before), groups, wanted, first_row),
        [out, out],
        [VMEM] * (5 + len(before)) + [SMEM] * len(scalars),
        [VMEM] * 2,
        flops=4 * tokens.size * columns,
        moved=2 * tokens.shape[1] * columns,
    )(tokens, *in_vmem(factors, *weights, *before), *scalars)


def attention_kernel(starts, *refs):
    refs, out_ref = refs[:-1], refs[-1]
    blocks = [(refs[2 * i], refs[2 * i + 1], start) for i, start in enumerate(starts)]
    columns = out_ref.shape[1]

    def part(which, head):
        pieces = []
        for mine, other, start in blocks:
            here = which * columns + head * HD
            there = here + start
            pieces.append((mine[:, there:there + HD] + other[:, here:here + HD]).astype(BF16))
        return jnp.concatenate(pieces, axis=0)

    heads = columns // HD
    all_scores = [
        lax.dot_general(
            part(0, head), part(1, head), (((1,), (1,)), ((), ())), preferred_element_type=F32
        )
        for head in range(heads)
    ]
    all_probs = []
    for scores in all_scores:
        scores = scores * (1.0 / math.sqrt(HD))
        scores = jnp.exp(scores - jnp.max(scores, axis=1, keepdims=True))
        all_probs.append((scores / jnp.sum(scores, axis=1, keepdims=True)).astype(BF16))
    for head, probs in enumerate(all_probs):
        out_ref[:, head * HD:(head + 1) * HD] = dot(probs, part(2, head)).astype(BF16)


def attention(blocks, columns):
    flat = [array for block in blocks for array in block[:2]]
    rows = flat[0].shape[0]
    return call(
        functools.partial(attention_kernel, [block[2] for block in blocks]),
        pltpu.VMEM((rows * len(blocks), columns), BF16),
        [VMEM] * len(flat),
        VMEM,
        flops=4 * (rows * len(blocks)) ** 2 * columns,
        moved=12 * rows * len(blocks) * columns,
    )(*in_vmem(*flat))


def gate_of(mine, branch_ref, step_ref, guidance_ref, modulation_ref, columns):
    step = 2.0 * (1.0 + step_ref[0].astype(F32)) / NSTEPS
    scale = 1.5 + 0.5 * guidance_ref[0].astype(F32)
    conditional = (branch_ref[0] == 0) == mine
    share = jnp.where(conditional, step * scale, step * (1.0 - scale))
    half = pl.ds(pl.multiple_of(branch_ref[0] * columns, HD), columns)
    return share * (1.0 + modulation_ref[2, :, half])


def rest_kernel(source_ref, _, out_ref, sems):
    rows = out_ref.shape[0]
    size = rows // sems.shape[0]
    copies = []
    for index in range(sems.shape[0]):
        there = pl.ds(source_ref.shape[0] - rows + index * size, size)
        here = pl.ds(index * size, size)
        copies.append(pltpu.make_async_copy(source_ref.at[there], out_ref.at[here], sems.at[index]))
        copies[-1].start()
    for copy in copies:
        copy.wait()


def last_rows(array, rows, after):
    return call(
        rest_kernel,
        pltpu.VMEM((rows, array.shape[1]), array.dtype),
        [HBM, ANY],
        VMEM,
        [pltpu.SemaphoreType.DMA((1,))],
        moved=2 * rows * array.shape[1],
    )(*in_hbm(array), after)


def project_kernel(mine, cuts, added, *refs):
    scalar_refs, attended_refs, refs = refs[:3], refs[3:3 + cuts], refs[3 + cuts:]
    modulation_ref, held_ref, rest_ref, *refs = refs
    before, out_refs = refs[:added], refs[added:]
    held_rows = held_ref.shape[0]
    rows, columns = out_refs[0].shape
    chunk = math.gcd(columns, 512)
    gate = gate_of(mine, *scalar_refs, modulation_ref, columns)
    attended = jnp.concatenate([ref[...] for ref in attended_refs], axis=1)
    for start in range(0, columns, chunk):
        sl = slice(start, start + chunk)
        partial = dot(attended[:, :held_rows], held_ref[:, sl]) + dot(attended[:, held_rows:], rest_ref[:, sl])
        increment = gate[:, sl] * partial.astype(BF16).astype(F32)
        if before:
            increment = before[0][:, sl] + increment
        for block, out_ref in enumerate(out_refs):
            out_ref[:, sl] = increment[block * rows:(block + 1) * rows]


def project(mine, scalars, attended, held, rest, modulation, before=(), blocks=1):
    lat, columns = attended[0].shape[0], held.shape[1]
    return call(
        functools.partial(project_kernel, mine, len(attended), len(before)),
        [pltpu.VMEM((lat // blocks, columns), F32)] * blocks,
        [SMEM] * 3 + [VMEM] * (3 + len(attended) + len(before)),
        [VMEM] * blocks,
        flops=2 * lat * columns * (held.shape[0] + rest.shape[0]),
        moved=2 * columns * (held.shape[0] + rest.shape[0]),
    )(*scalars, *attended, modulation, *in_vmem(held, rest, *before))


def finish_kernel(place_ref, start_ref, added_ref, *refs):
    refs[-1][...] = start_ref[...] + added_ref[...].astype(F32)


def finish(place, start_state, added, target=None):
    rows, columns = added.shape
    half = pl.BlockSpec((rows, columns), lambda step, place_ref: (place_ref[0], 0))
    whole = pl.BlockSpec((rows, columns), lambda step, place_ref: (0, 0))
    given = [] if target is None else [target]
    return pl.pallas_call(
        finish_kernel,
        out_shape=jax.ShapeDtypeStruct(start_state.shape, F32),
        grid_spec=pltpu.PrefetchScalarGridSpec(
            num_scalar_prefetch=1,
            grid=(1,),
            in_specs=[half, whole] + [ANY] * len(given),
            out_specs=half,
        ),
        input_output_aliases={3: 0} if given else {},
        compiler_params=pltpu.CompilerParams(vmem_limit_bytes=6 << 20),
    )(place[None], start_state, added, *given)


def scan_general(parts, start_state):
    total = parts[0]
    for mask in range(1, len(parts)):
        total = total + xor_permute(parts[mask].astype(BF16), "tok", mask).astype(F32)
    position = lax.axis_index("tm")
    result, group = total, total
    mask = 1
    while mask < lax.axis_size("tm"):
        received = xor_permute(group.astype(BF16), "tm", mask).astype(F32)
        result = result + jnp.where(position & mask != 0, received, 0.0)
        group = group + received
        mask *= 2
    return start_state + result


def scan_planes(parts, start_state):
    axes = ("tm", "tok")
    position = lax.axis_index("tm")
    odd = position & 1 == 1
    rows = parts[0].shape[0] // 2

    def near(x):
        return jnp.where(odd, x[rows:], x[:rows])

    def far(x):
        return jnp.where(odd, x[:rows], x[rows:])

    diagonal = xor_permute(far(parts[1]).astype(BF16), axes, 3)
    across = xor_permute(near(parts[1]).astype(BF16), axes, 1)
    beside = xor_permute(far(parts[0]).astype(BF16), axes, 2)
    own_time = near(parts[0]) + across.astype(F32)
    pair_time = beside.astype(F32) + diagonal.astype(F32)
    group = own_time + pair_time
    earlier = jnp.zeros_like(group)
    mask = 2
    while mask < lax.axis_size("tm"):
        received = xor_permute(group.astype(BF16), "tm", mask).astype(F32)
        earlier = earlier + jnp.where(position & mask != 0, received, 0.0)
        group = group + received
        mask *= 2
    own = earlier + own_time + jnp.where(odd, pair_time, 0.0)
    for_pair = earlier + pair_time + jnp.where(odd, 0.0, own_time)
    returned = xor_permute(for_pair.astype(BF16), "tm", 1)
    place = position & 1
    return finish(1 - place, start_state, returned, finish(place, start_state, own))


def body(
    states, start_state, timesteps, guidance_index, modulation, w_query, w_key, w_value, w_out
):
    tok_count = lax.axis_size("tok")
    branch_index = lax.axis_index("branch")
    rows, model_width = states.shape[1:]
    half_width = model_width // 2
    widths = (half_width // 2, half_width // 2)
    modulation, *normed = normed_half(
        states[0], jnp.transpose(modulation, (1, 0, 2)), branch_index, widths
    )
    tokens = [
        [xor_permute(piece, "tok", mask) for piece in normed]
        for mask in range(1, tok_count)
    ]
    embedding = embed_half(timesteps, half_width, branch_index)
    modulation = same(modulation, embedding)
    other_modulation = xor_permute(modulation, "branch", 1)

    columns = w_query.shape[1]
    groups = 2 if columns % (2 * HD) == 0 else 1
    factors, keep, sends, weights, out_held = project_first(
        branch_index, normed, modulation, other_modulation, embedding,
        (w_query, w_key, w_value), w_out, groups
    )
    blocks = [
        [(keep, xor_permute(send, "branch", 1), 3 * columns // groups * group)]
        for group, send in enumerate(sends)
    ]
    for block in tokens:
        first_row, before = 0, ()
        for piece, factor in zip(block[:-1], factors):
            before = project_later(
                piece, factor, weights, groups, range(groups), first_row, before, (guidance_index,)
            )
            first_row += piece.shape[1]
        for group in range(groups):
            keep, send = project_later(
                block[-1], factors[-1], weights, groups, [group], first_row, before
            )
            blocks[group].append((keep, xor_permute(send, "branch", 1), 0))
    attended = [attention(blocks[group], columns // groups) for group in range(groups)]
    attended_other = [xor_permute(array, "branch", 1) for array in attended]
    scalars = (branch_index[None], timesteps, guidance_index)
    out_rest = last_rows(w_out, w_out.shape[0] - out_held.shape[0], attended[0])
    increments = project(True, scalars, attended, out_held, out_rest, modulation)
    parts = project(
        False, scalars, attended_other, out_held, out_rest, other_modulation, increments, tok_count
    )
    pairs = tok_count == 2 and lax.axis_size("tm") % 2 == 0 and rows % 32 == 0
    scan = scan_planes if pairs else scan_general
    return scan(parts, start_state)[None]


def solution(mesh):
    in_specs = (
        P("tm", "tok", None),
        P("tok", "branch"),
        P("tm"),
        P(),
        P("branch", None, None),
        P("branch", "tok"),
        P("branch", "tok"),
        P("branch", "tok"),
        P("tok", "branch"),
    )
    out_specs = P("tm", "tok", "branch")
    return jax.shard_map(body, mesh=mesh, in_specs=in_specs, out_specs=out_specs, check_vma=False)
```

time: 42.5 us -> 44.3 us (1.042)
  Pallas kernels: 10.9 us -> 12.5 us
  other arithmetic: 1.4 us -> 0.46 us
  waiting for transfers between devices: 14.2 us -> 15 us
    pallas_call x6 -> x11, Pallas kernels: 9.84 us -> 11.4 us  [the longest x1 4.46 us: project_first(): call(functools.partial(first_kernel, groups, cuts), factors + [keep] + [s...]
    ppermute x14 -> x15, waiting for transfers between devices: 14.2 us -> 15 us  [xor_permute(): lax.ppermute(x, axes, [(i, i ^ mask) for i in range(lax.axis_size(axes))])]
    broadcast_in_dim x1 -> x0, other arithmetic: 0.8 us -> none  [body(): return (start_state + scan(parts))[None]]
    ppermute x14 -> x15, starting transfers between devices: 14.4 us -> 14.6 us  [xor_permute(): lax.ppermute(x, axes, [(i, i ^ mask) for i in range(lax.axis_size(axes))])]
  transfers between devices with their start and end apart: 14 -> 15, of which waited for: 8 -> 8; matrix products, arithmetic and copies ran while one was open for 1% -> 1% of each run, Pallas kernels for 21% -> 22%
where the time goes in v6:
time: 44.3 us; the launch traced here: 44.1 us
  waiting for transfers between devices  15 us (34%)
  starting transfers between devices  14.6 us (33%)
  Pallas kernels  12.5 us (28%)
  between operations  1.46 us (3%)
  other arithmetic  0.46 us (1%)
    ppermute x15, waiting for transfers between devices, xor_permute(): lax.ppermute(x, axes, [(i, i ^ mask) for i in range(lax.axis_size(axes))])  15 us
    ppermute x15, starting transfers between devices, xor_permute(): lax.ppermute(x, axes, [(i, i ^ mask) for i in range(lax.axis_size(axes))])  14.6 us
    pallas_call x1, Pallas kernels, project_first(): call(functools.partial(first_kernel, groups, cuts), factors + [keep] + [s...  4.46 us
    pallas_call x3, Pallas kernels, project_later(): call(functools.partial(later_kernel, len(before), groups, wanted, first_r...  1.81 us
    pallas_call x1, Pallas kernels, normed_half(): call(norm_kernel, [pltpu.VMEM(modulation.shape, F32)] + [pltpu.VMEM((rows...  1.44 us
    pallas_call x2, Pallas kernels, finish(): pl.pallas_call(finish_kernel, out_shape=jax.ShapeDtypeStruct(start_state....  1.39 us
    pallas_call x2, Pallas kernels, project(): call(functools.partial(project_kernel, mine, len(attended), len(before)),...  1.19 us
    pallas_call x1, Pallas kernels, last_rows(): call(rest_kernel, pltpu.VMEM((rows, array.shape[1]), array.dtype), [HBM,...  1.14 us
  transfers between devices with their start and end apart: 15, of which 8 were waited for; matrix products, arithmetic and copies ran while one was open for 1% of the time, Pallas kernels for 22%

profile of v6, /device:TPU:0, one launch (start us, length us, event | category | flops | bytes accessed | tf_op | source)
XLA Modules:
  0.0 44.1 jit_solution(4701812905842006437)
XLA Ops:
  0.0 1.4 %shard_map.91 = (f32[3,1,3072]{2,1,0:T(1,128)S(1)}, f32[64,768]{1,0:T(8,128)S(1)}, f32[64,768]{1,0:T(8,128)S(1)}) custom-call(s32[1]{0:T(128)} %bitcast.1.branch_ref.refs_0_, f32[64,3072]{1,0:T(8,128)} %bitcast.7, f32[3,1,3072]{2,1,0:T(1,128)} %bitcast.8), custom_call_target="tpu_custom_call" | custom-call | bytes 786432 | tf_op jit(solution)/shard_map/pallas_call | solution.py:86
  1.4 3.0 %collective-permute-start.3 = (f32[64,768]{1,0:T(8,128)S(1)}, f32[64,768]{1,0:T(8,128)S(1)}, u32[]{:S(2)}, u32[]{:S(2)}) collective-permute-start(f32[64,768]{1,0:T(8,128)S(1)} %get-tuple-element.25.refs_0_), channel_id=1, source_target_pairs={{0,1},{1,0},{2,3},{3,2},{4,5},{5,4},{6,7},{7,6},{8,9},{9,8},{10,11... | collective-permute-start | bytes 589832 | tf_op jit(solution)/shard_map/ppermute | solution.py:22
  5.1 0.2 broadcast_select_fusion._.refs_4_
  6.1 0.5 %collective-permute-done.refs_3_.refs_5_ = f32[3,1,3072]{2,1,0:T(1,128)S(1)} collective-permute-done((f32[3,1,3072]{2,1,0:T(1,128)S(1)}, f32[3,1,3072]{2,1,0:T(1,128)S(1)}, u32[]{:S(2)}, u32[]{:S(2)}) %collective-permute-start) | collective-permute-done | bytes 36896 | tf_op jit(solution)/shard_map/ppermute | solution.py:22
  6.6 4.5 %shard_map.93 = (f32[5,768]{1,0:T(8,128)S(1)}, f32[5,768]{1,0:T(8,128)S(1)}, f32[64,3072]{1,0:T(8,128)S(1)}, f32[64,1536]{1,0:T(8,128)S(1)}, f32[64,1536]{1,0:T(...) custom-call(s32[1]{0:T(128)} %bitcast.1.branch_ref.refs_0_, ...), custom_call_target="tpu_custom_call" | custom-call | flops 1207959552 | bytes 9437184 | tf_op jit(solution)/shard_map/pallas_call | solution.py:179
  11.1 0.2 collective-permute-start.6
  11.3 0.3 collective-permute-start.1
  11.7 0.8 %shard_map.94 = (f32[64,3072]{1,0:T(8,128)S(1)}, f32[64,3072]{1,0:T(8,128)S(1)}) custom-call(f32[64,768]{1,0:T(8,128)S(1)} %collective-permute-done.3.tokens_ref, f32[5,768]{1,0:T(8,128)S(1)} %get-tuple-element.34.factors_ref, bf16[1536,1024]{1,0:T(8,128)(2,1)S(1)} %get-tuple-element.31.wq_ref, bf16[1536,1024]{1,0:T(8,128)(2,1)S(1)} %get-tuple-element.32.wk_ref, ...), custom_call_target="tpu_custom_call" | custom-call | flops 603979776 | bytes 4718592 | tf_op jit(solution)/shard_map/pallas_call | solution.py:213
  12.5 1.1 %collective-permute-done.2.tokens_ref = f32[64,768]{1,0:T(8,128)S(1)} collective-permute-done((f32[64,768]{1,0:T(8,128)S(1)}, f32[64,768]{1,0:T(8,128)S(1)}, u32[]{:S(2)}, u32[]{:S(2)}) %collective-permute-start.2) | collective-permute-done | bytes 196640 | tf_op jit(solution)/shard_map/ppermute | solution.py:22
  13.6 0.5 %shard_map.97 = (f32[64,1536]{1,0:T(8,128)S(1)}, f32[64,1536]{1,0:T(8,128)S(1)}) custom-call(f32[64,768]{1,0:T(8,128)S(1)} %collective-permute-done.2.tokens_ref, f32[5,768]{1,0:T(8,128)S(1)} %get-tuple-element.30.factors_ref, bf16[1536,1024]{1,0:T(8,128)(2,1)S(1)} %get-tuple-element.31.wq_ref, bf16[1536,1024]{1,0:T(8,128)(2,1)S(1)} %get-tuple-element.32.wk_ref, ...), custom_call_target="tpu_custom_call" | custom-call | flops 301989888 | bytes 2359296 | tf_op jit(solution)/shard_map/pallas_call | solution.py:213
  14.2 0.5 %shard_map.95 = (f32[64,1536]{1,0:T(8,128)S(1)}, f32[64,1536]{1,0:T(8,128)S(1)}) custom-call(f32[64,768]{1,0:T(8,128)S(1)} %collective-permute-done.2.tokens_ref, f32[5,768]{1,0:T(8,128)S(1)} %get-tuple-element.30.factors_ref, bf16[1536,1024]{1,0:T(8,128)(2,1)S(1)} %get-tuple-element.31.wq_ref, bf16[1536,1024]{1,0:T(8,128)(2,1)S(1)} %get-tuple-element.32.wk_ref, ...), custom_call_target="tpu_custom_call" | custom-call | flops 301989888 | bytes 2359296 | tf_op jit(solution)/shard_map/pallas_call | solution.py:213
  14.7 0.6 %collective-permute-start.4 = (f32[64,1536]{1,0:T(8,128)S(1)}, f32[64,1536]{1,0:T(8,128)S(1)}, u32[]{:S(2)}, u32[]{:S(2)}) collective-permute-start(f32[64,1536]{1,0:T(8,128)S(1)} %get-tuple-element.38), channel_id=1, source_target_pairs={{0,16},{16,0},{1,17},{17,1},{2,18},{18,2},{3,19},{19,3},{4,20},{20... | collective-permute-start | bytes 1179656 | tf_op jit(solution)/shard_map/ppermute | solution.py:22
  15.2 0.6 %collective-permute-done.7.refs_3_ = f32[64,1536]{1,0:T(8,128)S(1)} collective-permute-done((f32[64,1536]{1,0:T(8,128)S(1)}, f32[64,1536]{1,0:T(8,128)S(1)}, u32[]{:S(2)}, u32[]{:S(2)}) %collective-permute-start.7) | collective-permute-done | bytes 393248 | tf_op jit(solution)/shard_map/ppermute | solution.py:22
  15.9 0.5 %shard_map.98.refs_4_ = bf16[128,512]{1,0:T(8,128)(2,1)S(1)} custom-call(f32[64,3072]{1,0:T(8,128)S(1)} %get-tuple-element.28.refs_0_, f32[64,1536]{1,0:T(8,128)S(1)} %collective-permute-done.6.refs_1_, f32[64,1536]{1,0:T(8,128)S(1)} %get-tuple-element.40.refs_2_, f32[64,1536]{1,0:T(8,128)S(1)} %collective-permute-done.7.refs_3_), custom_call_target="tpu_custom_call" | custom-call | flops 33554432 | bytes 786432 | tf_op jit(solution)/shard_map/pallas_call | solution.py:255
  16.6 0.5 %shard_map.96._.refs_3_ = bf16[128,512]{1,0:T(8,128)(2,1)S(1)} custom-call(f32[64,3072]{1,0:T(8,128)S(1)} %get-tuple-element.28.refs_0_, f32[64,1536]{1,0:T(8,128)S(1)} %collective-permute-done.1.refs_1_, f32[64,1536]{1,0:T(8,128)S(1)} %get-tuple-element.37.refs_2_, f32[64,1536]{1,0:T(8,128)S(1)} %collective-permute-done.4.refs_3_), custom_call_target="tpu_custom_call" | custom-call | flops 33554432 | bytes 786432 | tf_op jit(solution)/shard_map/pallas_call | solution.py:255
  17.1 0.4 collective-permute-start.5
  17.6 1.1 %shard_map.99.refs_7_ = bf16[256,1536]{1,0:T(8,128)(2,1)S(1)} custom-call(bf16[1024,1536]{1,0:T(8,128)(2,1)} %source_ref.1, bf16[128,512]{1,0:T(8,128)(2,1)S(1)} %shard_map.96._.refs_3_), custom_call_target="tpu_custom_call" | custom-call | bytes 786432 | tf_op jit(solution)/shard_map/pallas_call | solution.py:288
  18.7 0.6 %shard_map.100.refs_8_ = f32[128,1536]{1,0:T(8,128)S(1)} custom-call(s32[1]{0:T(128)} %bitcast.1.branch_ref.refs_0_, s32[1]{0:T(128)S(6)} %copy.14.refs_1_, s32[1]{0:T(128)S(6)} %copy.15.refs_0_.refs_2_, bf16[128,512]{1,0:T(8,128)(2,1)S(1)} %shard_map.96._.refs_3_, bf16[128,512]{1,0:T(8,128)(2,1)S(1)} %shard_map.98.refs_4_, ...), custom_call_target="tpu_custom_call" | custom-call | flops 402653184 | bytes 3145728 | tf_op jit(solution)/shard_map/pallas_call | solution.py:319
  19.4 0.6 %shard_map.101 = (f32[64,1536]{1,0:T(8,128)S(1)}, f32[64,1536]{1,0:T(8,128)S(1)}) custom-call(s32[1]{0:T(128)} %bitcast.1.branch_ref.refs_0_, s32[1]{0:T(128)S(6)} %copy.14.refs_1_, s32[1]{0:T(128)S(6)} %copy.15.refs_0_.refs_2_, bf16[128,512]{1,0:T(8,128)(2,1)S(1)} %collective-permute-done.5.refs_3_, bf16[128,512]{1,0:T(8,128)(2,1)S(1)} %collective-permute-done.8.refs_4_, ...), custom_call_target="tpu_custom_call" | custom-call | flops 402653184 | bytes 3145728 | tf_op jit(solution)/shard_map/pallas_call | solution.py:319
  20.0 2.7 %collective-permute-start.11 = (bf16[32,1536]{1,0:T(8,128)(2,1)S(1)}, bf16[32,1536]{1,0:T(8,128)(2,1)S(1)}, u32[]{:S(2)}, u32[]{:S(2)}) collective-permute-start(bf16[32,1536]{1,0:T(8,128)(2,1)S(1)} %get-tuple-element.50), channel_id=1, source_target_pairs={{0,3},{1,2},{2,1},{3,0},{4,7},{5,6},{6,5},{7,4},{8,11},{9,10},{10,... | collective-permute-start | bytes 294920 | tf_op jit(solution)/shard_map/ppermute | solution.py:22
  22.8 0.5 %collective-permute-start.9 = (bf16[32,1536]{1,0:T(8,128)(2,1)S(1)}, bf16[32,1536]{1,0:T(8,128)(2,1)S(1)}, u32[]{:S(2)}, u32[]{:S(2)}) collective-permute-start(bf16[32,1536]{1,0:T(8,128)(2,1)S(1)} %get-tuple-element.49), channel_id=1, source_target_pairs={{0,1},{1,0},{2,3},{3,2},{4,5},{5,4},{6,7},{7,6},{8,9},{9,8},{10,11... | collective-permute-start | bytes 294920 | tf_op jit(solution)/shard_map/ppermute | solution.py:22
  23.3 0.3 collective-permute-start.10
  23.6 3.0 %collective-permute-done.11 = bf16[32,1536]{1,0:T(8,128)(2,1)S(1)} collective-permute-done((bf16[32,1536]{1,0:T(8,128)(2,1)S(1)}, bf16[32,1536]{1,0:T(8,128)(2,1)S(1)}, u32[]{:S(2)}, u32[]{:S(2)}) %collective-permute-start.11) | collective-permute-done | bytes 98336 | tf_op jit(solution)/shard_map/ppermute | solution.py:22
  26.6 1.6 %collective-permute-done.9 = bf16[32,1536]{1,0:T(8,128)(2,1)S(1)} collective-permute-done((bf16[32,1536]{1,0:T(8,128)(2,1)S(1)}, bf16[32,1536]{1,0:T(8,128)(2,1)S(1)}, u32[]{:S(2)}, u32[]{:S(2)}) %collective-permute-start.9) | collective-permute-done | bytes 98336 | tf_op jit(solution)/shard_map/ppermute | solution.py:22
  28.3 1.7 %collective-permute-start.12 = (bf16[32,1536]{1,0:T(8,128)(2,1)S(1)}, bf16[32,1536]{1,0:T(8,128)(2,1)S(1)}, u32[]{:S(2)}, u32[]{:S(2)}) collective-permute-start(bf16[32,1536]{1,0:T(8,128)(2,1)S(1)} %get-tuple-element.45), channel_id=1, source_target_pairs={{0,4},{2,6},{4,0},{6,2},{8,12},{10,14},{12,8},{14,10},{1,5},{3,7},... | collective-permute-start | bytes 294920 | tf_op jit(solution)/shard_map/ppermute | solution.py:22
  30.0 3.0 %collective-permute-done.12 = bf16[32,1536]{1,0:T(8,128)(2,1)S(1)} collective-permute-done((bf16[32,1536]{1,0:T(8,128)(2,1)S(1)}, bf16[32,1536]{1,0:T(8,128)(2,1)S(1)}, u32[]{:S(2)}, u32[]{:S(2)}) %collective-permute-start.12) | collective-permute-done | bytes 98336 | tf_op jit(solution)/shard_map/ppermute | solution.py:22
  33.0 2.7 %collective-permute-start.13 = (bf16[32,1536]{1,0:T(8,128)(2,1)S(1)}, bf16[32,1536]{1,0:T(8,128)(2,1)S(1)}, u32[]{:S(2)}, u32[]{:S(2)}) collective-permute-start(bf16[32,1536]{1,0:T(8,128)(2,1)S(1)} %fusion.1), channel_id=1, source_target_pairs={{0,8},{2,10},{4,12},{6,14},{8,0},{10,2},{12,4},{14,6},{1,9},{3,11}... | collective-permute-start | bytes 294920 | tf_op jit(solution)/shard_map/ppermute | solution.py:22
  35.7 2.8 %collective-permute-done.13 = bf16[32,1536]{1,0:T(8,128)(2,1)S(1)} collective-permute-done((bf16[32,1536]{1,0:T(8,128)(2,1)S(1)}, bf16[32,1536]{1,0:T(8,128)(2,1)S(1)}, u32[]{:S(2)}, u32[]{:S(2)}) %collective-permute-start.13) | collective-permute-done | bytes 98336 | tf_op jit(solution)/shard_map/ppermute | solution.py:22
  38.7 1.5 %collective-permute-start.14 = (bf16[32,1536]{1,0:T(8,128)(2,1)S(1)}, bf16[32,1536]{1,0:T(8,128)(2,1)S(1)}, u32[]{:S(2)}, u32[]{:S(2)}) collective-permute-start(bf16[32,1536]{1,0:T(8,128)(2,1)S(1)} %get-tuple-element.48), channel_id=1, source_target_pairs={{0,2},{2,0},{4,6},{6,4},{8,10},{10,8},{12,14},{14,12},{1,3},{3,1},... | collective-permute-start | bytes 294920 | tf_op jit(solution)/shard_map/ppermute | solution.py:22
  40.2 0.7 %shard_map.102.refs_0_ = f32[64,1536]{1,0:T(8,128)} custom-call(s32[1]{0:T(128)} %bitcast.5.place_ref, f32[64,1536]{1,0:T(8,128)S(1)} %copy-done, f32[32,1536]{1,0:T(8,128)S(1)} %get-tuple-element.47.added_ref), custom_call_target="tpu_custom_call" | custom-call | tf_op jit(solution)/shard_map/pallas_call | solution.py:338
  40.9 2.4 %collective-permute-done.14.added_ref = bf16[32,1536]{1,0:T(8,128)(2,1)S(1)} collective-permute-done((bf16[32,1536]{1,0:T(8,128)(2,1)S(1)}, bf16[32,1536]{1,0:T(8,128)(2,1)S(1)}, u32[]{:S(2)}, u32[]{:S(2)}) %collective-permute-start.14) | collective-permute-done | bytes 98336 | tf_op jit(solution)/shard_map/ppermute | solution.py:22
  43.4 0.7 %shard_map.103 = f32[64,1536]{1,0:T(8,128)} custom-call(s32[1]{0:T(128)} %bitcast.place_ref, f32[64,1536]{1,0:T(8,128)S(1)} %copy-done, bf16[32,1536]{1,0:T(8,128)(2,1)S(1)} %collective-permute-done.14.added_ref, f32[64,1536]{1,0:T(8,128)} %shard_map.102.refs_0_), custom_call_target="tpu_custom_call", output_to_operand_aliasing={{}: (3, {})} | custom-call | tf_op jit(solution)/shard_map/pallas_call | solution.py:338
  (19 shorter events, 0.7 us)
Async XLA Ops:
  1.4 10.2 %collective-permute-start.3 = (f32[64,768]{1,0:T(8,128)S(1)}, f32[64,768]{1,0:T(8,128)S(1)}, u32[]{:S(2)}, u32[]{:S(2)}) collective-permute-start(f32[64,768]{1,0:T(8,128)S(1)} %get-tuple-element.25.refs_0_), channel_id=1, source_target_pairs={{0,1},{1,0},{2,3},{3,2},{4,5},{5,4},{6,7},{7,6},{8,9},{9,8},{10,11... | collective-permute-start | bytes 589832 | tf_op jit(solution)/shard_map/ppermute | solution.py:22
  5.3 1.3 %collective-permute-start = (f32[3,1,3072]{2,1,0:T(1,128)S(1)}, f32[3,1,3072]{2,1,0:T(1,128)S(1)}, u32[]{:S(2)}, u32[]{:S(2)}) collective-permute-start(f32[3,1,3072]{2,1,0:T(1,128)S(1)} %shard_map.92.refs_2_.refs_5_), channel_id=1, source_target_pairs={{0,16},{16,0},{1,17},{17,1},{2,18},{18,2},{3,19},{19,3},{4,20},{20... | collective-permute-start | bytes 110600 | tf_op jit(solution)/shard_map/ppermute | solution.py:22
  5.4 8.2 %collective-permute-start.2 = (f32[64,768]{1,0:T(8,128)S(1)}, f32[64,768]{1,0:T(8,128)S(1)}, u32[]{:S(2)}, u32[]{:S(2)}) collective-permute-start(f32[64,768]{1,0:T(8,128)S(1)} %get-tuple-element.26.refs_1_), channel_id=1, source_target_pairs={{0,1},{1,0},{2,3},{3,2},{4,5},{5,4},{6,7},{7,6},{8,9},{9,8},{10,11... | collective-permute-start | bytes 589832 | tf_op jit(solution)/shard_map/ppermute | solution.py:22
  11.1 4.2 %collective-permute-start.6 = (f32[64,1536]{1,0:T(8,128)S(1)}, f32[64,1536]{1,0:T(8,128)S(1)}, u32[]{:S(2)}, u32[]{:S(2)}) collective-permute-start(f32[64,1536]{1,0:T(8,128)S(1)} %get-tuple-element.39), channel_id=1, source_target_pairs={{0,16},{16,0},{1,17},{17,1},{2,18},{18,2},{3,19},{19,3},{4,20},{20... | collective-permute-start | bytes 1179656 | tf_op jit(solution)/shard_map/ppermute | solution.py:22
  11.3 5.3 %collective-permute-start.1 = (f32[64,1536]{1,0:T(8,128)S(1)}, f32[64,1536]{1,0:T(8,128)S(1)}, u32[]{:S(2)}, u32[]{:S(2)}) collective-permute-start(f32[64,1536]{1,0:T(8,128)S(1)} %get-tuple-element.29), channel_id=1, source_target_pairs={{0,16},{16,0},{1,17},{17,1},{2,18},{18,2},{3,19},{19,3},{4,20},{20... | collective-permute-start | bytes 1179656 | tf_op jit(solution)/shard_map/ppermute | solution.py:22
  14.1 1.8 %collective-permute-start.7 = (f32[64,1536]{1,0:T(8,128)S(1)}, f32[64,1536]{1,0:T(8,128)S(1)}, u32[]{:S(2)}, u32[]{:S(2)}) collective-permute-start(f32[64,1536]{1,0:T(8,128)S(1)} %get-tuple-element.41), channel_id=1, source_target_pairs={{0,16},{16,0},{1,17},{17,1},{2,18},{18,2},{3,19},{19,3},{4,20},{20... | collective-permute-start | bytes 1179656 | tf_op jit(solution)/shard_map/ppermute | solution.py:22
  14.7 1.9 %collective-permute-start.4 = (f32[64,1536]{1,0:T(8,128)S(1)}, f32[64,1536]{1,0:T(8,128)S(1)}, u32[]{:S(2)}, u32[]{:S(2)}) collective-permute-start(f32[64,1536]{1,0:T(8,128)S(1)} %get-tuple-element.38), channel_id=1, source_target_pairs={{0,16},{16,0},{1,17},{17,1},{2,18},{18,2},{3,19},{19,3},{4,20},{20... | collective-permute-start | bytes 1179656 | tf_op jit(solution)/shard_map/ppermute | solution.py:22
  16.4 2.9 %collective-permute-start.8 = (bf16[128,512]{1,0:T(8,128)(2,1)S(1)}, bf16[128,512]{1,0:T(8,128)(2,1)S(1)}, u32[]{:S(2)}, u32[]{:S(2)}) collective-permute-start(bf16[128,512]{1,0:T(8,128)(2,1)S(1)} %shard_map.98.refs_4_), channel_id=1, source_target_pairs={{0,16},{16,0},{1,17},{17,1},{2,18},{18,2},{3,19},{19,3},{4,20},{20... | collective-permute-start | bytes 393224 | tf_op jit(solution)/shard_map/ppermute | solution.py:22
  17.1 2.2 %collective-permute-start.5 = (bf16[128,512]{1,0:T(8,128)(2,1)S(1)}, bf16[128,512]{1,0:T(8,128)(2,1)S(1)}, u32[]{:S(2)}, u32[]{:S(2)}) collective-permute-start(bf16[128,512]{1,0:T(8,128)(2,1)S(1)} %shard_map.96._.refs_3_), channel_id=1, source_target_pairs={{0,16},{16,0},{1,17},{17,1},{2,18},{18,2},{3,19},{19,3},{4,20},{20... | collective-permute-start | bytes 393224 | tf_op jit(solution)/shard_map/ppermute | solution.py:22
  19.3 20.9 %copy-start = (f32[64,1536]{1,0:T(8,128)S(1)}, f32[64,1536]{1,0:T(8,128)}, u32[]{:S(2)}) copy-start(f32[64,1536]{1,0:T(8,128)} %start_ref.3) | copy-start | bytes 1179652
  20.0 6.6 %collective-permute-start.11 = (bf16[32,1536]{1,0:T(8,128)(2,1)S(1)}, bf16[32,1536]{1,0:T(8,128)(2,1)S(1)}, u32[]{:S(2)}, u32[]{:S(2)}) collective-permute-start(bf16[32,1536]{1,0:T(8,128)(2,1)S(1)} %get-tuple-element.50), channel_id=1, source_target_pairs={{0,3},{1,2},{2,1},{3,0},{4,7},{5,6},{6,5},{7,4},{8,11},{9,10},{10,... | collective-permute-start | bytes 294920 | tf_op jit(solution)/shard_map/ppermute | solution.py:22
  22.8 5.5 %collective-permute-start.9 = (bf16[32,1536]{1,0:T(8,128)(2,1)S(1)}, bf16[32,1536]{1,0:T(8,128)(2,1)S(1)}, u32[]{:S(2)}, u32[]{:S(2)}) collective-permute-start(bf16[32,1536]{1,0:T(8,128)(2,1)S(1)} %get-tuple-element.49), channel_id=1, source_target_pairs={{0,1},{1,0},{2,3},{3,2},{4,5},{5,4},{6,7},{7,6},{8,9},{9,8},{10,11... | collective-permute-start | bytes 294920 | tf_op jit(solution)/shard_map/ppermute | solution.py:22
  23.3 4.9 %collective-permute-start.10 = (bf16[32,1536]{1,0:T(8,128)(2,1)S(1)}, bf16[32,1536]{1,0:T(8,128)(2,1)S(1)}, u32[]{:S(2)}, u32[]{:S(2)}) collective-permute-start(bf16[32,1536]{1,0:T(8,128)(2,1)S(1)} %select_convert_fusion.1), channel_id=1, source_target_pairs={{0,2},{1,3},{2,0},{3,1},{4,6},{5,7},{6,4},{7,5},{8,10},{9,11},{10,... | collective-permute-start | bytes 294920 | tf_op jit(solution)/shard_map/ppermute | solution.py:22
  28.3 4.7 %collective-permute-start.12 = (bf16[32,1536]{1,0:T(8,128)(2,1)S(1)}, bf16[32,1536]{1,0:T(8,128)(2,1)S(1)}, u32[]{:S(2)}, u32[]{:S(2)}) collective-permute-start(bf16[32,1536]{1,0:T(8,128)(2,1)S(1)} %get-tuple-element.45), channel_id=1, source_target_pairs={{0,4},{2,6},{4,0},{6,2},{8,12},{10,14},{12,8},{14,10},{1,5},{3,7},... | collective-permute-start | bytes 294920 | tf_op jit(solution)/shard_map/ppermute | solution.py:22
  33.0 5.6 %collective-permute-start.13 = (bf16[32,1536]{1,0:T(8,128)(2,1)S(1)}, bf16[32,1536]{1,0:T(8,128)(2,1)S(1)}, u32[]{:S(2)}, u32[]{:S(2)}) collective-permute-start(bf16[32,1536]{1,0:T(8,128)(2,1)S(1)} %fusion.1), channel_id=1, source_target_pairs={{0,8},{2,10},{4,12},{6,14},{8,0},{10,2},{12,4},{14,6},{1,9},{3,11}... | collective-permute-start | bytes 294920 | tf_op jit(solution)/shard_map/ppermute | solution.py:22
  38.7 4.7 %collective-permute-start.14 = (bf16[32,1536]{1,0:T(8,128)(2,1)S(1)}, bf16[32,1536]{1,0:T(8,128)(2,1)S(1)}, u32[]{:S(2)}, u32[]{:S(2)}) collective-permute-start(bf16[32,1536]{1,0:T(8,128)(2,1)S(1)} %get-tuple-element.48), channel_id=1, source_target_pairs={{0,2},{2,0},{4,6},{6,4},{8,10},{10,8},{12,14},{14,12},{1,3},{3,1},... | collective-permute-start | bytes 294920 | tf_op jit(solution)/shard_map/ppermute | solution.py:22
